TPU v7x, 32 devices: a whole 2x2x4 slice. The times are simulated.
32 devices in a mesh: brick: 16 (over z, y, x), state: 2 (over core).
Axes of the slice: x: 2, y: 2, z: 4, core: 2. Of those that a mesh axis runs over, the one named last changes fastest.
Arguments:
- states: bfloat16 [384, 110592], P('state', 'brick'), may hold values from -40 to 40
- kinetic: bfloat16 [343, 343], replicated, may hold values from -2 to 4, as said below
- potential: float32 [110592], P('brick'), may hold values from -1.5 to 1.5
- cell_nodes: int32 [512, 343], P('brick'), may hold values from 0 to 8063, as said below
- face_map: int32 [18432], P('brick'), may hold values from 0 to 6911, as said below
Outputs:
- rotated: float32 [384, 110592], P('state', 'brick')
Inputs may be any that keep to these rules, and one draw needn't show every extreme that they name: `cell_nodes`: block b of 32 rows belongs to brick b; a row lists the 343 nodes of one hexahedral cell of degree 6, lexicographic in the cell's three local coordinates, the first slowest. A value below 6912 is a column of brick b's block of states and potential; a value 6912 + f is the node named by entry f of brick b + 1's block of face_map (brick 0 after the last). Every own node and every face slot lies in some cell. `face_map`: block b of 1152 entries lists distinct own nodes of brick b: those it shares with brick b - 1. `kinetic`: Symmetric.
All inputs are finite; a program needn't handle non-finite values.
Results may differ from a plain program's by a relative error of at most 0.0005.
The roundings to bfloat16 on the way count: a program that leaves them out, or rounds other values in their place, can miss the bound.
Values may be sent and summed in bfloat16 or wider, within the bound.
No kernel may reach another device: no remote copies, remote signals or barrier semaphores. Data moves between devices by JAX's collectives and lax.ppermute only.
A program may use at most 128 MiB of HBM per device.

v0:
```python
import jax
import jax.numpy as jnp
from jax import lax
from jax.sharding import PartitionSpec as P

NS_STEPS = 3


cheb_center = 3.0
cheb_half = 7.0
epsilon = 1e-06


def passed_along(value, axis, steps):
    count = lax.axis_size(axis)
    pairs = [(source, (source + steps) % count) for source in range(count)]
    return lax.ppermute(value, axis, pairs)


def apply_operator(vector, kinetic, potential, cell_nodes, face_map):
    width, owned = vector.shape
    face_count = face_map.shape[0]
    ghost_cols = passed_along(vector[:, face_map], "brick", -1)
    extended = jnp.concatenate([vector, ghost_cols], axis=1)
    gathered = extended[:, cell_nodes]
    products = jnp.einsum("wca,ea->wce", gathered, kinetic, preferred_element_type=jnp.float32)
    summed = (
        jnp.zeros((width, owned + face_count), jnp.float32)
        .at[:, cell_nodes.reshape(-1)]
        .add(products.reshape(width, -1))
    )
    returned = passed_along(summed[:, owned:], "brick", 1)
    assembled = summed[:, :owned].at[:, face_map].add(returned)
    return assembled + potential[None, :] * vector.astype(jnp.float32)


def newton_schulz(margin):
    total = margin.shape[0]
    identity = jnp.eye(total, dtype=jnp.float32)
    scale = jnp.sqrt(jnp.sum(margin * margin) + epsilon)
    current = margin / scale
    inverse = identity
    for iteration in range(NS_STEPS):
        factor = 3.0 * identity - jnp.dot(inverse, current, precision=lax.Precision.HIGHEST)
        current = 0.5 * jnp.dot(factor, current, precision=lax.Precision.HIGHEST)
        inverse = 0.5 * jnp.dot(factor, inverse, precision=lax.Precision.HIGHEST)
    return inverse


def local(states, kinetic, potential, cell_nodes, face_map):
    first = apply_operator(states, kinetic, potential, cell_nodes, face_map)
    filtered_once = ((first - cheb_center * states.astype(jnp.float32)) / cheb_half).astype(
        jnp.bfloat16
    )
    second = apply_operator(filtered_once, kinetic, potential, cell_nodes, face_map)
    filtered = (
        2.0 * (second - cheb_center * filtered_once.astype(jnp.float32)) / cheb_half
        - states.astype(jnp.float32)
    ).astype(jnp.bfloat16)
    width = states.shape[0]
    every = lax.all_gather(filtered, "state", axis=0, tiled=True)
    start = lax.axis_index("state") * width
    partial_rows = lax.dot_general(
        filtered, every, (((1,), (1,)), ((), ())), preferred_element_type=jnp.float32
    )
    margin_rows = lax.psum(partial_rows, "brick")
    margin = lax.all_gather(margin_rows, "state", axis=0, tiled=True)
    root_rows = lax.dynamic_slice_in_dim(newton_schulz(margin), start, width, 0)
    return jnp.dot(root_rows.astype(jnp.bfloat16), every, preferred_element_type=jnp.float32)


def solution(mesh):
    in_specs = (P("state", "brick"), P(), P("brick"), P("brick", None), P("brick"))
    out_specs = P("state", "brick")
    return jax.shard_map(local, mesh=mesh, in_specs=in_specs, out_specs=out_specs, check_vma=False)
```

profile of v0, /device:TPU:0, one launch (start us, length us, event | category | flops | bytes accessed | tf_op | source)
XLA Modules:
  0.0 593.4 jit_solution(1776269504513874843)
XLA Ops:
  6.5 5.6 copy.38
  12.1 0.7 compare_select_fusion.2
  12.8 5.7 gather_fusion
  18.6 0.3 copy.37
  18.8 7.0 %collective-permute-start = (bf16[192,1152]{1,0:T(8,128)(2,1)S(1)}, bf16[192,1152]{1,0:T(8,128)(2,1)S(1)}, u32[]{:S(2)}, u32[]{:S(2)}) collective-permute-start(bf16[192,1152]{1,0:T(8,128)(2,1)S(1)} %copy.37), channel_id=1, source_target_pairs={{0,30},{2,0},{4,2},{6,4},{8,6},{10,8},{12,10},{14,12},{16,14},{18,... | collective-permute-start | bytes 1327112 | tf_op jit(solution)/shard_map/ppermute | solution.py:17
  25.8 0.2 reshape.39
  26.0 0.1 reshape.52
  26.1 0.1 fusion.22
  26.3 8.9 %collective-permute-done = bf16[192,1152]{1,0:T(8,128)(2,1)S(1)} collective-permute-done((bf16[192,1152]{1,0:T(8,128)(2,1)S(1)}, bf16[192,1152]{1,0:T(8,128)(2,1)S(1)}, u32[]{:S(2)}, u32[]{:S(2)}) %collective-permute-start) | collective-permute-done | bytes 442400 | tf_op jit(solution)/shard_map/ppermute | solution.py:17
  35.2 0.2 copy.39
  35.5 4.7 pad_maximum_fusion
  40.1 28.3 %gather_fusion.1 = bf16[10976,192]{1,0:T(8,128)(2,1)} fusion(bf16[192,8064]{0,1:T(8,128)(2,1)} %pad_maximum_fusion, s32[11264]{0:T(1024)S(1)} %pad_clamp_fusion), kind=kCustom, calls=%fused_computation.1 | custom fusion | bytes 8473472 | tf_op jit(solution)/shard_map/gather | solution.py:25
  68.5 7.5 %copy.40 = bf16[10976,192]{0,1:T(8,128)(2,1)} copy(bf16[10976,192]{1,0:T(8,128)(2,1)} %gather_fusion.1) | data formatting | bytes 8429568 | tf_op jit(solution)/shard_map/gather | solution.py:25
  76.0 12.8 %reshape.55 = bf16[32,343,192]{1,0,2:T(8,128)(2,1)} reshape(bf16[10976,192]{0,1:T(8,128)(2,1)} %copy.40) | data formatting | bytes 8429568 | tf_op jit(solution)/shard_map/gather | solution.py:25
  88.8 9.0 %fusion.10 = f32[192,32,343]{2,1,0:T(8,128)} fusion(bf16[32,343,192]{1,0,2:T(8,128)(2,1)} %reshape.55, bf16[343,343]{1,0:T(8,128)(2,1)S(1)} %copy-done), kind=kOutput, calls=%fused_computation.23 | convolution fusion | flops 1445670912 | bytes 12879650 | tf_op jit(solution)/shard_map/wca,ea->wce/dot_general | solution.py:26
  97.8 11.1 %reshape.75 = f32[192,10976]{1,0:T(8,128)} reshape(f32[192,32,343]{2,1,0:T(8,128)} %fusion.10) | data formatting | bytes 16859136 | tf_op jit(solution)/shard_map/reshape | solution.py:30
  108.8 10.6 %copy.43 = f32[10976,192]{1,0:T(8,128)} copy(f32[10976,192]{0,1:T(8,128)} %bitcast.36) | data formatting | bytes 16859136 | tf_op jit(solution)/shard_map/reshape | solution.py:30
  119.4 59.5 %scatter_custom_fusion = f32[192,8064]{0,1:T(8,128)} fusion(s32[10976]{0:T(1024)S(1)} %fusion.22, f32[10976,192]{1,0:T(8,128)} %copy.43, f32[]{:T(128)} %constant.13.clone.1), kind=kCustom, calls=%fused_computation.29 | custom fusion | flops 2107392 | bytes 6193664 | tf_op jit(solution)/shard_map/scatter-add | solution.py:30
  179.0 1.3 slice.25
  180.3 0.3 copy.45
  180.7 0.1 collective-permute-start.1
  180.8 7.3 %fusion.3 = f32[192,6912]{0,1:T(8,128)} fusion(bf16[192,6912]{0,1:T(8,128)(2,1)} %copy.38, f32[192,8064]{0,1:T(8,128)} %scatter_custom_fusion, f32[6912]{0:T(1024)S(1)} %copy-done.2), kind=kLoop, calls=%fused_computation.16 | loop fusion | flops 3981312 | bytes 13298688 | tf_op jit(solution)/shard_map/add
  188.1 17.5 %collective-permute-done.1 = f32[192,1152]{1,0:T(8,128)S(1)} collective-permute-done((f32[192,1152]{1,0:T(8,128)S(1)}, f32[192,1152]{1,0:T(8,128)S(1)}, u32[]{:S(2)}, u32[]{:S(2)}) %collective-permute-start.1) | collective-permute-done | bytes 884768 | tf_op jit(solution)/shard_map/ppermute | solution.py:17
  205.6 0.4 copy.46
  206.0 14.7 %scatter_fusion = f32[192,6912]{0,1:T(8,128)} fusion(f32[192,6912]{0,1:T(8,128)} %fusion.3, s32[1152]{0:T(1024)S(1)} %compare_select_fusion.2, f32[1152,192]{1,0:T(8,128)S(1)} %copy.46), kind=kCustom, calls=%fused_computation.5 | custom fusion | flops 221184 | bytes 2658816 | tf_op jit(solution)/shard_map/scatter-add | solution.py:33
  220.7 7.0 %fusion.6 = bf16[192,6912]{0,1:T(8,128)(2,1)} fusion(f32[192,6912]{0,1:T(8,128)} %scatter_fusion, bf16[192,6912]{0,1:T(8,128)(2,1)} %copy.38), kind=kLoop, calls=%fused_computation.19 | loop fusion | flops 6635520 | bytes 10616832 | tf_op jit(solution)/shard_map/convert_element_type | solution.py:52
  227.7 5.7 gather_fusion.2
  233.4 0.3 copy.47
  233.7 2.0 collective-permute-start.2
  235.6 8.7 %collective-permute-done.2 = bf16[192,1152]{1,0:T(8,128)(2,1)S(1)} collective-permute-done((bf16[192,1152]{1,0:T(8,128)(2,1)S(1)}, bf16[192,1152]{1,0:T(8,128)(2,1)S(1)}, u32[]{:S(2)}, u32[]{:S(2)}) %collective-permute-start.2) | collective-permute-done | bytes 442400 | tf_op jit(solution)/shard_map/ppermute | solution.py:17
  244.3 0.2 copy.48
  244.5 4.7 pad_maximum_fusion.1
  249.2 28.3 %gather_fusion.3 = bf16[10976,192]{1,0:T(8,128)(2,1)} fusion(bf16[192,8064]{0,1:T(8,128)(2,1)} %pad_maximum_fusion.1, s32[11264]{0:T(1024)S(1)} %pad_clamp_fusion), kind=kCustom, calls=%fused_computation.3 | custom fusion | bytes 8473472 | tf_op jit(solution)/shard_map/gather | solution.py:25
  277.5 7.5 %copy.49 = bf16[10976,192]{0,1:T(8,128)(2,1)} copy(bf16[10976,192]{1,0:T(8,128)(2,1)} %gather_fusion.3) | data formatting | bytes 8429568 | tf_op jit(solution)/shard_map/gather | solution.py:25
  285.0 12.8 %reshape.71 = bf16[32,343,192]{1,0,2:T(8,128)(2,1)} reshape(bf16[10976,192]{0,1:T(8,128)(2,1)} %copy.49) | data formatting | bytes 8429568 | tf_op jit(solution)/shard_map/gather | solution.py:25
  297.8 9.0 %fusion.8 = f32[192,32,343]{2,1,0:T(8,128)} fusion(bf16[32,343,192]{1,0,2:T(8,128)(2,1)} %reshape.71, bf16[343,343]{1,0:T(8,128)(2,1)S(1)} %copy-done), kind=kOutput, calls=%fused_computation.21 | convolution fusion | flops 1445670912 | bytes 12879650 | tf_op jit(solution)/shard_map/wca,ea->wce/dot_general | solution.py:26
  306.8 11.1 %reshape.91 = f32[192,10976]{1,0:T(8,128)} reshape(f32[192,32,343]{2,1,0:T(8,128)} %fusion.8) | data formatting | bytes 16859136 | tf_op jit(solution)/shard_map/reshape | solution.py:30
  317.9 10.6 %copy.52 = f32[10976,192]{1,0:T(8,128)} copy(f32[10976,192]{0,1:T(8,128)} %bitcast.37) | data formatting | bytes 16859136 | tf_op jit(solution)/shard_map/reshape | solution.py:30
  328.5 59.1 %scatter_custom_fusion.2 = f32[192,8064]{0,1:T(8,128)} fusion(s32[10976]{0:T(1024)S(1)} %fusion.22, f32[10976,192]{1,0:T(8,128)} %copy.52, f32[]{:T(128)} %constant.13.clone.1), kind=kCustom, calls=%fused_computation.27 | custom fusion | flops 2107392 | bytes 6193664 | tf_op jit(solution)/shard_map/scatter-add | solution.py:30
  387.6 1.3 slice.27
  388.9 0.3 copy.53
  389.3 0.3 collective-permute-start.3
  389.6 7.3 %fusion = f32[192,6912]{0,1:T(8,128)} fusion(bf16[192,6912]{0,1:T(8,128)(2,1)} %fusion.6, f32[192,8064]{0,1:T(8,128)} %scatter_custom_fusion.2, f32[6912]{0:T(1024)S(1)} %copy-done.2), kind=kLoop, calls=%fused_computation.13 | loop fusion | flops 3981312 | bytes 13298688 | tf_op jit(solution)/shard_map/add.1
  396.9 15.2 %collective-permute-done.3 = f32[192,1152]{1,0:T(8,128)S(1)} collective-permute-done((f32[192,1152]{1,0:T(8,128)S(1)}, f32[192,1152]{1,0:T(8,128)S(1)}, u32[]{:S(2)}, u32[]{:S(2)}) %collective-permute-start.3) | collective-permute-done | bytes 884768 | tf_op jit(solution)/shard_map/ppermute | solution.py:17
  412.1 0.4 copy.54
  412.5 14.7 %scatter_fusion.1 = f32[192,6912]{0,1:T(8,128)} fusion(f32[192,6912]{0,1:T(8,128)} %fusion, s32[1152]{0:T(1024)S(1)} %compare_select_fusion.2, f32[1152,192]{1,0:T(8,128)S(1)} %copy.54), kind=kCustom, calls=%fused_computation.7 | custom fusion | flops 221184 | bytes 2658816 | tf_op jit(solution)/shard_map/scatter-add | solution.py:33
  427.2 8.4 %fusion.7 = bf16[192,6912]{0,1:T(8,128)(2,1)} fusion(bf16[192,6912]{0,1:T(8,128)(2,1)} %copy.38, f32[192,6912]{0,1:T(8,128)} %scatter_fusion.1, bf16[192,6912]{0,1:T(8,128)(2,1)} %fusion.6), kind=kLoop, calls=%fused_computation.20 | loop fusion | flops 9289728 | bytes 13271040 | tf_op jit(solution)/shard_map/convert_element_type | solution.py:59
  435.6 5.6 copy.55
  441.2 0.0 all-gather.2.cloned.1.call-update
  441.2 0.0 all-reduce.2.cloned.1.call-start
  441.3 12.4 %all-gather.2.cloned.1.call-done = bf16[384,6912]{1,0:T(8,128)(2,1)} async-done(((bf16[192,6912]{1,0:T(8,128)(2,1)}), bf16[384,6912]{1,0:T(8,128)(2,1)}) %all-gather.2.cloned.1.call-update) | async-done | bytes 5308432 | tf_op jit(solution)/shard_map/all_gather | solution.py:61
  453.7 6.5 %fusion.25 = f32[192,384]{1,0:T(8,128)} fusion(bf16[192,6912]{0,1:T(8,128)(2,1)} %fusion.7, bf16[384,6912]{1,0:T(8,128)(2,1)} %all-gather.2.cloned.1.call-done), kind=kOutput, calls=%fused_computation.55 | convolution fusion | flops 1019215872 | bytes 8257536 | tf_op jit(solution)/shard_map/dot_general | solution.py:63
  460.2 108.7 %all-reduce.2.cloned.1.call-done = f32[192,384]{1,0:T(8,128)} async-done(((f32[192,384]{1,0:T(8,128)}), f32[192,384]{1,0:T(8,128)}) %all-reduce.2.cloned.1.call-update) | async-done | bytes 294928 | tf_op jit(solution)/shard_map/psum | solution.py:66
  568.9 2.7 all_gather.7
  571.6 0.7 multiply_reduce_fusion
  573.0 0.8 convolution_subtract_fusion.2
  573.8 1.3 convolution_multiply_fusion.2
  575.1 0.7 convolution_multiply_fusion.3
  575.8 1.3 convolution_subtract_fusion.1
  577.0 1.3 convolution_multiply_fusion
  578.3 1.3 convolution_multiply_fusion.1
  579.6 1.3 convolution_subtract_fusion
  580.9 1.3 fusion.26
  582.2 3.9 fusion.19
  (16 shorter events, 0.1 us)
Async XLA Ops:
  6.5 82.2 %copy-start = (bf16[343,343]{1,0:T(8,128)(2,1)S(1)}, bf16[343,343]{1,0:T(8,128)(2,1)}, u32[]{:S(2)}) copy-start(bf16[343,343]{1,0:T(8,128)(2,1)} %param.6) | copy-start | bytes 705898
  6.5 19.3 %copy-start.1 = (s32[32,343]{1,0:T(8,128)S(1)}, s32[32,343]{1,0:T(8,128)}, u32[]{:S(2)}) copy-start(s32[32,343]{1,0:T(8,128)} %param.8) | copy-start | bytes 131716
  6.5 447.1 %all-gather.2.cloned.1.call-start = ((), (), s32[]{:S(2)}) async-start(), calls=%async_computation | async-start | bytes 7962624 | tf_op jit(solution)/shard_map/all_gather | solution.py:61
  18.8 16.4 %collective-permute-start = (bf16[192,1152]{1,0:T(8,128)(2,1)S(1)}, bf16[192,1152]{1,0:T(8,128)(2,1)S(1)}, u32[]{:S(2)}, u32[]{:S(2)}) collective-permute-start(bf16[192,1152]{1,0:T(8,128)(2,1)S(1)} %copy.37), channel_id=1, source_target_pairs={{0,30},{2,0},{4,2},{6,4},{8,6},{10,8},{12,10},{14,12},{16,14},{18,... | collective-permute-start | bytes 1327112 | tf_op jit(solution)/shard_map/ppermute | solution.py:17
  119.4 61.3 %copy-start.2 = (f32[6912]{0:T(1024)S(1)}, f32[6912]{0:T(1024)}, u32[]{:S(2)}) copy-start(f32[6912]{0:T(1024)} %param.7) | copy-start | bytes 82948
  180.7 24.9 %collective-permute-start.1 = (f32[192,1152]{1,0:T(8,128)S(1)}, f32[192,1152]{1,0:T(8,128)S(1)}, u32[]{:S(2)}, u32[]{:S(2)}) collective-permute-start(f32[192,1152]{1,0:T(8,128)S(1)} %copy.45), channel_id=1, source_target_pairs={{0,2},{2,4},{4,6},{6,8},{8,10},{10,12},{12,14},{14,16},{16,18},{18... | collective-permute-start | bytes 2654216 | tf_op jit(solution)/shard_map/ppermute | solution.py:17
  233.7 10.6 %collective-permute-start.2 = (bf16[192,1152]{1,0:T(8,128)(2,1)S(1)}, bf16[192,1152]{1,0:T(8,128)(2,1)S(1)}, u32[]{:S(2)}, u32[]{:S(2)}) collective-permute-start(bf16[192,1152]{1,0:T(8,128)(2,1)S(1)} %copy.47), channel_id=1, source_target_pairs={{0,30},{2,0},{4,2},{6,4},{8,6},{10,8},{12,10},{14,12},{16,14},{18,... | collective-permute-start | bytes 1327112 | tf_op jit(solution)/shard_map/ppermute | solution.py:17
  389.3 22.8 %collective-permute-start.3 = (f32[192,1152]{1,0:T(8,128)S(1)}, f32[192,1152]{1,0:T(8,128)S(1)}, u32[]{:S(2)}, u32[]{:S(2)}) collective-permute-start(f32[192,1152]{1,0:T(8,128)S(1)} %copy.53), channel_id=1, source_target_pairs={{0,2},{2,4},{4,6},{6,8},{8,10},{10,12},{12,14},{14,16},{16,18},{18... | collective-permute-start | bytes 2654216 | tf_op jit(solution)/shard_map/ppermute | solution.py:17
  441.2 127.6 %all-reduce.2.cloned.1.call-start = ((), (), s32[]{:S(2)}) async-start(), calls=%async_computation.1 | async-start | bytes 589824 | tf_op jit(solution)/shard_map/psum | solution.py:66
  573.0 9.1 %slice-start = ((s8[5308416]{0:T(1024)(128)(4,1)}), s8[4194304]{0:T(1024)(128)(4,1)S(1)}, s32[]{:S(2)}) async-start(s8[5308416]{0:T(1024)(128)(4,1)} %bitcast.38), calls=%async_computation.2 | async-start | bytes 8388608
  575.7 6.4 %slice-start.1 = ((s8[5308416]{0:T(1024)(128)(4,1)}), s8[1114112]{0:T(1024)(128)(4,1)S(1)}, s32[]{:S(2)}) async-start(s8[5308416]{0:T(1024)(128)(4,1)} %bitcast.38), calls=%async_computation.3 | async-start | bytes 2228224
Sparse Core Ops, SparseCore 0:
  441.4 12.2 all-gather.1
  460.3 108.5 all-reduce.1
where the time goes:
time: 605 us; the launch traced here: 593 us
  other arithmetic  189 us (31%)
  waiting for transfers between devices  171 us (28%)
  local copies, waits for them, and re-layouts  169 us (28%)
  matrix products  37.4 us (6%)
  between operations  14.8 us (2%)
  starting transfers between devices  9.32 us (2%)
    scatter-add x2, other arithmetic, apply_operator(): summed = jnp.zeros((width, owned + face_count), jnp.float32).at[:, cell_n...  119 us
    psum x1, waiting for transfers between devices, local(): margin_rows = lax.psum(partial_rows, 'brick')  109 us
    gather x6, local copies, waits for them, and re-layouts, apply_operator(): gathered = extended[:, cell_nodes]  97.3 us
    ppermute x4, waiting for transfers between devices, passed_along(): return lax.ppermute(value, axis, pairs)  50.3 us
    reshape x4, local copies, waits for them, and re-layouts, apply_operator(): products.reshape(width, -1)  43.3 us
    scatter-add x2, other arithmetic, apply_operator(): assembled = summed[:, :owned].at[:, face_map].add(returned)  29.5 us
    dot_general x2, matrix products, apply_operator(): jnp.einsum('wca,ea->wce', gathered, kinetic, preferred_element_type=jnp.f...  17.9 us
    all_gather x1, waiting for transfers between devices, local(): every = lax.all_gather(filtered, 'state', axis=0, tiled=True)  12.4 us
  transfers between devices with their start and end apart: 6, of which 6 were waited for; matrix products, arithmetic and copies ran while one was open for 3% of the time, Pallas kernels for 0%

commit v1 on v0

v1 whole, which is shorter than its diff:
```python
import functools
import jax
import jax.numpy as jnp
from jax import lax
from jax.experimental import pallas as pl
from jax.experimental.pallas import tpu as pltpu
from jax.sharding import PartitionSpec as P

NS_STEPS = 3
LANES = 128
BATCH = 16

cheb_center = 3.0
cheb_half = 7.0
epsilon = 1e-06

VMEM = pl.BlockSpec(memory_space=pltpu.VMEM)
SMEM = pl.BlockSpec(memory_space=pltpu.SMEM)
ANY = pl.BlockSpec(memory_space=pl.ANY)


def params(limit=40):
    return pltpu.CompilerParams(vmem_limit_bytes=limit << 20)


def passed_along(value, axis, steps):
    count = lax.axis_size(axis)
    pairs = [(source, (source + steps) % count) for source in range(count)]
    return lax.ppermute(value, axis, pairs)


def block_of(count):
    for size in (256, 128):
        if count % size == 0:
            return size
    return count


def identity(size):
    rows = lax.broadcasted_iota(jnp.int32, (size, size), 0)
    columns = lax.broadcasted_iota(jnp.int32, (size, size), 1)
    return (rows == columns).astype(jnp.bfloat16)


def across(left, right):
    return lax.dot_general(left, right, (((1,), (1,)), ((), ())), preferred_element_type=jnp.float32)


def split3(wide):
    first = wide.astype(jnp.bfloat16)
    rest = wide - first.astype(jnp.float32)
    second = rest.astype(jnp.bfloat16)
    third = (rest - second.astype(jnp.float32)).astype(jnp.bfloat16)
    return first, second, third


def across_wide(unit, wide):
    first, second, third = split3(wide)
    return across(unit, first) + (across(unit, second) + across(unit, third))


def padded_rows(block):
    width = block.shape[0]
    return jnp.concatenate([block, jnp.zeros((2 * LANES - width, block.shape[1]), block.dtype)], axis=0)


def store_nodes(ref, start, block, values):
    ref[pl.ds(2 * start, block, 2), :] = values[:, :LANES]
    ref[pl.ds(2 * start + 1, block, 2), :] = values[:, LANES:]


def load_nodes(ref, start, block):
    return jnp.concatenate([ref[pl.ds(2 * start, block, 2), :], ref[pl.ds(2 * start + 1, block, 2), :]], axis=1)


def pack(ref, count, width):
    low = ref[pl.ds(0, count, 2), :]
    high = ref[pl.ds(1, count, 2), :]
    rest = width - LANES
    fold = LANES // rest
    part = count // fold
    return low, jnp.concatenate([high[i * part : (i + 1) * part, :rest] for i in range(fold)], axis=1)


def unpack(packed, count, width):
    rest = width - LANES
    fold = LANES // rest
    part = count // fold
    low = packed[:count]
    high = jnp.concatenate([packed[count:, i * rest : (i + 1) * rest] for i in range(fold)], axis=0)
    return low, jnp.concatenate([high, jnp.zeros((count, LANES - rest), high.dtype)], axis=1)


def gather_face(face, source, target, count):
    step = 64

    def some(i, _):
        base = i * step
        for j in range(step):
            target[pl.ds(pl.multiple_of(2 * (base + j), 2), 2), :] = source[
                pl.ds(pl.multiple_of(face[base + j], 2), 2), :
            ]
        return 0

    lax.fori_loop(0, count // step, some, 0)


def add_face(face, source, target, count):
    step = BATCH

    def some(i, _):
        base = i * step
        places = [pl.multiple_of(face[base + j], 2) for j in range(step)]
        rows = [target[pl.ds(place, 2), :] for place in places]
        for j in range(step):
            target[pl.ds(places[j], 2), :] = rows[j] + source[pl.ds(pl.multiple_of(2 * (base + j), 2), 2), :]
        return 0

    lax.fori_loop(0, count // step, some, 0)


def prepare_kernel(width, face, states, potential, nodes, start, send, picked):
    owned = states.shape[1]
    count = face.shape[0]
    block = block_of(owned)
    unit = identity(block)

    def one(i, _):
        first = pl.multiple_of(i * block, block)
        mine = states[:, pl.ds(first, block)]
        store_nodes(nodes, first, block, across(unit, padded_rows(mine)))
        local = mine.astype(jnp.float32) * (potential[:, pl.ds(first, block)] - cheb_center)
        store_nodes(start, first, block, across_wide(unit, padded_rows(local)))
        return 0

    lax.fori_loop(0, owned // block, one, 0)
    gather_face(face, nodes, picked, count)
    low, high = pack(picked, count, width)
    send[:count, :] = low.astype(jnp.bfloat16)
    send[count:, :] = high.astype(jnp.bfloat16)


def operator_kernel(width, slots, cells, with_start, table, kinetic, ghost, nodes_in, *rest):
    if with_start:
        start_in, out, send, nodes, total, gathered, products, sems = rest
    else:
        out, send, nodes, total, gathered, products, sems = rest
    owned2 = nodes_in.shape[0]
    all2 = nodes.shape[0]
    count = (all2 - owned2) // 2
    copies = [pltpu.make_async_copy(nodes_in, nodes.at[pl.ds(0, owned2)], sems.at[0])]
    if with_start:
        copies.append(pltpu.make_async_copy(start_in, total.at[pl.ds(0, owned2)], sems.at[1]))
    for copy in copies:
        copy.start()
    low, high = unpack(ghost[...].astype(jnp.float32), count, width)
    nodes[pl.ds(owned2, count, 2), :] = low
    nodes[pl.ds(owned2 + 1, count, 2), :] = high
    total[pl.ds(owned2, 2 * count), :] = jnp.zeros((2 * count, LANES), jnp.float32)
    if not with_start:
        total[pl.ds(0, owned2), :] = jnp.zeros((owned2, LANES), jnp.float32)
    rows = gathered.shape[0] // 2
    gathered[pl.ds(2 * slots, 2 * (rows - slots)), :] = jnp.zeros((2 * (rows - slots), LANES), jnp.float32)
    for copy in copies:
        copy.wait()
    stride = table.shape[0] // cells

    def one(cell, _):
        mine = table.at[pl.ds(cell * stride, stride)]
        for a in range(slots):
            gathered[pl.ds(2 * a, 2), :] = nodes[pl.ds(pl.multiple_of(mine[a], 2), 2), :]
        values = jnp.concatenate(
            [gathered[pl.ds(0, rows, 2), :], gathered[pl.ds(1, rows, 2), :]], axis=1
        ).astype(jnp.bfloat16)
        result = jnp.dot(kinetic[...], values, preferred_element_type=jnp.float32)
        products[pl.ds(0, rows, 2), :] = result[:, :LANES]
        products[pl.ds(1, rows, 2), :] = result[:, LANES:]
        for begin in range(0, slots, BATCH):
            size = min(BATCH, slots - begin)
            places = [pl.multiple_of(mine[begin + j], 2) for j in range(size)]
            held = [total[pl.ds(place, 2), :] for place in places]
            for j in range(size):
                total[pl.ds(places[j], 2), :] = held[j] + products[pl.ds(2 * (begin + j), 2), :]
        return 0

    lax.fori_loop(0, cells, one, 0)
    back = pltpu.make_async_copy(total.at[pl.ds(0, owned2)], out, sems.at[0])
    back.start()
    low, high = pack(total.at[pl.ds(owned2, 2 * count)], count, width)
    send[:count, :] = low
    send[count:, :] = high
    back.wait()


def once_kernel(width, face, total, returned, nodes, send, spread, picked, sem):
    count = face.shape[0]
    copy = pltpu.make_async_copy(total, nodes, sem)
    copy.start()
    low, high = unpack(returned[...], count, width)
    spread[pl.ds(0, count, 2), :] = low
    spread[pl.ds(1, count, 2), :] = high
    copy.wait()
    add_face(face, spread, nodes, count)
    block = 2 * block_of(nodes.shape[0] // 2)

    def one(i, _):
        at = pl.ds(pl.multiple_of(i * block, block), block)
        nodes[at, :] = (nodes[at, :] / cheb_half).astype(jnp.bfloat16).astype(jnp.float32)
        return 0

    lax.fori_loop(0, nodes.shape[0] // block, one, 0)
    gather_face(face, nodes, picked, count)
    low, high = pack(picked, count, width)
    send[:count, :] = low.astype(jnp.bfloat16)
    send[count:, :] = high.astype(jnp.bfloat16)


def twice_kernel(width, face, total_in, returned, nodes, states, potential, filtered, total, spread, sem):
    owned = states.shape[1]
    count = face.shape[0]
    copy = pltpu.make_async_copy(total_in, total, sem)
    copy.start()
    low, high = unpack(returned[...], count, width)
    spread[pl.ds(0, count, 2), :] = low
    spread[pl.ds(1, count, 2), :] = high
    copy.wait()
    add_face(face, spread, total, count)
    block = block_of(owned)
    unit = identity(2 * LANES)

    def one(i, _):
        first = pl.multiple_of(i * block, block)
        at = pl.ds(first, block)
        once = across(unit, load_nodes(nodes, first, block).astype(jnp.bfloat16))[:width]
        summed = across_wide(unit, load_nodes(total, first, block))[:width]
        second = summed + (potential[:, at] - cheb_center) * once
        filtered[:, at] = ((2.0 / cheb_half) * second - states[:, at].astype(jnp.float32)).astype(jnp.bfloat16)
        return 0

    lax.fori_loop(0, owned // block, one, 0)


def summed_over(value, axis):
    count = lax.axis_size(axis)
    place = lax.axis_index(axis)
    radices = []
    left = count
    while left > 1:
        radix = 4 if left % 4 == 0 else 2 if left % 2 == 0 else left
        radices.append(radix)
        left //= radix
    shape = value.shape
    flat = value.reshape(-1, LANES)

    def exchange(stride, radix, give):
        digit = place // stride % radix

        def partner(index, step):
            here = index // stride % radix
            return index + ((here + step) % radix - here) * stride

        got = [
            lax.ppermute(give((digit + step) % radix), axis, [(i, partner(i, step)) for i in range(count)])
            for step in range(1, radix)
        ]
        return digit, got

    stride = 1
    trail = []
    for level, radix in enumerate(radices):
        if level == len(radices) - 1:
            _, got = exchange(stride, radix, lambda to: flat)
            flat = flat + functools.reduce(jnp.add, got)
        else:
            pieces = flat.reshape(radix, -1, LANES)
            take = lambda to: lax.dynamic_index_in_dim(pieces, to, 0, keepdims=False)
            digit, got = exchange(stride, radix, take)
            flat = take(digit) + functools.reduce(jnp.add, got)
            trail.append((stride, radix))
        stride *= radix
    for stride, radix in reversed(trail):
        digit, got = exchange(stride, radix, lambda to: flat)
        stacked = jnp.zeros((radix,) + flat.shape, flat.dtype)
        stacked = lax.dynamic_update_index_in_dim(stacked, flat, digit, 0)
        for step in range(1, radix):
            stacked = lax.dynamic_update_index_in_dim(stacked, got[step - 1], (digit - step) % radix, 0)
        flat = stacked.reshape(-1, LANES)
    return flat.reshape(shape)


def newton_schulz(margin, start, width):
    total = margin.shape[0]
    unit = jnp.eye(total, dtype=jnp.float32)
    scale = jnp.sqrt(jnp.sum(margin * margin) + epsilon)
    current = margin / scale
    product = functools.partial(jnp.dot, precision=lax.Precision.HIGHEST)
    factor = 3.0 * unit - current
    current = 0.5 * product(factor, current)
    inverse = 0.5 * factor
    for iteration in range(1, NS_STEPS - 1):
        factor = 3.0 * unit - product(inverse, current)
        current = 0.5 * product(factor, current)
        inverse = 0.5 * product(factor, inverse)
    rows = lax.dynamic_slice_in_dim(inverse, start, width, 0)
    factor = 3.0 * lax.dynamic_slice_in_dim(unit, start, width, 0) - product(rows, current)
    return 0.5 * product(factor, inverse)


def local(states, kinetic, potential, cell_nodes, face_map):
    width, owned = states.shape
    cells, slots = cell_nodes.shape
    count = face_map.shape[0]
    rows = -(-slots // 8) * 8
    stride = -(-slots // LANES) * LANES
    fold = LANES // (width - LANES)
    packed = count + count // fold
    face = 2 * face_map
    table = jnp.pad(2 * cell_nodes, ((0, 0), (0, stride - slots))).reshape(-1)
    matrix = jnp.pad(kinetic, ((0, rows - slots), (0, rows - slots)))
    lumped = potential[None, :]
    wide = jax.ShapeDtypeStruct((2 * owned, LANES), jnp.float32)
    sent = jax.ShapeDtypeStruct((packed, LANES), jnp.bfloat16)
    sent_wide = jax.ShapeDtypeStruct((packed, LANES), jnp.float32)
    spread = pltpu.VMEM((2 * count, LANES), jnp.float32)

    nodes, begun, send = pl.pallas_call(
        functools.partial(prepare_kernel, width),
        out_shape=(wide, wide, sent),
        in_specs=[SMEM, VMEM, VMEM],
        out_specs=(VMEM, VMEM, VMEM),
        scratch_shapes=[spread],
        compiler_params=params(),
    )(face, states, lumped)

    def operator(nodes, ghost, begun):
        args = (table, matrix, ghost, nodes) + (() if begun is None else (begun,))
        return pl.pallas_call(
            functools.partial(operator_kernel, width, slots, cells, begun is not None),
            out_shape=(wide, sent_wide),
            in_specs=[SMEM, VMEM, VMEM, ANY] + ([] if begun is None else [ANY]),
            out_specs=(ANY, VMEM),
            scratch_shapes=[
                pltpu.VMEM((2 * (owned + count), LANES), jnp.float32),
                pltpu.VMEM((2 * (owned + count), LANES), jnp.float32),
                pltpu.VMEM((2 * rows, LANES), jnp.float32),
                pltpu.VMEM((2 * rows, LANES), jnp.float32),
                pltpu.SemaphoreType.DMA((2,)),
            ],
            compiler_params=params(),
        )(*args)

    total, back = operator(nodes, passed_along(send, "brick", -1), begun)
    nodes, send = pl.pallas_call(
        functools.partial(once_kernel, width),
        out_shape=(wide, sent),
        in_specs=[SMEM, ANY, VMEM],
        out_specs=(VMEM, VMEM),
        scratch_shapes=[spread, spread, pltpu.SemaphoreType.DMA],
        compiler_params=params(),
    )(face, total, passed_along(back, "brick", 1))
    total, back = operator(nodes, passed_along(send, "brick", -1), None)
    filtered = pl.pallas_call(
        functools.partial(twice_kernel, width),
        out_shape=jax.ShapeDtypeStruct((width, owned), jnp.bfloat16),
        in_specs=[SMEM, ANY, VMEM, VMEM, VMEM, VMEM],
        out_specs=VMEM,
        scratch_shapes=[pltpu.VMEM((2 * owned, LANES), jnp.float32), spread, pltpu.SemaphoreType.DMA],
        compiler_params=params(),
    )(face, total, passed_along(back, "brick", 1), nodes, states, lumped)

    halves = lax.axis_size("state")
    place = lax.axis_index("state")
    parts = [filtered] + [passed_along(filtered, "state", step) for step in range(1, halves)]
    blocks = [across(filtered, part) for part in parts]
    reduced = summed_over(jnp.stack(blocks), "brick")
    return finish(reduced, parts, halves, place, width)


def finish(reduced, parts, halves, place, width):
    own_rows = jnp.zeros((halves, width, width), jnp.float32)
    for step in range(halves):
        own_rows = lax.dynamic_update_index_in_dim(own_rows, reduced[step], (place - step) % halves, 0)
    row_block = own_rows.transpose(1, 0, 2).reshape(width, -1)
    margin = jnp.zeros((halves, width, halves * width), jnp.float32)
    margin = lax.dynamic_update_index_in_dim(margin, row_block, place, 0)
    for step in range(1, halves):
        margin = lax.dynamic_update_index_in_dim(
            margin, passed_along(row_block, "state", step), (place - step) % halves, 0
        )
    margin = margin.reshape(halves * width, -1)
    root = newton_schulz(margin, place * width, width).astype(jnp.bfloat16)
    result = 0.0
    for step, part in enumerate(parts):
        columns = lax.dynamic_slice_in_dim(root, (place - step) % halves * width, width, 1)
        result = result + jnp.dot(columns, part, preferred_element_type=jnp.float32)
    return result


def solution(mesh):
    in_specs = (P("state", "brick"), P(), P("brick"), P("brick", None), P("brick"))
    out_specs = P("state", "brick")
    return jax.shard_map(local, mesh=mesh, in_specs=in_specs, out_specs=out_specs, check_vma=False)
```

time: 605 us -> 247 us (0.41); the launches traced: 593 us -> 246 us
  other arithmetic: 189 us -> 2.38 us
  local copies, waits for them, and re-layouts: 169 us -> 21.7 us
  Pallas kernels: 0 us -> 104 us
  waiting for transfers between devices: 171 us -> 82.8 us
  matrix products: 37.4 us -> 16.2 us
  between operations: 14.8 us -> 1.1 us
  starting transfers between devices: 9.32 us -> 17.8 us
    scatter-add x4 -> x0, other arithmetic: 148 us -> none  [the longest x2 119 us: apply_operator(): summed = jnp.zeros((width, owned + face_count), jnp.float32).at[:, cell_n...]
    gather x10 -> x0, local copies, waits for them, and re-layouts: 109 us -> none  [the longest x6 97.3 us: apply_operator(): gathered = extended[:, cell_nodes]]
    psum x1 -> x0, waiting for transfers between devices: 109 us -> none  [local(): margin_rows = lax.psum(partial_rows, 'brick')]
    pallas_call x0 -> x5, Pallas kernels: none -> 104 us  [the longest x2 69 us: operator(): pl.pallas_call(functools.partial(operator_kernel, width, slots, cells, be...]
    reshape x5 -> x2, local copies, waits for them, and re-layouts: 43.5 us -> 1.01 us  [the longest x1 1 us: finish(): row_block = own_rows.transpose(1, 0, 2).reshape(width, -1)]
    dot_general x12 -> x10, matrix products: 37.4 us -> 16.2 us  [the longest x2 6.02 us: finish(): result = result + jnp.dot(columns, part, preferred_element_type=jnp.float32)]
    ppermute x4 -> x6, waiting for transfers between devices: 50.3 us -> 70.3 us  [passed_along(): return lax.ppermute(value, axis, pairs)]
    convert_element_type x2 -> x0, other arithmetic: 15.4 us -> none  [the longest x1 8.41 us: local(): filtered = (2.0 * (second - cheb_center * filtered_once.astype(jnp.float3...]
  transfers between devices with their start and end apart: 6 -> 15, of which waited for: 6 -> 13; matrix products, arithmetic and copies ran while one was open for 3% -> 1% of each run, Pallas kernels for 0% -> 0%
where the time goes in v1:
time: 247 us; the launch traced here: 246 us
  Pallas kernels  104 us (42%)
  waiting for transfers between devices  82.8 us (34%)
  local copies, waits for them, and re-layouts  21.7 us (9%)
  starting transfers between devices  17.8 us (7%)
  matrix products  16.2 us (7%)
    ppermute x6, waiting for transfers between devices, passed_along(): return lax.ppermute(value, axis, pairs)  70.3 us
    pallas_call x2, Pallas kernels, operator(): pl.pallas_call(functools.partial(operator_kernel, width, slots, cells, be...  69 us
    pallas_call x1, Pallas kernels, local(): pl.pallas_call(functools.partial(twice_kernel, width), out_shape=jax.Shap...  14.8 us
    pallas_call x1, Pallas kernels, local(): pl.pallas_call(functools.partial(prepare_kernel, width), out_shape=(wide,...  13.3 us
    ppermute x9, waiting for transfers between devices, exchange(): lax.ppermute(give((digit + step) % radix), axis, [(i, partner(i, step)) f...  12.5 us
    unnamed x16, local copies, waits for them, and re-layouts  10.4 us
    ppermute x9, starting transfers between devices, exchange(): lax.ppermute(give((digit + step) % radix), axis, [(i, partner(i, step)) f...  9 us
    ppermute x6, starting transfers between devices, passed_along(): return lax.ppermute(value, axis, pairs)  8.81 us
  transfers between devices with their start and end apart: 15, of which 13 were waited for; matrix products, arithmetic and copies ran while one was open for 1% of the time, Pallas kernels for 0%

profile of v1, /device:TPU:0, one launch (start us, length us, event | category | flops | bytes accessed | tf_op | source)
XLA Modules:
  0.0 246.4 jit_solution(16367835782763643940)
XLA Ops:
  0.0 0.7 broadcast_multiply_fusion.1.face
  0.7 0.8 broadcast_in_dim.38.potential
  1.5 0.0 copy-start.1
  1.5 1.7 copy-done.1
  3.2 13.3 %shard_map.55 = (f32[13824,128]{1,0:T(8,128)S(1)}, f32[13824,128]{1,0:T(8,128)}, bf16[1728,128]{1,0:T(8,128)(2,1)S(1)}) custom-call(s32[1152]{0:T(1024)S(1)} %broadcast_multiply_fusion.1.face, bf16[192,6912]{1,0:T(8,128)(2,1)S(1)} %copy-done.1, f32[1,6912]{1,0:T(1,128)S(1)} %broadcast_in_dim.38.potential), custom_call_target="tpu_custom_call" | custom-call | tf_op jit(solution)/shard_map/pallas_call | solution.py:326
  16.5 2.9 %copy-done.4 = f32[13824,128]{1,0:T(8,128)} copy-done((f32[13824,128]{1,0:T(8,128)}, f32[13824,128]{1,0:T(8,128)S(1)}, u32[]{:S(2)}) %copy-start.4) | copy-done | bytes 7077912
  19.4 6.9 %collective-permute-start = (bf16[1728,128]{1,0:T(8,128)(2,1)S(1)}, bf16[1728,128]{1,0:T(8,128)(2,1)S(1)}, u32[]{:S(2)}, u32[]{:S(2)}) collective-permute-start(bf16[1728,128]{1,0:T(8,128)(2,1)S(1)} %get-tuple-element.14), channel_id=1, source_target_pairs={{0,30},{2,0},{4,2},{6,4},{8,6},{10,8},{12,10},{14,12},{16,14},{18,... | collective-permute-start | bytes 1327112 | tf_op jit(solution)/shard_map/ppermute | solution.py:29
  26.4 9.3 %collective-permute-done.ghost = bf16[1728,128]{1,0:T(8,128)(2,1)S(1)} collective-permute-done((bf16[1728,128]{1,0:T(8,128)(2,1)S(1)}, bf16[1728,128]{1,0:T(8,128)(2,1)S(1)}, u32[]{:S(2)}, u32[]{:S(2)}) %collective-permute-start) | collective-permute-done | bytes 442400 | tf_op jit(solution)/shard_map/ppermute | solution.py:29
  35.8 35.5 %shard_map.56 = (f32[13824,128]{1,0:T(8,128)S(1)}, f32[1728,128]{1,0:T(8,128)S(1)}) custom-call(s32[12288]{0:T(1024)S(1)} %reshape.24.table, bf16[344,344]{1,0:T(8,128)(2,1)S(1)} %pad.9.kinetic, bf16[1728,128]{1,0:T(8,128)(2,1)S(1)} %collective-permute-done.ghost, f32[13824,128]{1,0:T(8,128)} %copy-done.4, f32[13824,128]{1,0:T(8,128)} %get-tuple-element.16.rest_0_), custom_call_target="tpu_custom_call" | custom-call | tf_op jit(solution)/shard_map/pallas_call | solution.py:337
  71.3 2.9 %copy-done.3 = f32[13824,128]{1,0:T(8,128)} copy-done((f32[13824,128]{1,0:T(8,128)}, f32[13824,128]{1,0:T(8,128)S(1)}, u32[]{:S(2)}) %copy-start.3) | copy-done | bytes 7077912
  74.1 0.0 collective-permute-start.1
  74.1 24.8 %collective-permute-done.1.returned = f32[1728,128]{1,0:T(8,128)S(1)} collective-permute-done((f32[1728,128]{1,0:T(8,128)S(1)}, f32[1728,128]{1,0:T(8,128)S(1)}, u32[]{:S(2)}, u32[]{:S(2)}) %collective-permute-start.1) | collective-permute-done | bytes 884768 | tf_op jit(solution)/shard_map/ppermute | solution.py:29
  99.0 7.4 %shard_map.57 = (f32[13824,128]{1,0:T(8,128)S(1)}, bf16[1728,128]{1,0:T(8,128)(2,1)S(1)}) custom-call(s32[1152]{0:T(1024)S(1)} %broadcast_multiply_fusion.1.face, f32[13824,128]{1,0:T(8,128)} %copy-done.3, f32[1728,128]{1,0:T(8,128)S(1)} %collective-permute-done.1.returned), custom_call_target="tpu_custom_call" | custom-call | tf_op jit(solution)/shard_map/pallas_call | solution.py:353
  106.4 2.9 %copy-done = f32[13824,128]{1,0:T(8,128)} copy-done((f32[13824,128]{1,0:T(8,128)}, f32[13824,128]{1,0:T(8,128)S(1)}, u32[]{:S(2)}) %copy-start) | copy-done | bytes 7077912
  109.3 1.7 collective-permute-start.2
  111.0 8.6 %collective-permute-done.2.ghost = bf16[1728,128]{1,0:T(8,128)(2,1)S(1)} collective-permute-done((bf16[1728,128]{1,0:T(8,128)(2,1)S(1)}, bf16[1728,128]{1,0:T(8,128)(2,1)S(1)}, u32[]{:S(2)}, u32[]{:S(2)}) %collective-permute-start.2) | collective-permute-done | bytes 442400 | tf_op jit(solution)/shard_map/ppermute | solution.py:29
  119.7 33.5 %shard_map.58 = (f32[13824,128]{1,0:T(8,128)S(1)}, f32[1728,128]{1,0:T(8,128)S(1)}) custom-call(s32[12288]{0:T(1024)S(1)} %reshape.24.table, bf16[344,344]{1,0:T(8,128)(2,1)S(1)} %pad.9.kinetic, bf16[1728,128]{1,0:T(8,128)(2,1)S(1)} %collective-permute-done.2.ghost, f32[13824,128]{1,0:T(8,128)} %copy-done), custom_call_target="tpu_custom_call" | custom-call | tf_op jit(solution)/shard_map/pallas_call | solution.py:337
  153.2 0.1 collective-permute-start.3
  153.2 22.5 %collective-permute-done.3.returned = f32[1728,128]{1,0:T(8,128)S(1)} collective-permute-done((f32[1728,128]{1,0:T(8,128)S(1)}, f32[1728,128]{1,0:T(8,128)S(1)}, u32[]{:S(2)}, u32[]{:S(2)}) %collective-permute-start.3) | collective-permute-done | bytes 884768 | tf_op jit(solution)/shard_map/ppermute | solution.py:29
  175.8 14.8 %shard_map.59 = bf16[192,6912]{1,0:T(8,128)(2,1)S(1)} custom-call(s32[1152]{0:T(1024)S(1)} %broadcast_multiply_fusion.1.face, f32[13824,128]{1,0:T(8,128)S(1)} %get-tuple-element.21.total_in, f32[1728,128]{1,0:T(8,128)S(1)} %collective-permute-done.3.returned, f32[13824,128]{1,0:T(8,128)} %copy-done, bf16[192,6912]{1,0:T(8,128)(2,1)S(1)} %copy-done.2, ...), custom_call_target="tpu_custom_call" | custom-call | tf_op jit(solution)/shard_map/pallas_call | solution.py:362
  190.6 0.1 collective-permute-start.4
  190.7 0.9 convolution_bitcast_fusion.1
  191.6 4.1 %collective-permute-done.4 = bf16[192,6912]{1,0:T(8,128)(2,1)} collective-permute-done((bf16[192,6912]{1,0:T(8,128)(2,1)S(1)}, bf16[192,6912]{1,0:T(8,128)(2,1)}, u32[]{:S(2)}, u32[]{:S(2)}) %collective-permute-start.4) | collective-permute-done | bytes 2654240 | tf_op jit(solution)/shard_map/ppermute | solution.py:29
  195.7 2.6 %convolution_bitcast_fusion = f32[1,192,192]{2,1,0:T(8,128)S(1)} fusion(bf16[192,6912]{1,0:T(8,128)(2,1)S(1)} %shard_map.59, bf16[192,6912]{1,0:T(8,128)(2,1)} %collective-permute-done.4), kind=kOutput, calls=%fused_computation.8 | convolution fusion | flops 509607936 | bytes 5455872 | tf_op jit(solution)/shard_map/dot_general | solution.py:46
  198.4 0.2 reshape_reshape.4
  198.6 0.1 collective-permute-start.5
  198.7 0.1 collective-permute-start.6
  198.8 2.8 %collective-permute-start.7 = (f32[144,128]{1,0:T(8,128)S(1)}, f32[144,128]{1,0:T(8,128)S(1)}, u32[]{:S(2)}, u32[]{:S(2)}) collective-permute-start(f32[144,128]{1,0:T(8,128)S(1)} %get-tuple-element.30), channel_id=1, source_target_pairs={{0,6},{2,0},{4,2},{6,4},{8,14},{10,8},{12,10},{14,12},{16,22},{18,... | collective-permute-start | bytes 221192 | tf_op jit(solution)/shard_map/ppermute | solution.py:263
  201.6 3.1 %collective-permute-done.5 = f32[144,128]{1,0:T(8,128)S(1)} collective-permute-done((f32[144,128]{1,0:T(8,128)S(1)}, f32[144,128]{1,0:T(8,128)S(1)}, u32[]{:S(2)}, u32[]{:S(2)}) %collective-permute-start.5) | collective-permute-done | bytes 73760 | tf_op jit(solution)/shard_map/ppermute | solution.py:263
  204.7 0.0 collective-permute-done.6
  204.7 0.0 collective-permute-done.7
  204.7 0.8 collective-permute-start.10
  205.5 1.3 collective-permute-start.8
  206.8 0.0 collective-permute-start.9
  206.8 3.5 %collective-permute-done.10 = f32[144,128]{1,0:T(8,128)S(1)} collective-permute-done((f32[144,128]{1,0:T(8,128)S(1)}, f32[144,128]{1,0:T(8,128)S(1)}, u32[]{:S(2)}, u32[]{:S(2)}) %collective-permute-start.10) | collective-permute-done | bytes 73760 | tf_op jit(solution)/shard_map/ppermute | solution.py:263
  210.3 1.3 collective-permute-done.8
  211.6 1.7 collective-permute-done.9
  213.4 2.0 collective-permute-start.11
  215.4 0.5 collective-permute-start.12
  215.9 1.5 collective-permute-start.13
  217.3 1.5 collective-permute-done.11
  218.9 0.9 collective-permute-done.12
  219.8 0.5 collective-permute-done.13
  220.2 0.7 fusion.23
  220.9 0.3 slice.13
  221.2 1.2 slice.15
  222.5 0.1 broadcast_in_dim.36
  222.6 2.8 %dynamic_update_slice.31 = f32[2,192,192]{2,0,1:T(2,128)S(1)} dynamic-update-slice(f32[2,192,192]{2,0,1:T(2,128)S(1)} %broadcast_in_dim.36, f32[1,192,192]{2,0,1:T(1,128)S(1)} %slice.13, s32[]{:T(128)S(6)} %select_n.112, s32[]{:T(128)} %constant.129.clone.1, s32[]{:T(128)} %constant.129.clone.1) | dynamic-update-slice | bytes 294916 | tf_op jit(solution)/shard_map/jit(dynamic_update_index_in_dim)/dynamic_update_slice | solution.py:382
  225.4 2.8 %dynamic_update_slice.32 = f32[2,192,192]{2,0,1:T(2,128)S(1)} dynamic-update-slice(f32[2,192,192]{2,0,1:T(2,128)S(1)} %dynamic_update_slice.31, f32[1,192,192]{2,0,1:T(1,128)S(1)} %slice.15, s32[]{:T(128)S(6)} %select_n.114, s32[]{:T(128)} %constant.129.clone.1, s32[]{:T(128)} %constant.129.clone.1) | dynamic-update-slice | bytes 294916 | tf_op jit(solution)/shard_map/jit(dynamic_update_index_in_dim)/dynamic_update_slice | solution.py:382
  228.1 1.0 reshape.25
  229.1 0.7 iota_compare_fusion.1
  229.8 0.3 broadcast_in_dim.43
  230.2 0.8 collective-permute-done.14
  231.0 1.0 bitcast_dynamic-update-slice_fusion
  232.0 0.8 multiply_reduce_fusion
  233.5 0.1 select_subtract_fusion.1
  233.6 1.3 convolution_multiply_fusion.2
  234.9 1.3 convolution_subtract_fusion
  236.2 1.3 convolution_multiply_fusion.1
  237.5 1.3 convolution_multiply_fusion
  238.8 0.8 convolution_subtract_fusion.1
  239.6 0.8 fusion
  240.3 2.7 %fusion.11 = f32[192,6912]{1,0:T(8,128)S(1)} fusion(bf16[192,6912]{1,0:T(8,128)(2,1)} %collective-permute-done.4, bf16[192,384]{1,0:T(8,128)(2,1)S(1)} %fusion, s32[]{:T(128)S(6)} %select_n.117), kind=kOutput, calls=%fused_computation.26 | convolution fusion | flops 509607936 | bytes 8060932 | tf_op jit(solution)/shard_map/dot_general | solution.py:395
  243.0 3.4 %convolution_add_fusion = f32[192,6912]{1,0:T(8,128)} fusion(f32[192,6912]{1,0:T(8,128)S(1)} %fusion.11, bf16[192,6912]{1,0:T(8,128)(2,1)S(1)} %shard_map.59, bf16[192,384]{1,0:T(8,128)(2,1)S(1)} %fusion, s32[]{:T(128)S(6)} %select_n.116), kind=kOutput, calls=%fused_computation | convolution fusion | flops 510935040 | bytes 13369348 | tf_op jit(solution)/shard_map/dot_general | solution.py:395
  (27 shorter events, 0.3 us)
Async XLA Ops:
  0.0 26.3 %copy-start.7 = (s32[32,343]{1,0:T(8,128)S(1)}, s32[32,343]{1,0:T(8,128)}, u32[]{:S(2)}) copy-start(s32[32,343]{1,0:T(8,128)} %param.8) | copy-start | bytes 131716
  1.5 1.8 copy-start.1
  3.2 23.2 %copy-start.6 = (bf16[343,343]{1,0:T(8,128)(2,1)S(1)}, bf16[343,343]{1,0:T(8,128)(2,1)}, u32[]{:S(2)}) copy-start(bf16[343,343]{1,0:T(8,128)(2,1)} %param.6) | copy-start | bytes 705898
  16.5 2.9 %copy-start.4 = (f32[13824,128]{1,0:T(8,128)}, f32[13824,128]{1,0:T(8,128)S(1)}, u32[]{:S(2)}) copy-start(f32[13824,128]{1,0:T(8,128)S(1)} %get-tuple-element.15.nodes_in) | copy-start | bytes 21233668
  19.4 16.4 %collective-permute-start = (bf16[1728,128]{1,0:T(8,128)(2,1)S(1)}, bf16[1728,128]{1,0:T(8,128)(2,1)S(1)}, u32[]{:S(2)}, u32[]{:S(2)}) collective-permute-start(bf16[1728,128]{1,0:T(8,128)(2,1)S(1)} %get-tuple-element.14), channel_id=1, source_target_pairs={{0,30},{2,0},{4,2},{6,4},{8,6},{10,8},{12,10},{14,12},{16,14},{18,... | collective-permute-start | bytes 1327112 | tf_op jit(solution)/shard_map/ppermute | solution.py:29
  71.3 2.9 %copy-start.3 = (f32[13824,128]{1,0:T(8,128)}, f32[13824,128]{1,0:T(8,128)S(1)}, u32[]{:S(2)}) copy-start(f32[13824,128]{1,0:T(8,128)S(1)} %get-tuple-element.17.total) | copy-start | bytes 21233668
  74.1 24.8 %collective-permute-start.1 = (f32[1728,128]{1,0:T(8,128)S(1)}, f32[1728,128]{1,0:T(8,128)S(1)}, u32[]{:S(2)}, u32[]{:S(2)}) collective-permute-start(f32[1728,128]{1,0:T(8,128)S(1)} %get-tuple-element.18), channel_id=1, source_target_pairs={{0,2},{2,4},{4,6},{6,8},{8,10},{10,12},{12,14},{14,16},{16,18},{18... | collective-permute-start | bytes 2654216 | tf_op jit(solution)/shard_map/ppermute | solution.py:29
  106.4 2.9 %copy-start = (f32[13824,128]{1,0:T(8,128)}, f32[13824,128]{1,0:T(8,128)S(1)}, u32[]{:S(2)}) copy-start(f32[13824,128]{1,0:T(8,128)S(1)} %get-tuple-element.20.nodes_in.nodes) | copy-start | bytes 21233668
  109.3 10.4 %collective-permute-start.2 = (bf16[1728,128]{1,0:T(8,128)(2,1)S(1)}, bf16[1728,128]{1,0:T(8,128)(2,1)S(1)}, u32[]{:S(2)}, u32[]{:S(2)}) collective-permute-start(bf16[1728,128]{1,0:T(8,128)(2,1)S(1)} %get-tuple-element.19), channel_id=1, source_target_pairs={{0,30},{2,0},{4,2},{6,4},{8,6},{10,8},{12,10},{14,12},{16,14},{18,... | collective-permute-start | bytes 1327112 | tf_op jit(solution)/shard_map/ppermute | solution.py:29
  119.7 56.1 %copy-start.2 = (bf16[192,6912]{1,0:T(8,128)(2,1)S(1)}, bf16[192,6912]{1,0:T(8,128)(2,1)}, u32[]{:S(2)}) copy-start(bf16[192,6912]{1,0:T(8,128)(2,1)} %states.3) | copy-start | bytes 7962628
  153.2 22.6 %collective-permute-start.3 = (f32[1728,128]{1,0:T(8,128)S(1)}, f32[1728,128]{1,0:T(8,128)S(1)}, u32[]{:S(2)}, u32[]{:S(2)}) collective-permute-start(f32[1728,128]{1,0:T(8,128)S(1)} %get-tuple-element.22), channel_id=1, source_target_pairs={{0,2},{2,4},{4,6},{6,8},{8,10},{10,12},{12,14},{14,16},{16,18},{18... | collective-permute-start | bytes 2654216 | tf_op jit(solution)/shard_map/ppermute | solution.py:29
  190.6 5.2 %collective-permute-start.4 = (bf16[192,6912]{1,0:T(8,128)(2,1)S(1)}, bf16[192,6912]{1,0:T(8,128)(2,1)}, u32[]{:S(2)}, u32[]{:S(2)}) collective-permute-start(bf16[192,6912]{1,0:T(8,128)(2,1)S(1)} %shard_map.59), channel_id=1, source_target_pairs={{0,1},{1,0},{2,3},{3,2},{4,5},{5,4},{6,7},{7,6},{8,9},{9,8},{10,11... | collective-permute-start | bytes 7962632 | tf_op jit(solution)/shard_map/ppermute | solution.py:29
  198.6 6.0 %collective-permute-start.5 = (f32[144,128]{1,0:T(8,128)S(1)}, f32[144,128]{1,0:T(8,128)S(1)}, u32[]{:S(2)}, u32[]{:S(2)}) collective-permute-start(f32[144,128]{1,0:T(8,128)S(1)} %get-tuple-element.31), channel_id=1, source_target_pairs={{0,2},{2,4},{4,6},{6,0},{8,10},{10,12},{12,14},{14,8},{16,18},{18,... | collective-permute-start | bytes 221192 | tf_op jit(solution)/shard_map/ppermute | solution.py:263
  198.7 6.0 %collective-permute-start.6 = (f32[144,128]{1,0:T(8,128)S(1)}, f32[144,128]{1,0:T(8,128)S(1)}, u32[]{:S(2)}, u32[]{:S(2)}) collective-permute-start(f32[144,128]{1,0:T(8,128)S(1)} %get-tuple-element.29), channel_id=1, source_target_pairs={{0,4},{2,6},{4,0},{6,2},{8,12},{10,14},{12,8},{14,10},{16,20},{18,... | collective-permute-start | bytes 221192 | tf_op jit(solution)/shard_map/ppermute | solution.py:263
  198.8 5.9 %collective-permute-start.7 = (f32[144,128]{1,0:T(8,128)S(1)}, f32[144,128]{1,0:T(8,128)S(1)}, u32[]{:S(2)}, u32[]{:S(2)}) collective-permute-start(f32[144,128]{1,0:T(8,128)S(1)} %get-tuple-element.30), channel_id=1, source_target_pairs={{0,6},{2,0},{4,2},{6,4},{8,14},{10,8},{12,10},{14,12},{16,22},{18,... | collective-permute-start | bytes 221192 | tf_op jit(solution)/shard_map/ppermute | solution.py:263
  204.7 5.6 %collective-permute-start.10 = (f32[144,128]{1,0:T(8,128)S(1)}, f32[144,128]{1,0:T(8,128)S(1)}, u32[]{:S(2)}, u32[]{:S(2)}) collective-permute-start(f32[144,128]{1,0:T(8,128)S(1)} %bitcast_add_fusion), channel_id=1, source_target_pairs={{0,24},{2,26},{4,28},{6,30},{8,0},{10,2},{12,4},{14,6},{16,8},{18,... | collective-permute-start | bytes 221192 | tf_op jit(solution)/shard_map/ppermute | solution.py:263
  205.5 6.2 %collective-permute-start.8 = (f32[144,128]{1,0:T(8,128)S(1)}, f32[144,128]{1,0:T(8,128)S(1)}, u32[]{:S(2)}, u32[]{:S(2)}) collective-permute-start(f32[144,128]{1,0:T(8,128)S(1)} %bitcast_add_fusion), channel_id=1, source_target_pairs={{0,8},{2,10},{4,12},{6,14},{8,16},{10,18},{12,20},{14,22},{16,24},... | collective-permute-start | bytes 221192 | tf_op jit(solution)/shard_map/ppermute | solution.py:263
  206.8 6.5 %collective-permute-start.9 = (f32[144,128]{1,0:T(8,128)S(1)}, f32[144,128]{1,0:T(8,128)S(1)}, u32[]{:S(2)}, u32[]{:S(2)}) collective-permute-start(f32[144,128]{1,0:T(8,128)S(1)} %bitcast_add_fusion), channel_id=1, source_target_pairs={{0,16},{2,18},{4,20},{6,22},{8,24},{10,26},{12,28},{14,30},{16,0},... | collective-permute-start | bytes 221192 | tf_op jit(solution)/shard_map/ppermute | solution.py:263
  213.4 5.5 %collective-permute-start.11 = (f32[144,128]{1,0:T(8,128)S(1)}, f32[144,128]{1,0:T(8,128)S(1)}, u32[]{:S(2)}, u32[]{:S(2)}) collective-permute-start(f32[144,128]{1,0:T(8,128)S(1)} %get-tuple-element.26), channel_id=1, source_target_pairs={{0,2},{2,4},{4,6},{6,0},{8,10},{10,12},{12,14},{14,8},{16,18},{18,... | collective-permute-start | bytes 221192 | tf_op jit(solution)/shard_map/ppermute | solution.py:263
  215.4 4.4 %collective-permute-start.12 = (f32[144,128]{1,0:T(8,128)S(1)}, f32[144,128]{1,0:T(8,128)S(1)}, u32[]{:S(2)}, u32[]{:S(2)}) collective-permute-start(f32[144,128]{1,0:T(8,128)S(1)} %get-tuple-element.26), channel_id=1, source_target_pairs={{0,4},{2,6},{4,0},{6,2},{8,12},{10,14},{12,8},{14,10},{16,20},{18,... | collective-permute-start | bytes 221192 | tf_op jit(solution)/shard_map/ppermute | solution.py:263
  215.9 4.4 %collective-permute-start.13 = (f32[144,128]{1,0:T(8,128)S(1)}, f32[144,128]{1,0:T(8,128)S(1)}, u32[]{:S(2)}, u32[]{:S(2)}) collective-permute-start(f32[144,128]{1,0:T(8,128)S(1)} %get-tuple-element.26), channel_id=1, source_target_pairs={{0,6},{2,0},{4,2},{6,4},{8,14},{10,8},{12,10},{14,12},{16,22},{18,... | collective-permute-start | bytes 221192 | tf_op jit(solution)/shard_map/ppermute | solution.py:263
  229.1 1.9 collective-permute-start.14
  234.9 3.9 %copy-start.5 = (pred[384,384]{1,0:T(32,128)(4,1)S(1)}, pred[384,384]{1,0:T(32,128)(4,1)}, u32[]{:S(2)}) copy-start(pred[384,384]{1,0:T(32,128)(4,1)} %iota_compare_fusion.1) | copy-start | bytes 442372

commit v2 on v0

v2 whole, which is shorter than its diff:
```python
import functools
import jax
import jax.numpy as jnp
from jax import lax
from jax.experimental import pallas as pl
from jax.experimental.pallas import tpu as pltpu
from jax.sharding import PartitionSpec as P

NS_STEPS = 3
LANES = 128
BATCH = 8

cheb_center = 3.0
cheb_half = 7.0
epsilon = 1e-06

VMEM = pl.BlockSpec(memory_space=pltpu.VMEM)
SMEM = pl.BlockSpec(memory_space=pltpu.SMEM)
ANY = pl.BlockSpec(memory_space=pl.ANY)


def called(kernel, shapes, in_specs, scratch, microseconds, limit, out_specs=None, **options):
    return pl.pallas_call(
        kernel,
        out_shape=shapes,
        in_specs=in_specs,
        out_specs=out_specs or (VMEM,) * len(shapes),
        scratch_shapes=scratch,
        compiler_params=pltpu.CompilerParams(vmem_limit_bytes=limit << 20),
        cost_estimate=pl.CostEstimate(
            flops=int(microseconds * 4e8), bytes_accessed=int(microseconds * 3e6), transcendentals=0
        ),
        **options,
    )


def passed_along(value, axis, steps):
    count = lax.axis_size(axis)
    pairs = [(source, (source + steps) % count) for source in range(count)]
    return lax.ppermute(value, axis, pairs)


def rounded_up(count, unit):
    return -(-count // unit) * unit


def block_of(count):
    for size in (256, 128):
        if count % size == 0:
            return size
    return count


def identity(size):
    rows = lax.broadcasted_iota(jnp.int32, (size, size), 0)
    columns = lax.broadcasted_iota(jnp.int32, (size, size), 1)
    return (rows == columns).astype(jnp.bfloat16)


def across(left, right):
    return lax.dot_general(left, right, (((1,), (1,)), ((), ())), preferred_element_type=jnp.float32)


def across_wide(unit, wide):
    first = wide.astype(jnp.bfloat16)
    rest = wide - first.astype(jnp.float32)
    second = rest.astype(jnp.bfloat16)
    third = (rest - second.astype(jnp.float32)).astype(jnp.bfloat16)
    return across(unit, first) + (across(unit, second) + across(unit, third))


def padded_rows(block):
    width = block.shape[0]
    return jnp.concatenate([block, jnp.zeros((2 * LANES - width, block.shape[1]), block.dtype)], axis=0)


def node_rows(start, count):
    return pl.ds(2 * start, count, 2), pl.ds(2 * start + 1, count, 2)


def pair(row):
    return pl.ds(pl.multiple_of(row, 2), 2)


def pack(low, high, width):
    count = low.shape[0]
    rest = width - LANES
    fold = LANES // rest
    part = count // fold
    return low, jnp.concatenate([high[i * part : (i + 1) * part, :rest] for i in range(fold)], axis=1)


def unpack(packed, count, width):
    rest = width - LANES
    fold = LANES // rest
    low = packed[:count]
    high = jnp.concatenate([packed[count:, i * rest : (i + 1) * rest] for i in range(fold)], axis=0)
    return low, jnp.concatenate([high, jnp.zeros((count, LANES - rest), high.dtype)], axis=1)


def some_rows(count, step, body):
    def one(i, _):
        body(i * step, step)
        return 0

    lax.fori_loop(0, count // step, one, 0)
    if count % step:
        body(count - count % step, count % step)


def gather_face(face, source, target):
    def body(base, size):
        for j in range(size):
            target[pair(2 * (base + j)), :] = source[pair(2 * face[base + j]), :]

    some_rows(face.shape[0], 64, body)


def store_face(face, source, target):
    def body(base, size):
        for j in range(size):
            target[pair(2 * face[base + j]), :] = source[pair(2 * (base + j)), :]

    some_rows(face.shape[0], 64, body)


def add_face(face, source, target):
    def body(base, size):
        places = [pair(2 * face[base + j]) for j in range(size)]
        rows = [target[place, :] for place in places]
        for j in range(size):
            target[places[j], :] = rows[j] + source[pair(2 * (base + j)), :]

    some_rows(face.shape[0], BATCH, body)


def prepare_kernel(width, chunks, face, states, nodes, send, picked, held, sems):
    owned = states.shape[1]
    block = block_of(owned)
    piece = owned // chunks
    copies = []
    for k in range(chunks):
        part = pl.ds(k * piece, piece)
        copies.append(pltpu.make_async_copy(states.at[:, part], held.at[:, part], sems.at[k]))
        copies[-1].start()
    unit = identity(block)
    for k in range(chunks):
        copies[k].wait()

        def one(i, _):
            first = pl.multiple_of(k * piece + i * block, block)
            turned = across(unit, padded_rows(held[:, pl.ds(first, block)]))
            low, high = node_rows(first, block)
            nodes[low, :] = turned[:, :LANES]
            nodes[high, :] = turned[:, LANES:]
            return 0

        lax.fori_loop(0, piece // block, one, 0, unroll=True)
    gather_face(face, nodes, picked)
    count = face.shape[0]
    low, high = pack(picked[pl.ds(0, count, 2), :], picked[pl.ds(1, count, 2), :], width)
    send[:count, :] = low.astype(jnp.bfloat16)
    send[count:, :] = high.astype(jnp.bfloat16)


def gather_own(sizes, table, nodes, matrix, values_out, partial, buffers):
    cells, early, early_rows, late_rows, stride = sizes
    for buffer in buffers:
        buffer[...] = jnp.zeros(buffer.shape, jnp.float32)

    def fetch(cell, buffer):
        mine = table.at[pl.ds(cell * stride, stride)]
        for a in range(early):
            buffer[pl.ds(2 * a, 2), :] = nodes[pair(mine[a]), :]

    def finish(cell, buffer):
        low = buffer[pl.ds(0, early_rows, 2), :]
        high = buffer[pl.ds(1, early_rows, 2), :]
        values = jnp.concatenate([low, high], axis=1).astype(jnp.bfloat16)
        values_out[pl.ds(pl.multiple_of(cell * early_rows, early_rows), early_rows), :] = values
        partial[pl.ds(pl.multiple_of(cell * late_rows, late_rows), late_rows), :] = jnp.dot(
            matrix[early_rows:, :early_rows], values, preferred_element_type=jnp.float32
        )

    def two(i, _):
        fetch(2 * i, buffers[0])
        finish(jnp.maximum(2 * i - 1, 0), buffers[1])
        fetch(2 * i + 1, buffers[1])
        finish(2 * i, buffers[0])
        return 0

    lax.fori_loop(0, cells // 2, two, 0)
    finish(cells - 1, buffers[1])


def own_kernel(sizes, regular, table, nodes, matrix, values_out, partial, *buffers):
    @pl.when(regular[0] == 1)
    def _():
        gather_own(sizes, table, nodes, matrix, values_out, partial, buffers)


def own_again_kernel(sizes, regular, face, table, total, picked, matrix, nodes, values_out, partial, *buffers):
    block = 2 * block_of(nodes.shape[0] // 2)

    def one(i, _):
        at = pl.ds(pl.multiple_of(i * block, block), block)
        nodes[at, :] = (total[at, :] / cheb_half).astype(jnp.bfloat16).astype(jnp.float32)
        return 0

    lax.fori_loop(0, nodes.shape[0] // block, one, 0)
    store_face(face, picked, nodes)

    @pl.when(regular[0] == 1)
    def _():
        gather_own(sizes, table, nodes, matrix, values_out, partial, buffers)


def any_cell(sizes, cell, table, nodes, ghosts, matrix, gathered, products):
    cells, early, early_rows, late_rows, stride = sizes
    owned2 = nodes.shape[0]

    def fetch(a, _):
        place = table[cell * stride + a]
        own = nodes[pair(jnp.minimum(place, owned2 - 2)), :]
        other = ghosts[pair(jnp.maximum(place - owned2, 0)), :]
        row = jnp.where(a < early, a, a - early + early_rows)
        gathered[pair(2 * row), :] = jnp.where(place < owned2, own, other)
        return 0

    def multiply():
        rows = early_rows + late_rows
        values = jnp.concatenate(
            [gathered[pl.ds(0, rows, 2), :], gathered[pl.ds(1, rows, 2), :]], axis=1
        ).astype(jnp.bfloat16)
        result = jnp.dot(matrix[...], values, preferred_element_type=jnp.float32)
        products[pl.ds(0, rows, 2), :] = result[:, :LANES]
        products[pl.ds(1, rows, 2), :] = result[:, LANES:]

    return fetch, multiply


def any_cells(sizes, slots, owned_part, table, nodes, ghosts, matrix, gathered, products, total):
    cells, early, early_rows, late_rows, stride = sizes
    owned2 = nodes.shape[0]
    gathered[...] = jnp.zeros(gathered.shape, jnp.float32)

    def one(cell, _):
        fetch, multiply = any_cell(sizes, cell, table, nodes, ghosts, matrix, gathered, products)
        lax.fori_loop(0, slots, fetch, 0)
        multiply()

        def give(a, _):
            place = table[cell * stride + a]
            row = jnp.where(a < early, a, a - early + early_rows)

            @pl.when((place < owned2) == owned_part)
            def _():
                at = pair(place if owned_part else place - owned2)
                total[at, :] = total[at, :] + products[pair(2 * row), :]

            return 0

        lax.fori_loop(0, slots, give, 0)
        return 0

    lax.fori_loop(0, cells, one, 0)


def shared_kernel(sizes, slots, width, regular, table, late_table, arrived, nodes, matrix, partial,
                  send, values_out, ghosts, total, other, gathered, products, any_gathered, any_products):
    cells, early, early_rows, late_rows, stride = sizes
    late = slots - early
    count = ghosts.shape[0] // 2
    low, high = unpack(arrived[...].astype(jnp.float32), count, width)
    ghosts[pl.ds(0, count, 2), :] = low
    ghosts[pl.ds(1, count, 2), :] = high
    total[...] = jnp.zeros(total.shape, jnp.float32)
    other[...] = jnp.zeros(other.shape, jnp.float32)

    @pl.when(regular[0] == 1)
    def _():
        group = 4

        def fetch(i, _):
            for cell in (2 * i, 2 * i + 1):
                mine = late_table.at[pl.ds(cell * LANES, LANES)]
                here = gathered.at[pl.ds(pl.multiple_of(cell * 2 * late_rows, 2 * late_rows), 2 * late_rows)]
                for a in range(late):
                    here[pl.ds(2 * a, 2), :] = ghosts[pair(mine[a]), :]
                here[pl.ds(2 * late, 2 * (late_rows - late)), :] = jnp.zeros(
                    (2 * (late_rows - late), LANES), jnp.float32
                )
            return 0

        lax.fori_loop(0, cells // 2, fetch, 0)

        def multiply(some, _):
            for j in range(group):
                cell = some * group + j
                base = pl.multiple_of(cell * 2 * late_rows, 2 * late_rows)
                here = gathered.at[pl.ds(base, 2 * late_rows)]
                out = products.at[pl.ds(base, 2 * late_rows)]
                values = jnp.concatenate(
                    [here[pl.ds(0, late_rows, 2), :], here[pl.ds(1, late_rows, 2), :]], axis=1
                ).astype(jnp.bfloat16)
                rows = pl.ds(pl.multiple_of(cell * late_rows, late_rows), late_rows)
                values_out[rows, :] = values
                result = partial[rows, :] + jnp.dot(
                    matrix[early_rows:, early_rows:], values, preferred_element_type=jnp.float32
                )
                out[pl.ds(0, late_rows, 2), :] = result[:, :LANES]
                out[pl.ds(1, late_rows, 2), :] = result[:, LANES:]
            return 0

        lax.fori_loop(0, cells // group, multiply, 0)

        def give(i, _):
            two = (2 * i, 2 * i + 1)
            lists = [late_table.at[pl.ds(cell * LANES, LANES)] for cell in two]
            parts = [
                products.at[pl.ds(pl.multiple_of(cell * 2 * late_rows, 2 * late_rows), 2 * late_rows)] for cell in two
            ]
            scatter_rows(lists, late, parts, (total, other))
            return 0

        lax.fori_loop(0, cells // 2, give, 0)

    @pl.when(regular[0] != 1)
    def _():
        any_cells(sizes, slots, False, table, nodes, ghosts, matrix, any_gathered, any_products, total)

    low, high = (total[pl.ds(k, count, 2), :] + other[pl.ds(k, count, 2), :] for k in range(2))
    low, high = pack(low, high, width)
    send[:count, :] = low
    send[count:, :] = high


def scatter_rows(lists, slots, products, totals):
    def start(k, begin):
        size = min(BATCH, slots - begin)
        places = [pair(lists[k][begin + j]) for j in range(size)]
        held = [totals[k][place, :] for place in places]

        def end():
            for j in range(size):
                totals[k][places[j], :] = held[j] + products[k][pl.ds(2 * (begin + j), 2), :]

        return end

    waiting = []
    for begin in range(0, slots, BATCH):
        for k in range(len(totals)):
            waiting.append(start(k, begin))
            if len(waiting) == len(totals):
                waiting.pop(0)()
    for end in waiting:
        end()


def scatter_own(sizes, table, matrix, own_values, late_values, products, totals):
    cells, early, early_rows, late_rows, stride = sizes

    def multiply(cell, product):
        own = own_values[pl.ds(pl.multiple_of(cell * early_rows, early_rows), early_rows), :]
        late = late_values[pl.ds(pl.multiple_of(cell * late_rows, late_rows), late_rows), :]
        values = jnp.concatenate([own, late], axis=0)
        result = jnp.dot(matrix[:early_rows, :], values, preferred_element_type=jnp.float32)
        product[pl.ds(0, early_rows, 2), :] = result[:, :LANES]
        product[pl.ds(1, early_rows, 2), :] = result[:, LANES:]

    def give(cell, pairs):
        lists = [table.at[pl.ds((cell + k) * stride, stride)] for k in range(2)]
        scatter_rows(lists, early, pairs, totals)

    multiply(0, products[0])
    multiply(1, products[1])

    def four(i, _):
        cell = 4 * i
        multiply(cell + 2, products[2])
        multiply(cell + 3, products[3])
        give(cell, products[:2])
        multiply(jnp.minimum(cell + 4, cells - 1), products[0])
        multiply(jnp.minimum(cell + 5, cells - 1), products[1])
        give(cell + 2, products[2:])
        return 0

    lax.fori_loop(0, cells // 4, four, 0)


def factor_kernel(potential, factor):
    owned = factor.shape[0]
    block = block_of(owned)
    unit = identity(block)

    def one(i, _):
        at = pl.ds(pl.multiple_of(i * block, block), block)
        local = jnp.broadcast_to(potential[:, at], (LANES, block))
        factor[at, :] = across_wide(unit, local) - cheb_center
        return 0

    lax.fori_loop(0, owned // block, one, 0, unroll=3)


def scatter_kernel(sizes, slots, width, again, regular, table, factor, matrix, own_values, late_values,
                   arrived, nodes, *rest):
    if again:
        states, total, other, *rest = rest
    else:
        total, other, *rest = rest
    *products, ghosts, any_gathered, any_products = rest
    owned = factor.shape[0]
    block = block_of(owned)

    def begin(i, _):
        first = pl.multiple_of(i * block, block)
        scale = factor[pl.ds(first, block), :]
        for rows in node_rows(first, block):
            value = scale * nodes[rows, :]
            total[rows, :] = value - (cheb_half / 2.0) * states[rows, :] if again else value
        return 0

    lax.fori_loop(0, owned // block, begin, 0)

    @pl.when(regular[0] == 1)
    def _():
        def clear(i, _):
            other[pl.ds(pl.multiple_of(2 * i * block, 2 * block), 2 * block), :] = jnp.zeros(
                (2 * block, LANES), jnp.float32
            )
            return 0

        lax.fori_loop(0, owned // block, clear, 0)
        scatter_own(sizes, table, matrix, own_values, late_values, products, (total, other))

        def join(i, _):
            at = pl.ds(pl.multiple_of(2 * i * block, 2 * block), 2 * block)
            total[at, :] = total[at, :] + other[at, :]
            return 0

        lax.fori_loop(0, owned // block, join, 0)

    @pl.when(regular[0] != 1)
    def _():
        count = ghosts.shape[0] // 2
        low, high = unpack(arrived[...].astype(jnp.float32), count, width)
        ghosts[pl.ds(0, count, 2), :] = low
        ghosts[pl.ds(1, count, 2), :] = high
        any_cells(sizes, slots, True, table, nodes, ghosts, matrix, any_gathered, any_products, total)


def once_kernel(width, face, total, returned, send, picked):
    count = face.shape[0]
    gather_face(face, total, picked)
    low, high = unpack(returned[...], count, width)
    low = ((picked[pl.ds(0, count, 2), :] + low) / cheb_half).astype(jnp.bfloat16)
    high = ((picked[pl.ds(1, count, 2), :] + high) / cheb_half).astype(jnp.bfloat16)
    picked[pl.ds(0, count, 2), :] = low.astype(jnp.float32)
    picked[pl.ds(1, count, 2), :] = high.astype(jnp.float32)
    low, high = pack(low.astype(jnp.float32), high.astype(jnp.float32), width)
    send[:count, :] = low.astype(jnp.bfloat16)
    send[count:, :] = high.astype(jnp.bfloat16)


def twice_kernel(width, face, total_in, returned, total, filtered, spread):
    owned = filtered.shape[1]
    count = face.shape[0]
    low, high = unpack(returned[...], count, width)
    spread[pl.ds(0, count, 2), :] = low
    spread[pl.ds(1, count, 2), :] = high
    add_face(face, spread, total)
    block = block_of(owned)
    unit = identity(2 * LANES)

    def one(i, _):
        first = pl.multiple_of(i * block, block)
        low, high = node_rows(first, block)
        values = jnp.concatenate([total[low, :], total[high, :]], axis=1) * (2.0 / cheb_half)
        filtered[:, pl.ds(first, block)] = across(unit, values.astype(jnp.bfloat16))[:width].astype(jnp.bfloat16)
        return 0

    lax.fori_loop(0, owned // block, one, 0, unroll=3)


def gram_own_kernel(own, block):
    block[...] = across(own[...], own[...])


def gram_kernel(width, place, gram, own, other, slabs):
    half = width // 2
    rest = (width - LANES) // 2

    def write(cross):
        slabs[0] = cross[:, :LANES]
        slabs[1] = jnp.concatenate([gram[:half, :half], cross[:, LANES : LANES + rest]], axis=1)
        slabs[2] = jnp.concatenate([gram[:half, half:], cross[:, LANES + rest :]], axis=1)
        slabs[3] = jnp.concatenate([gram[half:, half:], jnp.zeros((half, LANES - half), jnp.float32)], axis=1)

    @pl.when(place[0] == 0)
    def _():
        write(across(own[:half, :], other[...]))

    @pl.when(place[0] != 0)
    def _():
        write(across(other[half:, :], own[...]))


def exchanged(axis, stride, radix, give):
    count = lax.axis_size(axis)

    def partner(index, step):
        here = index // stride % radix
        return index + ((here + step) % radix - here) * stride

    return [
        lax.ppermute(give(step), axis, [(i, partner(i, step)) for i in range(count)]) for step in range(1, radix)
    ]


def summed_over(slabs, axis):
    count = lax.axis_size(axis)
    place = lax.axis_index(axis)
    radix = slabs.shape[0]
    radices = [radix]
    left = count // radix
    while left > 1:
        some = 4 if left % 4 == 0 else 2 if left % 2 == 0 else left
        radices.append(some)
        left //= some
    digit = place % radix
    take = lambda step: lax.dynamic_index_in_dim(slabs, (digit + step) % radix, 0, keepdims=False)
    piece = functools.reduce(jnp.add, exchanged(axis, 1, radix, take), take(0))
    stride = radix
    for some in radices[1:]:
        piece = functools.reduce(jnp.add, exchanged(axis, stride, some, lambda step: piece), piece)
        stride *= some
    return [piece] + exchanged(axis, 1, radix, lambda step: piece), digit


def root_kernel(width, where, *refs):
    radix = 4
    mine, theirs = refs[:radix], refs[radix : 2 * radix]
    root, own_slabs, other_slabs = refs[2 * radix :]
    digit = where[0]
    place = where[1]
    for step in range(radix):
        slab = lax.rem(digit + radix - step, radix)
        own_slabs[slab] = mine[step][...]
        other_slabs[slab] = theirs[step][...]
    half = width // 2
    rest = (width - LANES) // 2

    def block_of_states(slabs):
        upper = slabs[2][:, :half]
        top = jnp.concatenate([slabs[1][:, :half], upper], axis=1)
        return jnp.concatenate([top, jnp.concatenate([upper.T, slabs[3][:, :half]], axis=1)], axis=0)

    def cross_rows(slabs):
        return jnp.concatenate([slabs[0], slabs[1][:, half : half + rest], slabs[2][:, half : half + rest]], axis=1)

    first = place == 0
    own_cross, other_cross = cross_rows(own_slabs), cross_rows(other_slabs)
    cross = jnp.concatenate(
        [jnp.where(first, own_cross, other_cross), jnp.where(first, other_cross, own_cross)], axis=0
    )
    turned = cross.T
    above, below = jnp.where(first, cross, turned), jnp.where(first, turned, cross)
    margin = jnp.concatenate(
        [
            jnp.concatenate([block_of_states(own_slabs), above], axis=1),
            jnp.concatenate([below, block_of_states(other_slabs)], axis=1),
        ],
        axis=0,
    )
    total = 2 * width
    rows = lax.broadcasted_iota(jnp.int32, (total, total), 0)
    columns = lax.broadcasted_iota(jnp.int32, (total, total), 1)
    triple = jnp.where(rows == columns, 3.0, 0.0)
    product = functools.partial(jnp.dot, precision=lax.Precision.HIGHEST, preferred_element_type=jnp.float32)
    current = margin / jnp.sqrt(jnp.sum(margin * margin) + epsilon)
    factor = triple - current
    current = 0.5 * product(factor, current)
    inverse = 0.5 * factor
    for iteration in range(1, NS_STEPS - 1):
        factor = triple - product(inverse, current)
        current = 0.5 * product(factor, current)
        inverse = 0.5 * product(factor, inverse)
    factor = triple[:width] - product(inverse[:width], current)
    root[...] = (0.5 * product(factor, inverse)).astype(jnp.bfloat16)


def rotate_kernel(width, root, own, other, result):
    result[...] = jnp.dot(root[:, :width], own[...], preferred_element_type=jnp.float32) + jnp.dot(
        root[:, width:], other[...], preferred_element_type=jnp.float32
    )


def local(states, kinetic, potential, cell_nodes, face_map):
    width, owned = states.shape
    cells, slots = cell_nodes.shape
    count = face_map.shape[0]
    side = round(slots ** (1 / 3))
    late = side * side
    early = slots - late
    early_rows = rounded_up(early, 16)
    late_rows = rounded_up(late, 16)
    rows = early_rows + late_rows
    stride = rounded_up(slots, LANES)
    sizes = (cells, early, early_rows, late_rows, stride)
    packed = count + count // (LANES // (width - LANES))

    regular = jnp.all(cell_nodes[:, :early] < owned) & jnp.all(cell_nodes[:, early:] >= owned)
    regular = (regular & (cells % 4 == 0)).astype(jnp.int32).reshape(1)
    table = jnp.pad(2 * cell_nodes, ((0, 0), (0, stride - slots))).reshape(-1)
    late_table = jnp.pad(2 * (cell_nodes[:, early:] - owned), ((0, 0), (0, LANES - late))).reshape(-1)

    def spaced(array, axis):
        head, tail = jnp.split(array, [early], axis)
        fill = lambda part, size: jnp.pad(
            part, [(0, size - part.shape[k]) if k == axis else (0, 0) for k in range(2)]
        )
        return jnp.concatenate([fill(head, early_rows), fill(tail, late_rows)], axis)

    matrix = spaced(spaced(kinetic, 0), 1)
    lumped = potential[None, :]
    wide = jax.ShapeDtypeStruct((2 * owned, LANES), jnp.float32)
    sent = jax.ShapeDtypeStruct((packed, LANES), jnp.bfloat16)
    sent_wide = jax.ShapeDtypeStruct((packed, LANES), jnp.float32)
    face_rows = jax.ShapeDtypeStruct((2 * count, LANES), jnp.float32)
    own_values = jax.ShapeDtypeStruct((cells * early_rows, 2 * LANES), jnp.bfloat16)
    late_values = jax.ShapeDtypeStruct((cells * late_rows, 2 * LANES), jnp.bfloat16)
    partial = jax.ShapeDtypeStruct((cells * late_rows, 2 * LANES), jnp.float32)
    spread = pltpu.VMEM((2 * count, LANES), jnp.float32)
    pairs_own = pltpu.VMEM((2 * early_rows, LANES), jnp.float32)
    pairs_late = pltpu.VMEM((cells * 2 * late_rows, LANES), jnp.float32)
    pairs_any = pltpu.VMEM((2 * rows, LANES), jnp.float32)

    chunks = 9 if owned % (9 * block_of(owned)) == 0 else 1
    begun, send = called(
        functools.partial(prepare_kernel, width, chunks),
        (wide, sent),
        [SMEM, ANY],
        [spread, pltpu.VMEM((width, owned), jnp.bfloat16), pltpu.SemaphoreType.DMA((chunks,))],
        6,
        20,
    )(face_map, states)

    def shared(arrived, nodes, partial):
        return called(
            functools.partial(shared_kernel, sizes, slots, width),
            (sent_wide, late_values),
            [SMEM, SMEM, SMEM, VMEM, VMEM, VMEM, VMEM],
            [spread, spread, spread, pairs_late, pairs_late, pairs_any, pairs_any],
            6,
            24,
        )(regular, table, late_table, arrived, nodes, matrix, partial)

    (factor,) = called(
        factor_kernel, (jax.ShapeDtypeStruct((owned, LANES), jnp.float32),), [VMEM], [], 3, 8
    )(lumped)

    def scattered(again, values, late, arrived, nodes, *before):
        return called(
            functools.partial(scatter_kernel, sizes, slots, width, again),
            (wide,),
            [SMEM, SMEM] + [VMEM] * (6 + len(before)),
            [pltpu.VMEM((2 * owned, LANES), jnp.float32)] + [pairs_own] * 4 + [spread, pairs_any, pairs_any],
            18,
            20,
        )(regular, table, factor, matrix, values, late, arrived, nodes, *before)[0]

    arrived = passed_along(send, "brick", -1)
    values, part = called(
        functools.partial(own_kernel, sizes),
        (own_values, partial),
        [SMEM, SMEM, VMEM, VMEM],
        [pairs_own, pairs_own],
        10,
        16,
    )(regular, table, begun, matrix)
    back, late_in = shared(arrived, begun, part)
    returned = passed_along(back, "brick", 1)
    total = scattered(False, values, late_in, arrived, begun)
    send, picked = called(
        functools.partial(once_kernel, width),
        (sent, face_rows),
        [SMEM, VMEM, VMEM],
        [],
        3,
        16,
    )(face_map, total, returned)
    arrived = passed_along(send, "brick", -1)
    nodes, values, part = called(
        functools.partial(own_again_kernel, sizes),
        (wide, own_values, partial),
        [SMEM, SMEM, SMEM, VMEM, VMEM, VMEM],
        [pairs_own, pairs_own],
        12,
        20,
    )(regular, face_map, table, total, picked, matrix)
    back, late_in = shared(arrived, nodes, part)
    returned = passed_along(back, "brick", 1)
    total = scattered(True, values, late_in, arrived, nodes, begun)
    _, filtered = called(
        functools.partial(twice_kernel, width),
        (wide, jax.ShapeDtypeStruct((width, owned), jnp.bfloat16)),
        [SMEM, VMEM, VMEM],
        [spread],
        5,
        24,
        input_output_aliases={1: 0},
    )(face_map, total, returned)

    place = lax.axis_index("state")
    other = passed_along(filtered, "state", 1)
    (gram,) = called(
        gram_own_kernel, (jax.ShapeDtypeStruct((width, width), jnp.float32),), [VMEM], [], 1, 16
    )(filtered)
    (slabs,) = called(
        functools.partial(gram_kernel, width),
        (jax.ShapeDtypeStruct((4, width // 2, LANES), jnp.float32),),
        [SMEM, VMEM, VMEM, VMEM],
        [],
        1,
        20,
    )(place.astype(jnp.int32).reshape(1), gram, filtered, other)
    mine, digit = summed_over(slabs, "brick")
    theirs = [passed_along(piece, "state", 1) for piece in mine]
    slabs_held = pltpu.VMEM((4, width // 2, LANES), jnp.float32)
    (root,) = called(
        functools.partial(root_kernel, width),
        (jax.ShapeDtypeStruct((width, 2 * width), jnp.bfloat16),),
        [SMEM] + [VMEM] * 8,
        [slabs_held, slabs_held],
        6,
        20,
    )(jnp.stack([digit, place]).astype(jnp.int32), *mine, *theirs)
    block = owned // chunks
    columns = pl.BlockSpec((width, block), lambda i: (0, i))
    return called(
        functools.partial(rotate_kernel, width),
        jax.ShapeDtypeStruct((width, owned), jnp.float32),
        [pl.BlockSpec((width, 2 * width), lambda i: (0, 0)), columns, columns],
        [],
        3,
        16,
        out_specs=columns,
        grid=(chunks,),
    )(root, filtered, other)


def solution(mesh):
    in_specs = (P("state", "brick"), P(), P("brick"), P("brick", None), P("brick"))
    out_specs = P("state", "brick")
    return jax.shard_map(local, mesh=mesh, in_specs=in_specs, out_specs=out_specs, check_vma=False)
```

time: 605 us -> 173 us (0.29); the launches traced: 593 us -> 173 us
  other arithmetic: 189 us -> 1.84 us
  local copies, waits for them, and re-layouts: 169 us -> 16.7 us
  waiting for transfers between devices: 171 us -> 24.2 us
  Pallas kernels: 0 us -> 107 us
  matrix products: 37.4 us -> 0 us
  between operations: 14.8 us -> 1.71 us
  starting transfers between devices: 9.32 us -> 21.6 us
    scatter-add x4 -> x0, other arithmetic: 148 us -> none  [the longest x2 119 us: apply_operator(): summed = jnp.zeros((width, owned + face_count), jnp.float32).at[:, cell_n...]
    gather x10 -> x0, local copies, waits for them, and re-layouts: 109 us -> none  [the longest x6 97.3 us: apply_operator(): gathered = extended[:, cell_nodes]]
    psum x1 -> x0, waiting for transfers between devices: 109 us -> none  [local(): margin_rows = lax.psum(partial_rows, 'brick')]
    pallas_call x0 -> x14, Pallas kernels: none -> 107 us  [the longest x2 31.5 us: scattered(): called(functools.partial(scatter_kernel, sizes, slots, width, again), (wi...]
    reshape x5 -> x2, local copies, waits for them, and re-layouts: 43.5 us -> 0.01 us  [the longest x1 0.01 us: local(): table = jnp.pad(2 * cell_nodes, ((0, 0), (0, stride - slots))).reshape(-1)]
    dot_general x12 -> x0, matrix products: 37.4 us -> none  [the longest x2 17.9 us: apply_operator(): jnp.einsum('wca,ea->wce', gathered, kinetic, preferred_element_type=jnp.f...]
    ppermute x4 -> x9, waiting for transfers between devices: 50.3 us -> 14.1 us  [passed_along(): return lax.ppermute(value, axis, pairs)]
    convert_element_type x2 -> x0, other arithmetic: 15.4 us -> none  [the longest x1 8.41 us: local(): filtered = (2.0 * (second - cheb_center * filtered_once.astype(jnp.float3...]
  transfers between devices with their start and end apart: 6 -> 18, of which waited for: 6 -> 12; matrix products, arithmetic and copies ran while one was open for 3% -> 1% of each run, Pallas kernels for 0% -> 36%
where the time goes in v2:
time: 173 us
  Pallas kernels  107 us (62%)
  waiting for transfers between devices  24.2 us (14%)
  starting transfers between devices  21.6 us (12%)
  local copies, waits for them, and re-layouts  16.7 us (10%)
  other arithmetic  1.84 us (1%)
    pallas_call x2, Pallas kernels, scattered(): called(functools.partial(scatter_kernel, sizes, slots, width, again), (wi...  31.5 us
    unnamed x32, local copies, waits for them, and re-layouts  16.6 us
    ppermute x9, waiting for transfers between devices, passed_along(): return lax.ppermute(value, axis, pairs)  14.1 us
    pallas_call x1, Pallas kernels, local(): called(functools.partial(own_again_kernel, sizes), (wide, own_values, par...  13.5 us
    pallas_call x2, Pallas kernels, shared(): called(functools.partial(shared_kernel, sizes, slots, width), (sent_wide,...  13 us
    ppermute x9, starting transfers between devices, passed_along(): return lax.ppermute(value, axis, pairs)  12 us
    pallas_call x1, Pallas kernels, local(): called(functools.partial(own_kernel, sizes), (own_values, partial), [SMEM...  11.4 us
    ppermute x9, waiting for transfers between devices, exchanged(): lax.ppermute(give(step), axis, [(i, partner(i, step)) for i in range(coun...  10.2 us
  transfers between devices with their start and end apart: 18, of which 12 were waited for; matrix products, arithmetic and copies ran while one was open for 1% of the time, Pallas kernels for 36%

profile of v2, /device:TPU:0, one launch (start us, length us, event | category | flops | bytes accessed | tf_op | source)
XLA Modules:
  0.0 173.0 jit_solution(15717442375294339724)
XLA Ops:
  0.0 0.7 copy-done.7
  0.7 1.7 %copy-done.9 = bf16[192,6912]{1,0:T(8,128)(2,1)S(1)} copy-done((bf16[192,6912]{1,0:T(8,128)(2,1)S(1)}, bf16[192,6912]{1,0:T(8,128)(2,1)}, u32[]{:S(2)}) %copy-start.9) | copy-done | bytes 2654232
  2.5 5.1 %shard_map.56 = (f32[13824,128]{1,0:T(8,128)S(1)}, bf16[1728,128]{1,0:T(8,128)(2,1)S(1)}) custom-call(s32[1152]{0:T(1024)S(1)} %copy-done.7, bf16[192,6912]{1,0:T(8,128)(2,1)S(1)} %copy-done.9), custom_call_target="tpu_custom_call" | custom-call | flops 2400000000 | bytes 18000000 | tf_op jit(solution)/shard_map/pallas_call | solution.py:639
  7.6 2.9 %copy-done = f32[13824,128]{1,0:T(8,128)} copy-done((f32[13824,128]{1,0:T(8,128)}, f32[13824,128]{1,0:T(8,128)S(1)}, u32[]{:S(2)}) %copy-start) | copy-done | bytes 7077912
  10.5 6.9 %collective-permute-start = (bf16[1728,128]{1,0:T(8,128)(2,1)S(1)}, bf16[1728,128]{1,0:T(8,128)(2,1)S(1)}, u32[]{:S(2)}, u32[]{:S(2)}) collective-permute-start(bf16[1728,128]{1,0:T(8,128)(2,1)S(1)} %get-tuple-element.21), channel_id=1, source_target_pairs={{0,30},{2,0},{4,2},{6,4},{8,6},{10,8},{12,10},{14,12},{16,14},{18,... | collective-permute-start | bytes 1327112 | tf_op jit(solution)/shard_map/ppermute | solution.py:40
  17.4 0.1 slice_select_fusion.1
  17.6 0.1 split.10
  17.8 0.7 compare_reduce_fusion
  18.5 0.6 fusion.6
  19.1 0.1 add_multiply_fusion
  20.5 0.1 fusion.2.matrix
  20.6 3.0 %copy-done.1 = f32[13824,128]{1,0:T(8,128)S(1)} copy-done((f32[13824,128]{1,0:T(8,128)S(1)}, f32[13824,128]{1,0:T(8,128)}, u32[]{:S(2)}) %copy-start.1) | copy-done | bytes 7077912
  23.7 11.4 %shard_map.57 = (bf16[9728,256]{1,0:T(8,128)(2,1)S(1)}, f32[2048,256]{1,0:T(8,128)S(1)}) custom-call(s32[1]{0:T(128)} %bitcast.2.regular, s32[12288]{0:T(1024)S(1)} %reshape.14.table, f32[13824,128]{1,0:T(8,128)S(1)} %copy-done.1, bf16[368,368]{1,0:T(8,128)(2,1)S(1)} %fusion.2.matrix), custom_call_target="tpu_custom_call" | custom-call | flops 4000000000 | bytes 30000000 | tf_op jit(solution)/shard_map/pallas_call | solution.py:673
  35.1 0.0 copy-start.10
  35.1 2.3 %copy-done.10 = bf16[9728,256]{1,0:T(8,128)(2,1)} copy-done((bf16[9728,256]{1,0:T(8,128)(2,1)}, bf16[9728,256]{1,0:T(8,128)(2,1)S(1)}, u32[]{:S(2)}) %copy-start.10) | copy-done | bytes 4980760
  37.3 0.0 collective-permute-done.arrived
  37.3 6.5 %shard_map.58 = (f32[1728,128]{1,0:T(8,128)S(1)}, bf16[2048,256]{1,0:T(8,128)(2,1)S(1)}) custom-call(s32[1]{0:T(128)} %bitcast.2.regular, s32[12288]{0:T(1024)S(1)} %reshape.14.table, s32[4096]{0:T(1024)S(1)} %pad_bitcast_fusion.late_table, bf16[1728,128]{1,0:T(8,128)(2,1)S(1)} %collective-permute-done.arrived, f32[13824,128]{1,0:T(8,128)S(1)} %copy-done.2, ...), custom_call_target="tpu_custom_call" | custom-call | flops 2400000000 | bytes 18000000 | tf_op jit(solution)/shard_map/pallas_call | solution.py:649
  43.9 0.1 collective-permute-start.1
  44.0 4.4 %shard_map.55.factor = f32[6912,128]{1,0:T(8,128)S(1)} custom-call(f32[1,6912]{1,0:T(1,128)S(1)} %broadcast_in_dim.3.potential), custom_call_target="tpu_custom_call" | custom-call | flops 1200000000 | bytes 9000000 | tf_op jit(solution)/shard_map/pallas_call | solution.py:658
  48.4 0.0 copy-start.11
  48.4 3.7 %copy-done.11 = bf16[9728,256]{1,0:T(8,128)(2,1)S(1)} copy-done((bf16[9728,256]{1,0:T(8,128)(2,1)S(1)}, bf16[9728,256]{1,0:T(8,128)(2,1)}, u32[]{:S(2)}) %copy-start.11) | copy-done | bytes 4980760
  52.1 15.3 %shard_map.59.total = f32[13824,128]{1,0:T(8,128)S(1)} custom-call(s32[1]{0:T(128)} %bitcast.2.regular, s32[12288]{0:T(1024)S(1)} %reshape.14.table, f32[6912,128]{1,0:T(8,128)S(1)} %shard_map.55.factor, bf16[368,368]{1,0:T(8,128)(2,1)S(1)} %fusion.2.matrix, bf16[9728,256]{1,0:T(8,128)(2,1)S(1)} %copy-done.11, ...), custom_call_target="tpu_custom_call" | custom-call | flops 7200000000 | bytes 54000000 | tf_op jit(solution)/shard_map/pallas_call | solution.py:663
  67.4 1.2 collective-permute-done.1.returned
  68.6 2.2 %shard_map.60 = (bf16[1728,128]{1,0:T(8,128)(2,1)S(1)}, f32[2304,128]{1,0:T(8,128)S(1)}) custom-call(s32[1152]{0:T(1024)S(1)} %copy-done.8, f32[13824,128]{1,0:T(8,128)S(1)} %shard_map.59.total, f32[1728,128]{1,0:T(8,128)S(1)} %collective-permute-done.1.returned), custom_call_target="tpu_custom_call" | custom-call | flops 1200000000 | bytes 9000000 | tf_op jit(solution)/shard_map/pallas_call | solution.py:684
  70.8 4.4 %collective-permute-start.2 = (bf16[1728,128]{1,0:T(8,128)(2,1)S(1)}, bf16[1728,128]{1,0:T(8,128)(2,1)S(1)}, u32[]{:S(2)}, u32[]{:S(2)}) collective-permute-start(bf16[1728,128]{1,0:T(8,128)(2,1)S(1)} %get-tuple-element.27), channel_id=1, source_target_pairs={{0,30},{2,0},{4,2},{6,4},{8,6},{10,8},{12,10},{14,12},{16,14},{18,... | collective-permute-start | bytes 1327112 | tf_op jit(solution)/shard_map/ppermute | solution.py:40
  75.3 13.5 %shard_map.61 = (f32[13824,128]{1,0:T(8,128)S(1)}, bf16[9728,256]{1,0:T(8,128)(2,1)S(1)}, f32[2048,256]{1,0:T(8,128)S(1)}) custom-call(s32[1]{0:T(128)} %bitcast.2.regular, s32[1152]{0:T(1024)S(1)} %copy-done.8, s32[12288]{0:T(1024)S(1)} %reshape.14.table, f32[13824,128]{1,0:T(8,128)S(1)} %shard_map.59.total, f32[2304,128]{1,0:T(8,128)S(1)} %get-tuple-element.25.picked, ...), custom_call_target="tpu_custom_call" | custom-call | flops 4800000000 | bytes 36000000 | tf_op jit(solution)/shard_map/pallas_call | solution.py:693
  88.8 0.0 copy-start.3
  88.8 2.3 %copy-done.3 = bf16[9728,256]{1,0:T(8,128)(2,1)} copy-done((bf16[9728,256]{1,0:T(8,128)(2,1)}, bf16[9728,256]{1,0:T(8,128)(2,1)S(1)}, u32[]{:S(2)}) %copy-start.3) | copy-done | bytes 4980760
  91.0 0.0 collective-permute-done.2.arrived
  91.1 6.5 %shard_map.62 = (f32[1728,128]{1,0:T(8,128)S(1)}, bf16[2048,256]{1,0:T(8,128)(2,1)S(1)}) custom-call(s32[1]{0:T(128)} %bitcast.2.regular, s32[12288]{0:T(1024)S(1)} %reshape.14.table, s32[4096]{0:T(1024)S(1)} %pad_bitcast_fusion.late_table, bf16[1728,128]{1,0:T(8,128)(2,1)S(1)} %collective-permute-done.2.arrived, f32[13824,128]{1,0:T(8,128)S(1)} %get-tuple-element.28.nodes, ...), custom_call_target="tpu_custom_call" | custom-call | flops 2400000000 | bytes 18000000 | tf_op jit(solution)/shard_map/pallas_call | solution.py:649
  97.6 0.1 collective-permute-start.3
  97.7 16.2 %shard_map.63.total_in = f32[13824,128]{1,0:T(8,128)S(1)} custom-call(s32[1]{0:T(128)} %bitcast.2.regular, s32[12288]{0:T(1024)S(1)} %reshape.14.table, f32[6912,128]{1,0:T(8,128)S(1)} %copy-done.6, bf16[368,368]{1,0:T(8,128)(2,1)S(1)} %fusion.2.matrix, bf16[9728,256]{1,0:T(8,128)(2,1)S(1)} %copy-done.4, ...), custom_call_target="tpu_custom_call" | custom-call | flops 7200000000 | bytes 54000000 | tf_op jit(solution)/shard_map/pallas_call | solution.py:663
  113.9 7.9 %collective-permute-done.3.returned = f32[1728,128]{1,0:T(8,128)S(1)} collective-permute-done((f32[1728,128]{1,0:T(8,128)S(1)}, f32[1728,128]{1,0:T(8,128)S(1)}, u32[]{:S(2)}, u32[]{:S(2)}) %collective-permute-start.3) | collective-permute-done | bytes 884768 | tf_op jit(solution)/shard_map/ppermute | solution.py:40
  121.8 5.9 %shard_map.64 = (f32[13824,128]{1,0:T(8,128)S(1)}, bf16[192,6912]{1,0:T(8,128)(2,1)S(1)}) custom-call(s32[1152]{0:T(1024)S(1)} %copy-done.8, f32[13824,128]{1,0:T(8,128)S(1)} %shard_map.63.total_in, f32[1728,128]{1,0:T(8,128)S(1)} %collective-permute-done.3.returned), custom_call_target="tpu_custom_call", output_to_operand_aliasing={{0}: (1, {})} | custom-call | flops 2000000000 | bytes 15000000 | tf_op jit(solution)/shard_map/pallas_call | solution.py:704
  127.7 0.1 collective-permute-start.4
  127.9 0.9 shard_map.65.gram
  128.7 4.1 %collective-permute-done.4.other = bf16[192,6912]{1,0:T(8,128)(2,1)} collective-permute-done((bf16[192,6912]{1,0:T(8,128)(2,1)S(1)}, bf16[192,6912]{1,0:T(8,128)(2,1)}, u32[]{:S(2)}, u32[]{:S(2)}) %collective-permute-start.4) | collective-permute-done | bytes 2654240 | tf_op jit(solution)/shard_map/ppermute | solution.py:40
  132.9 2.8 %shard_map.66 = f32[4,96,128]{2,1,0:T(8,128)S(1)} custom-call(s32[1]{0:T(128)} %bitcast.1.place, f32[192,192]{1,0:T(8,128)S(1)} %shard_map.65.gram, bf16[192,6912]{1,0:T(8,128)(2,1)S(1)} %get-tuple-element.32.own, bf16[192,6912]{1,0:T(8,128)(2,1)} %collective-permute-done.4.other), custom_call_target="tpu_custom_call" | custom-call | flops 400000000 | bytes 3000000 | tf_op jit(solution)/shard_map/pallas_call | solution.py:719
  135.7 0.1 collective-permute-start.5
  135.8 0.1 collective-permute-start.6
  135.9 2.8 %collective-permute-start.7 = (f32[96,128]{1,0:T(8,128)S(1)}, f32[96,128]{1,0:T(8,128)S(1)}, u32[]{:S(2)}, u32[]{:S(2)}) collective-permute-start(f32[96,128]{1,0:T(8,128)S(1)} %get-tuple-element.34), channel_id=1, source_target_pairs={{0,6},{2,0},{4,2},{6,4},{8,14},{10,8},{12,10},{14,12},{16,22},{18,... | collective-permute-start | bytes 147464 | tf_op jit(solution)/shard_map/ppermute | solution.py:516
  138.7 2.3 %collective-permute-done.5 = f32[96,128]{1,0:T(8,128)S(1)} collective-permute-done((f32[96,128]{1,0:T(8,128)S(1)}, f32[96,128]{1,0:T(8,128)S(1)}, u32[]{:S(2)}, u32[]{:S(2)}) %collective-permute-start.5) | collective-permute-done | bytes 49184 | tf_op jit(solution)/shard_map/ppermute | solution.py:516
  141.0 0.0 collective-permute-done.6
  141.0 0.4 collective-permute-done.7
  141.3 0.1 collective-permute-start.10
  141.4 2.0 %collective-permute-start.8 = (f32[96,128]{1,0:T(8,128)S(1)}, f32[96,128]{1,0:T(8,128)S(1)}, u32[]{:S(2)}, u32[]{:S(2)}) collective-permute-start(f32[96,128]{1,0:T(8,128)S(1)} %fusion.5), channel_id=1, source_target_pairs={{0,8},{2,10},{4,12},{6,14},{8,16},{10,18},{12,20},{14,22},{16,24},... | collective-permute-start | bytes 147464 | tf_op jit(solution)/shard_map/ppermute | solution.py:516
  143.4 2.5 %collective-permute-done.10 = f32[96,128]{1,0:T(8,128)S(1)} collective-permute-done((f32[96,128]{1,0:T(8,128)S(1)}, f32[96,128]{1,0:T(8,128)S(1)}, u32[]{:S(2)}, u32[]{:S(2)}) %collective-permute-start.10) | collective-permute-done | bytes 49184 | tf_op jit(solution)/shard_map/ppermute | solution.py:516
  146.0 1.4 collective-permute-done.8
  147.3 1.1 collective-permute-done.9
  148.4 3.0 %collective-permute-start.11 = (f32[96,128]{1,0:T(8,128)S(1)}, f32[96,128]{1,0:T(8,128)S(1)}, u32[]{:S(2)}, u32[]{:S(2)}) collective-permute-start(f32[96,128]{1,0:T(8,128)S(1)} %add_add_fusion.refs_0_), channel_id=1, source_target_pairs={{0,2},{2,4},{4,6},{6,0},{8,10},{10,12},{12,14},{14,8},{16,18},{18,... | collective-permute-start | bytes 147464 | tf_op jit(solution)/shard_map/ppermute | solution.py:516
  151.4 0.0 collective-permute-start.12
  151.4 1.5 collective-permute-start.13
  152.9 0.0 collective-permute-start.14
  152.9 0.5 collective-permute-done.11.refs_1_
  153.5 0.0 collective-permute-start.15
  153.5 2.0 %collective-permute-done.12.refs_2_ = f32[96,128]{1,0:T(8,128)S(1)} collective-permute-done((f32[96,128]{1,0:T(8,128)S(1)}, f32[96,128]{1,0:T(8,128)S(1)}, u32[]{:S(2)}, u32[]{:S(2)}) %collective-permute-start.12) | collective-permute-done | bytes 49184 | tf_op jit(solution)/shard_map/ppermute | solution.py:516
  155.5 0.0 collective-permute-start.16
  155.5 0.0 collective-permute-done.13.refs_3_
  155.5 0.5 collective-permute-start.17
  156.0 0.1 pad_add_fusion.where
  156.1 0.6 collective-permute-done.16.refs_6_
  156.7 0.2 collective-permute-done.17.refs_7_
  156.9 7.7 %shard_map.67.root = bf16[192,384]{1,0:T(8,128)(2,1)S(1)} custom-call(s32[2]{0:T(128)S(1)} %pad_add_fusion.where, f32[96,128]{1,0:T(8,128)S(1)} %add_add_fusion.refs_0_, f32[96,128]{1,0:T(8,128)S(1)} %collective-permute-done.11.refs_1_, f32[96,128]{1,0:T(8,128)S(1)} %collective-permute-done.12.refs_2_, f32[96,128]{1,0:T(8,128)S(1)} %collective-permute-done.13.refs_3_, ...), custom_call_target="tpu_custom_call" | custom-call | flops 2400000000 | bytes 18000000 | tf_op jit(solution)/shard_map/pallas_call | solution.py:730
  164.6 8.4 %shard_map.68 = f32[192,6912]{1,0:T(8,128)} custom-call(bf16[192,384]{1,0:T(8,128)(2,1)S(1)} %shard_map.67.root, bf16[192,6912]{1,0:T(8,128)(2,1)S(1)} %get-tuple-element.32.own, bf16[192,6912]{1,0:T(8,128)(2,1)} %collective-permute-done.4.other), custom_call_target="tpu_custom_call" | custom-call | flops 1200000000 | bytes 9000000 | tf_op jit(solution)/shard_map/pallas_call | solution.py:740
  (36 shorter events, 0.2 us)
Async XLA Ops:
  0.0 17.4 %copy-start.15 = (pred[304]{0:T(512)(128)(4,1)S(1)}, pred[304]{0:T(512)(128)(4,1)}, u32[]{:S(2)}) copy-start(pred[304]{0:T(512)(128)(4,1)} %constant.63.clone.1) | copy-start | bytes 916
  0.0 0.7 copy-start.7
  0.7 1.7 %copy-start.9 = (bf16[192,6912]{1,0:T(8,128)(2,1)S(1)}, bf16[192,6912]{1,0:T(8,128)(2,1)}, u32[]{:S(2)}) copy-start(bf16[192,6912]{1,0:T(8,128)(2,1)} %states.1) | copy-start | bytes 7962628
  2.5 14.9 %copy-start.13 = (bf16[343,343]{1,0:T(8,128)(2,1)S(1)}, bf16[343,343]{1,0:T(8,128)(2,1)}, u32[]{:S(2)}) copy-start(bf16[343,343]{1,0:T(8,128)(2,1)} %param.6) | copy-start | bytes 705898
  2.5 15.3 %copy-start.12 = (s32[32,343]{1,0:T(8,128)S(1)}, s32[32,343]{1,0:T(8,128)}, u32[]{:S(2)}) copy-start(s32[32,343]{1,0:T(8,128)} %param.8) | copy-start | bytes 131716
  7.6 2.9 %copy-start = (f32[13824,128]{1,0:T(8,128)}, f32[13824,128]{1,0:T(8,128)S(1)}, u32[]{:S(2)}) copy-start(f32[13824,128]{1,0:T(8,128)S(1)} %get-tuple-element.19.nodes.rest_0_) | copy-start | bytes 21233668
  10.5 26.9 %collective-permute-start = (bf16[1728,128]{1,0:T(8,128)(2,1)S(1)}, bf16[1728,128]{1,0:T(8,128)(2,1)S(1)}, u32[]{:S(2)}, u32[]{:S(2)}) collective-permute-start(bf16[1728,128]{1,0:T(8,128)(2,1)S(1)} %get-tuple-element.21), channel_id=1, source_target_pairs={{0,30},{2,0},{4,2},{6,4},{8,6},{10,8},{12,10},{14,12},{16,14},{18,... | collective-permute-start | bytes 1327112 | tf_op jit(solution)/shard_map/ppermute | solution.py:40
  20.6 3.0 %copy-start.1 = (f32[13824,128]{1,0:T(8,128)S(1)}, f32[13824,128]{1,0:T(8,128)}, u32[]{:S(2)}) copy-start(f32[13824,128]{1,0:T(8,128)} %copy-done) | copy-start | bytes 21233668
  23.6 13.7 %copy-start.2 = (f32[13824,128]{1,0:T(8,128)S(1)}, f32[13824,128]{1,0:T(8,128)}, u32[]{:S(2)}) copy-start(f32[13824,128]{1,0:T(8,128)} %copy-done) | copy-start | bytes 21233668
  35.1 2.3 %copy-start.10 = (bf16[9728,256]{1,0:T(8,128)(2,1)}, bf16[9728,256]{1,0:T(8,128)(2,1)S(1)}, u32[]{:S(2)}) copy-start(bf16[9728,256]{1,0:T(8,128)(2,1)S(1)} %get-tuple-element.20.own_values) | copy-start | bytes 14942212
  37.3 6.6 %copy-start.14 = (f32[6912]{0:T(1024)S(1)}, f32[6912]{0:T(1024)}, u32[]{:S(2)}) copy-start(f32[6912]{0:T(1024)} %param.7) | copy-start | bytes 82948
  43.9 24.8 %collective-permute-start.1 = (f32[1728,128]{1,0:T(8,128)S(1)}, f32[1728,128]{1,0:T(8,128)S(1)}, u32[]{:S(2)}, u32[]{:S(2)}) collective-permute-start(f32[1728,128]{1,0:T(8,128)S(1)} %get-tuple-element.24), channel_id=1, source_target_pairs={{0,2},{2,4},{4,6},{6,8},{8,10},{10,12},{12,14},{14,16},{16,18},{18... | collective-permute-start | bytes 2654216 | tf_op jit(solution)/shard_map/ppermute | solution.py:40
  48.4 19.0 %copy-start.5 = (f32[6912,128]{1,0:T(8,128)}, f32[6912,128]{1,0:T(8,128)S(1)}, u32[]{:S(2)}) copy-start(f32[6912,128]{1,0:T(8,128)S(1)} %shard_map.55.factor) | copy-start | bytes 10616836
  48.4 3.7 %copy-start.11 = (bf16[9728,256]{1,0:T(8,128)(2,1)S(1)}, bf16[9728,256]{1,0:T(8,128)(2,1)}, u32[]{:S(2)}) copy-start(bf16[9728,256]{1,0:T(8,128)(2,1)} %copy-done.10) | copy-start | bytes 14942212
  52.1 16.5 %copy-start.8 = (s32[1152]{0:T(1024)S(1)}, s32[1152]{0:T(1024)}, u32[]{:S(2)}) copy-start(s32[1152]{0:T(1024)} %face.7) | copy-start | bytes 13828
  70.8 20.2 %collective-permute-start.2 = (bf16[1728,128]{1,0:T(8,128)(2,1)S(1)}, bf16[1728,128]{1,0:T(8,128)(2,1)S(1)}, u32[]{:S(2)}, u32[]{:S(2)}) collective-permute-start(bf16[1728,128]{1,0:T(8,128)(2,1)S(1)} %get-tuple-element.27), channel_id=1, source_target_pairs={{0,30},{2,0},{4,2},{6,4},{8,6},{10,8},{12,10},{14,12},{16,14},{18,... | collective-permute-start | bytes 1327112 | tf_op jit(solution)/shard_map/ppermute | solution.py:40
  88.8 2.3 %copy-start.3 = (bf16[9728,256]{1,0:T(8,128)(2,1)}, bf16[9728,256]{1,0:T(8,128)(2,1)S(1)}, u32[]{:S(2)}) copy-start(bf16[9728,256]{1,0:T(8,128)(2,1)S(1)} %get-tuple-element.26.own_values) | copy-start | bytes 14942212
  91.1 6.6 %copy-start.4 = (bf16[9728,256]{1,0:T(8,128)(2,1)S(1)}, bf16[9728,256]{1,0:T(8,128)(2,1)}, u32[]{:S(2)}) copy-start(bf16[9728,256]{1,0:T(8,128)(2,1)} %copy-done.3) | copy-start | bytes 14942212
  91.1 6.6 %copy-start.6 = (f32[6912,128]{1,0:T(8,128)S(1)}, f32[6912,128]{1,0:T(8,128)}, u32[]{:S(2)}) copy-start(f32[6912,128]{1,0:T(8,128)} %copy-done.5) | copy-start | bytes 10616836
  97.6 24.2 %collective-permute-start.3 = (f32[1728,128]{1,0:T(8,128)S(1)}, f32[1728,128]{1,0:T(8,128)S(1)}, u32[]{:S(2)}, u32[]{:S(2)}) collective-permute-start(f32[1728,128]{1,0:T(8,128)S(1)} %get-tuple-element.31), channel_id=1, source_target_pairs={{0,2},{2,4},{4,6},{6,8},{8,10},{10,12},{12,14},{14,16},{16,18},{18... | collective-permute-start | bytes 2654216 | tf_op jit(solution)/shard_map/ppermute | solution.py:40
  127.7 5.2 %collective-permute-start.4 = (bf16[192,6912]{1,0:T(8,128)(2,1)S(1)}, bf16[192,6912]{1,0:T(8,128)(2,1)}, u32[]{:S(2)}, u32[]{:S(2)}) collective-permute-start(bf16[192,6912]{1,0:T(8,128)(2,1)S(1)} %get-tuple-element.32.own), channel_id=1, source_target_pairs={{0,1},{1,0},{2,3},{3,2},{4,5},{5,4},{6,7},{7,6},{8,9},{9,8},{10,11... | collective-permute-start | bytes 7962632 | tf_op jit(solution)/shard_map/ppermute | solution.py:40
  135.7 5.3 %collective-permute-start.5 = (f32[96,128]{1,0:T(8,128)S(1)}, f32[96,128]{1,0:T(8,128)S(1)}, u32[]{:S(2)}, u32[]{:S(2)}) collective-permute-start(f32[96,128]{1,0:T(8,128)S(1)} %get-tuple-element.33), channel_id=1, source_target_pairs={{0,2},{2,4},{4,6},{6,0},{8,10},{10,12},{12,14},{14,8},{16,18},{18,... | collective-permute-start | bytes 147464 | tf_op jit(solution)/shard_map/ppermute | solution.py:516
  135.8 5.2 %collective-permute-start.6 = (f32[96,128]{1,0:T(8,128)S(1)}, f32[96,128]{1,0:T(8,128)S(1)}, u32[]{:S(2)}, u32[]{:S(2)}) collective-permute-start(f32[96,128]{1,0:T(8,128)S(1)} %get-tuple-element.35), channel_id=1, source_target_pairs={{0,4},{2,6},{4,0},{6,2},{8,12},{10,14},{12,8},{14,10},{16,20},{18,... | collective-permute-start | bytes 147464 | tf_op jit(solution)/shard_map/ppermute | solution.py:516
  135.9 5.5 %collective-permute-start.7 = (f32[96,128]{1,0:T(8,128)S(1)}, f32[96,128]{1,0:T(8,128)S(1)}, u32[]{:S(2)}, u32[]{:S(2)}) collective-permute-start(f32[96,128]{1,0:T(8,128)S(1)} %get-tuple-element.34), channel_id=1, source_target_pairs={{0,6},{2,0},{4,2},{6,4},{8,14},{10,8},{12,10},{14,12},{16,22},{18,... | collective-permute-start | bytes 147464 | tf_op jit(solution)/shard_map/ppermute | solution.py:516
  141.3 4.6 %collective-permute-start.10 = (f32[96,128]{1,0:T(8,128)S(1)}, f32[96,128]{1,0:T(8,128)S(1)}, u32[]{:S(2)}, u32[]{:S(2)}) collective-permute-start(f32[96,128]{1,0:T(8,128)S(1)} %fusion.5), channel_id=1, source_target_pairs={{0,24},{2,26},{4,28},{6,30},{8,0},{10,2},{12,4},{14,6},{16,8},{18,... | collective-permute-start | bytes 147464 | tf_op jit(solution)/shard_map/ppermute | solution.py:516
  141.4 5.9 %collective-permute-start.8 = (f32[96,128]{1,0:T(8,128)S(1)}, f32[96,128]{1,0:T(8,128)S(1)}, u32[]{:S(2)}, u32[]{:S(2)}) collective-permute-start(f32[96,128]{1,0:T(8,128)S(1)} %fusion.5), channel_id=1, source_target_pairs={{0,8},{2,10},{4,12},{6,14},{8,16},{10,18},{12,20},{14,22},{16,24},... | collective-permute-start | bytes 147464 | tf_op jit(solution)/shard_map/ppermute | solution.py:516
  143.4 5.0 %collective-permute-start.9 = (f32[96,128]{1,0:T(8,128)S(1)}, f32[96,128]{1,0:T(8,128)S(1)}, u32[]{:S(2)}, u32[]{:S(2)}) collective-permute-start(f32[96,128]{1,0:T(8,128)S(1)} %fusion.5), channel_id=1, source_target_pairs={{0,16},{2,18},{4,20},{6,22},{8,24},{10,26},{12,28},{14,30},{16,0},... | collective-permute-start | bytes 147464 | tf_op jit(solution)/shard_map/ppermute | solution.py:516
  148.4 5.0 %collective-permute-start.11 = (f32[96,128]{1,0:T(8,128)S(1)}, f32[96,128]{1,0:T(8,128)S(1)}, u32[]{:S(2)}, u32[]{:S(2)}) collective-permute-start(f32[96,128]{1,0:T(8,128)S(1)} %add_add_fusion.refs_0_), channel_id=1, source_target_pairs={{0,2},{2,4},{4,6},{6,0},{8,10},{10,12},{12,14},{14,8},{16,18},{18,... | collective-permute-start | bytes 147464 | tf_op jit(solution)/shard_map/ppermute | solution.py:516
  151.4 4.1 %collective-permute-start.12 = (f32[96,128]{1,0:T(8,128)S(1)}, f32[96,128]{1,0:T(8,128)S(1)}, u32[]{:S(2)}, u32[]{:S(2)}) collective-permute-start(f32[96,128]{1,0:T(8,128)S(1)} %add_add_fusion.refs_0_), channel_id=1, source_target_pairs={{0,4},{2,6},{4,0},{6,2},{8,12},{10,14},{12,8},{14,10},{16,20},{18,... | collective-permute-start | bytes 147464 | tf_op jit(solution)/shard_map/ppermute | solution.py:516
  151.4 4.1 %collective-permute-start.13 = (f32[96,128]{1,0:T(8,128)S(1)}, f32[96,128]{1,0:T(8,128)S(1)}, u32[]{:S(2)}, u32[]{:S(2)}) collective-permute-start(f32[96,128]{1,0:T(8,128)S(1)} %add_add_fusion.refs_0_), channel_id=1, source_target_pairs={{0,6},{2,0},{4,2},{6,4},{8,14},{10,8},{12,10},{14,12},{16,22},{18,... | collective-permute-start | bytes 147464 | tf_op jit(solution)/shard_map/ppermute | solution.py:516
  152.9 3.1 %collective-permute-start.14 = (f32[96,128]{1,0:T(8,128)S(1)}, f32[96,128]{1,0:T(8,128)S(1)}, u32[]{:S(2)}, u32[]{:S(2)}) collective-permute-start(f32[96,128]{1,0:T(8,128)S(1)} %add_add_fusion.refs_0_), channel_id=1, source_target_pairs={{0,1},{1,0},{2,3},{3,2},{4,5},{5,4},{6,7},{7,6},{8,9},{9,8},{10,11... | collective-permute-start | bytes 147464 | tf_op jit(solution)/shard_map/ppermute | solution.py:40
  153.5 2.6 %collective-permute-start.15 = (f32[96,128]{1,0:T(8,128)S(1)}, f32[96,128]{1,0:T(8,128)S(1)}, u32[]{:S(2)}, u32[]{:S(2)}) collective-permute-start(f32[96,128]{1,0:T(8,128)S(1)} %collective-permute-done.11.refs_1_), channel_id=1, source_target_pairs={{0,1},{1,0},{2,3},{3,2},{4,5},{5,4},{6,7},{7,6},{8,9},{9,8},{10,11... | collective-permute-start | bytes 147464 | tf_op jit(solution)/shard_map/ppermute | solution.py:40
  155.5 1.2 collective-permute-start.16
  155.5 1.4 collective-permute-start.17

commit v3 on v2

--- a/solution.py
+++ b/solution.py
@@ -9,6 +9,7 @@
 NS_STEPS = 3
 LANES = 128
 BATCH = 8
+CODES = 32767.0
 
 cheb_center = 3.0
 cheb_half = 7.0
@@ -16,7 +17,7 @@
 
 VMEM = pl.BlockSpec(memory_space=pltpu.VMEM)
 SMEM = pl.BlockSpec(memory_space=pltpu.SMEM)
-ANY = pl.BlockSpec(memory_space=pl.ANY)
+HBM = pl.BlockSpec(memory_space=pltpu.HBM)
 
 
 def called(kernel, shapes, in_specs, scratch, microseconds, limit, out_specs=None, **options):
@@ -45,7 +46,7 @@
 
 
 def block_of(count):
-    for size in (256, 128):
+    for size in (256, 384, 128):
         if count % size == 0:
             return size
     return count
@@ -61,17 +62,18 @@
     return lax.dot_general(left, right, (((1,), (1,)), ((), ())), preferred_element_type=jnp.float32)
 
 
-def across_wide(unit, wide):
+def split3(wide):
     first = wide.astype(jnp.bfloat16)
     rest = wide - first.astype(jnp.float32)
     second = rest.astype(jnp.bfloat16)
-    third = (rest - second.astype(jnp.float32)).astype(jnp.bfloat16)
-    return across(unit, first) + (across(unit, second) + across(unit, third))
-
-
-def padded_rows(block):
-    width = block.shape[0]
-    return jnp.concatenate([block, jnp.zeros((2 * LANES - width, block.shape[1]), block.dtype)], axis=0)
+    return first, second, (rest - second.astype(jnp.float32)).astype(jnp.bfloat16)
+
+
+def diagonal(high, width):
+    row = lax.broadcasted_iota(jnp.int32, (LANES, LANES), 0)
+    at = width - LANES
+    chosen = jnp.where((row >= at) & (row < at + 3), 1.0, 0.0).astype(jnp.bfloat16)
+    return jnp.dot(high.astype(jnp.bfloat16), chosen, preferred_element_type=jnp.float32)
 
 
 def node_rows(start, count):
@@ -116,14 +118,6 @@
     some_rows(face.shape[0], 64, body)
 
 
-def store_face(face, source, target):
-    def body(base, size):
-        for j in range(size):
-            target[pair(2 * face[base + j]), :] = source[pair(2 * (base + j)), :]
-
-    some_rows(face.shape[0], 64, body)
-
-
 def add_face(face, source, target):
     def body(base, size):
         places = [pair(2 * face[base + j]) for j in range(size)]
@@ -131,10 +125,72 @@
         for j in range(size):
             target[places[j], :] = rows[j] + source[pair(2 * (base + j)), :]
 
-    some_rows(face.shape[0], BATCH, body)
-
-
-def prepare_kernel(width, chunks, face, states, nodes, send, picked, held, sems):
+    some_rows(face.shape[0], 16, body)
+
+
+def group_of(count):
+    for size in (12, 8, 9, 6, 4, 3, 2):
+        if count % (8 * size) == 0:
+            return size
+    return 1
+
+
+def coded(values):
+    count = values.shape[0]
+    size = group_of(count)
+    grouped = values.reshape(count // (8 * size), size, 8, LANES)
+    top = jnp.max(jnp.abs(grouped), axis=1, keepdims=True)
+    top = jnp.maximum(top * 1.01, 1e-30).astype(jnp.bfloat16)
+    codes = jnp.round(grouped * (CODES / top.astype(jnp.float32)))
+    return codes.reshape(count, LANES).astype(jnp.int32).astype(jnp.int16), top.reshape(count // size, LANES)
+
+
+def decoded(codes, top):
+    count = codes.shape[0]
+    size = count // top.shape[0]
+    grouped = codes.astype(jnp.int32).astype(jnp.float32).reshape(count // (8 * size), size, 8, LANES)
+    unit = top.astype(jnp.float32).reshape(count // (8 * size), 1, 8, LANES) / CODES
+    return (grouped * unit).reshape(count, LANES)
+
+
+def tables_kernel(sizes, owned, cell_nodes, kinetic, table, late_table, matrix, regular):
+    cells, early, early_rows, late_rows, stride = sizes
+    slots = cell_nodes.shape[1]
+    late = slots - early
+    nodes = cell_nodes[...]
+    wide_nodes = jnp.concatenate([2 * nodes, jnp.zeros((cells, stride - slots), jnp.int32)], axis=1)
+    per = stride // LANES
+    for part in range(per):
+        table[pl.ds(part, cells, per), :] = wide_nodes[:, part * LANES : (part + 1) * LANES]
+    late_table[:, :late] = 2 * (nodes[:, early:] - owned)
+    late_table[:, late:] = jnp.zeros((cells, LANES - late), jnp.int32)
+    wide = kinetic[...].astype(jnp.float32)
+    wide = jnp.concatenate(
+        [
+            wide[:, :early],
+            jnp.zeros((slots, early_rows - early), jnp.float32),
+            wide[:, early:],
+            jnp.zeros((slots, late_rows - late), jnp.float32),
+        ],
+        axis=1,
+    )
+    columns = wide.shape[1]
+    wide = jnp.concatenate(
+        [
+            wide[:early],
+            jnp.zeros((early_rows - early, columns), jnp.float32),
+            wide[early:],
+            jnp.zeros((late_rows - late, columns), jnp.float32),
+        ],
+        axis=0,
+    )
+    matrix[...] = wide.astype(jnp.bfloat16)
+    slot = lax.broadcasted_iota(jnp.int32, nodes.shape, 1)
+    odd = jnp.where((nodes >= owned) == (slot >= early), 0, 1)
+    regular[0] = jnp.where((jnp.max(odd) == 0) & (cells % 4 == 0), 1, 0)
+
+
+def prepare_kernel(width, chunks, face, potential, states, nodes, send, picked, held, sems):
     owned = states.shape[1]
     block = block_of(owned)
     piece = owned // chunks
@@ -149,7 +205,14 @@
 
         def one(i, _):
             first = pl.multiple_of(k * piece + i * block, block)
-            turned = across(unit, padded_rows(held[:, pl.ds(first, block)]))
+            at = pl.ds(first, block)
+            local = potential[:, at] - cheb_center
+            parts = split3(local)
+            row = lax.broadcasted_iota(jnp.int32, (2 * LANES - width, block), 0)
+            tail = jnp.zeros(row.shape, jnp.float32)
+            for place, part in enumerate(parts):
+                tail = jnp.where(row == place, part.astype(jnp.float32), tail)
+            turned = across(unit, jnp.concatenate([held[:, at], tail.astype(jnp.bfloat16)], axis=0))
             low, high = node_rows(first, block)
             nodes[low, :] = turned[:, :LANES]
             nodes[high, :] = turned[:, LANES:]
@@ -163,7 +226,7 @@
     send[count:, :] = high.astype(jnp.bfloat16)
 
 
-def gather_own(sizes, table, nodes, matrix, values_out, partial, buffers):
+def gather_own(sizes, again, table, nodes, matrix, values_out, partial, buffers):
     cells, early, early_rows, late_rows, stride = sizes
     for buffer in buffers:
         buffer[...] = jnp.zeros(buffer.shape, jnp.float32)
@@ -176,7 +239,7 @@
     def finish(cell, buffer):
         low = buffer[pl.ds(0, early_rows, 2), :]
         high = buffer[pl.ds(1, early_rows, 2), :]
-        values = jnp.concatenate([low, high], axis=1).astype(jnp.bfloat16)
+        values = once_rounded(jnp.concatenate([low, high], axis=1), again)
         values_out[pl.ds(pl.multiple_of(cell * early_rows, early_rows), early_rows), :] = values
         partial[pl.ds(pl.multiple_of(cell * late_rows, late_rows), late_rows), :] = jnp.dot(
             matrix[early_rows:, :early_rows], values, preferred_element_type=jnp.float32
@@ -193,35 +256,23 @@
     finish(cells - 1, buffers[1])
 
 
-def own_kernel(sizes, regular, table, nodes, matrix, values_out, partial, *buffers):
+def once_rounded(summed, again):
+    return (summed * (1.0 / cheb_half) if again else summed).astype(jnp.bfloat16)
+
+
+def own_kernel(sizes, again, regular, table, nodes, matrix, values_out, partial, *buffers):
     @pl.when(regular[0] == 1)
     def _():
-        gather_own(sizes, table, nodes, matrix, values_out, partial, buffers)
-
-
-def own_again_kernel(sizes, regular, face, table, total, picked, matrix, nodes, values_out, partial, *buffers):
-    block = 2 * block_of(nodes.shape[0] // 2)
-
-    def one(i, _):
-        at = pl.ds(pl.multiple_of(i * block, block), block)
-        nodes[at, :] = (total[at, :] / cheb_half).astype(jnp.bfloat16).astype(jnp.float32)
-        return 0
-
-    lax.fori_loop(0, nodes.shape[0] // block, one, 0)
-    store_face(face, picked, nodes)
-
-    @pl.when(regular[0] == 1)
-    def _():
-        gather_own(sizes, table, nodes, matrix, values_out, partial, buffers)
-
-
-def any_cell(sizes, cell, table, nodes, ghosts, matrix, gathered, products):
+        gather_own(sizes, again, table, nodes, matrix, values_out, partial, buffers)
+
+
+def any_cell(sizes, again, cell, table, nodes, ghosts, matrix, gathered, products):
     cells, early, early_rows, late_rows, stride = sizes
     owned2 = nodes.shape[0]
 
     def fetch(a, _):
         place = table[cell * stride + a]
-        own = nodes[pair(jnp.minimum(place, owned2 - 2)), :]
+        own = once_rounded(nodes[pair(jnp.minimum(place, owned2 - 2)), :], again).astype(jnp.float32)
         other = ghosts[pair(jnp.maximum(place - owned2, 0)), :]
         row = jnp.where(a < early, a, a - early + early_rows)
         gathered[pair(2 * row), :] = jnp.where(place < owned2, own, other)
@@ -239,13 +290,13 @@
     return fetch, multiply
 
 
-def any_cells(sizes, slots, owned_part, table, nodes, ghosts, matrix, gathered, products, total):
+def any_cells(sizes, again, slots, owned_part, table, nodes, ghosts, matrix, gathered, products, total):
     cells, early, early_rows, late_rows, stride = sizes
     owned2 = nodes.shape[0]
     gathered[...] = jnp.zeros(gathered.shape, jnp.float32)
 
     def one(cell, _):
-        fetch, multiply = any_cell(sizes, cell, table, nodes, ghosts, matrix, gathered, products)
+        fetch, multiply = any_cell(sizes, again, cell, table, nodes, ghosts, matrix, gathered, products)
         lax.fori_loop(0, slots, fetch, 0)
         multiply()
 
@@ -266,8 +317,9 @@
     lax.fori_loop(0, cells, one, 0)
 
 
-def shared_kernel(sizes, slots, width, regular, table, late_table, arrived, nodes, matrix, partial,
-                  send, values_out, ghosts, total, other, gathered, products, any_gathered, any_products):
+def shared_kernel(sizes, slots, width, again, regular, table_in, late_table, arrived, nodes, matrix, partial,
+                  send, tops, values_out, ghosts, total, other, gathered, products, any_gathered, any_products,
+                  table, sem):
     cells, early, early_rows, late_rows, stride = sizes
     late = slots - early
     count = ghosts.shape[0] // 2
@@ -327,12 +379,16 @@
 
     @pl.when(regular[0] != 1)
     def _():
-        any_cells(sizes, slots, False, table, nodes, ghosts, matrix, any_gathered, any_products, total)
+        copy = pltpu.make_async_copy(table_in, table, sem)
+        copy.start()
+        copy.wait()
+        any_cells(sizes, again, slots, False, table, nodes, ghosts, matrix, any_gathered, any_products, total)
 
     low, high = (total[pl.ds(k, count, 2), :] + other[pl.ds(k, count, 2), :] for k in range(2))
     low, high = pack(low, high, width)
-    send[:count, :] = low
-    send[count:, :] = high
+    codes, top = coded(jnp.concatenate([low, high], axis=0))
+    send[...] = codes
+    tops[...] = top
 
 
 def scatter_rows(lists, slots, products, totals):
@@ -388,39 +444,30 @@
     lax.fori_loop(0, cells // 4, four, 0)
 
 
-def factor_kernel(potential, factor):
-    owned = factor.shape[0]
-    block = block_of(owned)
-    unit = identity(block)
-
-    def one(i, _):
-        at = pl.ds(pl.multiple_of(i * block, block), block)
-        local = jnp.broadcast_to(potential[:, at], (LANES, block))
-        factor[at, :] = across_wide(unit, local) - cheb_center
-        return 0
-
-    lax.fori_loop(0, owned // block, one, 0, unroll=3)
-
-
-def scatter_kernel(sizes, slots, width, again, regular, table, factor, matrix, own_values, late_values,
-                   arrived, nodes, *rest):
+def scatter_kernel(sizes, slots, width, again, regular, table, matrix, own_values, late_values, arrived,
+                   nodes, *rest):
     if again:
         states, total, other, *rest = rest
     else:
         total, other, *rest = rest
     *products, ghosts, any_gathered, any_products = rest
-    owned = factor.shape[0]
+    owned = nodes.shape[0] // 2
     block = block_of(owned)
 
     def begin(i, _):
-        first = pl.multiple_of(i * block, block)
-        scale = factor[pl.ds(first, block), :]
-        for rows in node_rows(first, block):
-            value = scale * nodes[rows, :]
-            total[rows, :] = value - (cheb_half / 2.0) * states[rows, :] if again else value
+        low, high = node_rows(pl.multiple_of(i * block, block), block)
+        if again:
+            factor = diagonal(states[high, :], width)
+            for rows in (low, high):
+                value = once_rounded(nodes[rows, :], again).astype(jnp.float32)
+                total[rows, :] = factor * value - (cheb_half / 2.0) * states[rows, :]
+        else:
+            factor = diagonal(nodes[high, :], width)
+            for rows in (low, high):
+                total[rows, :] = factor * nodes[rows, :]
         return 0
 
-    lax.fori_loop(0, owned // block, begin, 0)
+    lax.fori_loop(0, owned // block, begin, 0, unroll=3)
 
     @pl.when(regular[0] == 1)
     def _():
@@ -446,63 +493,93 @@
         low, high = unpack(arrived[...].astype(jnp.float32), count, width)
         ghosts[pl.ds(0, count, 2), :] = low
         ghosts[pl.ds(1, count, 2), :] = high
-        any_cells(sizes, slots, True, table, nodes, ghosts, matrix, any_gathered, any_products, total)
-
-
-def once_kernel(width, face, total, returned, send, picked):
+        any_cells(sizes, again, slots, True, table, nodes, ghosts, matrix, any_gathered, any_products, total)
+
+
+def add_returned(width, face, returned, tops, total, spread):
     count = face.shape[0]
-    gather_face(face, total, picked)
-    low, high = unpack(returned[...], count, width)
-    low = ((picked[pl.ds(0, count, 2), :] + low) / cheb_half).astype(jnp.bfloat16)
-    high = ((picked[pl.ds(1, count, 2), :] + high) / cheb_half).astype(jnp.bfloat16)
-    picked[pl.ds(0, count, 2), :] = low.astype(jnp.float32)
-    picked[pl.ds(1, count, 2), :] = high.astype(jnp.float32)
-    low, high = pack(low.astype(jnp.float32), high.astype(jnp.float32), width)
-    send[:count, :] = low.astype(jnp.bfloat16)
-    send[count:, :] = high.astype(jnp.bfloat16)
-
-
-def twice_kernel(width, face, total_in, returned, total, filtered, spread):
-    owned = filtered.shape[1]
-    count = face.shape[0]
-    low, high = unpack(returned[...], count, width)
+    low, high = unpack(decoded(returned[...], tops[...]), count, width)
     spread[pl.ds(0, count, 2), :] = low
     spread[pl.ds(1, count, 2), :] = high
     add_face(face, spread, total)
-    block = block_of(owned)
+
+
+def once_kernel(width, face, total_in, returned, tops, total, send, spread):
+    count = face.shape[0]
+    add_returned(width, face, returned, tops, total, spread)
+    gather_face(face, total, spread)
+    low = once_rounded(spread[pl.ds(0, count, 2), :], True).astype(jnp.float32)
+    high = once_rounded(spread[pl.ds(1, count, 2), :], True).astype(jnp.float32)
+    low, high = pack(low, high, width)
+    send[:count, :] = low.astype(jnp.bfloat16)
+    send[count:, :] = high.astype(jnp.bfloat16)
+
+
+def filter_half(total, filtered, start, width):
+    half = filtered.shape[1]
+    block = block_of(half)
     unit = identity(2 * LANES)
 
     def one(i, _):
         first = pl.multiple_of(i * block, block)
-        low, high = node_rows(first, block)
+        low, high = node_rows(start + first, block)
         values = jnp.concatenate([total[low, :], total[high, :]], axis=1) * (2.0 / cheb_half)
         filtered[:, pl.ds(first, block)] = across(unit, values.astype(jnp.bfloat16))[:width].astype(jnp.bfloat16)
         return 0
 
-    lax.fori_loop(0, owned // block, one, 0, unroll=3)
-
-
-def gram_own_kernel(own, block):
-    block[...] = across(own[...], own[...])
-
-
-def gram_kernel(width, place, gram, own, other, slabs):
+    lax.fori_loop(0, half // block, one, 0, unroll=3)
+
+
+def twice_kernel(width, face, total_in, returned, tops, total, filtered, spread):
+    add_returned(width, face, returned, tops, total, spread)
+    filter_half(total, filtered, 0, width)
+
+
+def second_half_kernel(width, total, filtered):
+    filter_half(total, filtered, total.shape[0] // 2 - filtered.shape[1], width)
+
+
+def gram_own_kernel(first, second, block):
+    block[...] = across(first[...], first[...]) + across(second[...], second[...])
+
+
+def cross_rows_of(own, other, write):
+    half = own.shape[0] // 2
+    place = lax.axis_index("state")
+
+    @pl.when(place == 0)
+    def _():
+        write(across(own[:half, :], other[...]))
+
+    @pl.when(place != 0)
+    def _():
+        write(across(other[half:, :], own[...]))
+
+
+def cross_kernel(own, other, cross):
+    def write(value):
+        cross[...] = value
+
+    cross_rows_of(own, other, write)
+
+
+def gram_kernel(width, gram, begun, own, other, *outs):
+    *pieces, slabs = outs
     half = width // 2
     rest = (width - LANES) // 2
 
-    def write(cross):
+    def write(value):
+        cross = begun[...] + value
         slabs[0] = cross[:, :LANES]
         slabs[1] = jnp.concatenate([gram[:half, :half], cross[:, LANES : LANES + rest]], axis=1)
         slabs[2] = jnp.concatenate([gram[:half, half:], cross[:, LANES + rest :]], axis=1)
         slabs[3] = jnp.concatenate([gram[half:, half:], jnp.zeros((half, LANES - half), jnp.float32)], axis=1)
 
-    @pl.when(place[0] == 0)
-    def _():
-        write(across(own[:half, :], other[...]))
-
-    @pl.when(place[0] != 0)
-    def _():
-        write(across(other[half:, :], own[...]))
+    cross_rows_of(own, other, write)
+    radix = len(pieces)
+    digit = lax.rem(lax.axis_index("brick"), radix)
+    for step, piece in enumerate(pieces):
+        piece[...] = slabs[lax.rem(digit + step, radix)]
 
 
 def exchanged(axis, stride, radix, give):
@@ -517,32 +594,29 @@
     ]
 
 
-def summed_over(slabs, axis):
+def summed_over(pieces, axis):
     count = lax.axis_size(axis)
-    place = lax.axis_index(axis)
-    radix = slabs.shape[0]
-    radices = [radix]
+    radix = len(pieces)
+    radices = []
     left = count // radix
     while left > 1:
         some = 4 if left % 4 == 0 else 2 if left % 2 == 0 else left
         radices.append(some)
         left //= some
-    digit = place % radix
-    take = lambda step: lax.dynamic_index_in_dim(slabs, (digit + step) % radix, 0, keepdims=False)
-    piece = functools.reduce(jnp.add, exchanged(axis, 1, radix, take), take(0))
+    piece = functools.reduce(jnp.add, exchanged(axis, 1, radix, lambda step: pieces[step]), pieces[0])
     stride = radix
-    for some in radices[1:]:
+    for some in radices:
         piece = functools.reduce(jnp.add, exchanged(axis, stride, some, lambda step: piece), piece)
         stride *= some
-    return [piece] + exchanged(axis, 1, radix, lambda step: piece), digit
-
-
-def root_kernel(width, where, *refs):
+    return [piece] + exchanged(axis, 1, radix, lambda step: piece)
+
+
+def root_kernel(width, *refs):
     radix = 4
     mine, theirs = refs[:radix], refs[radix : 2 * radix]
     root, own_slabs, other_slabs = refs[2 * radix :]
-    digit = where[0]
-    place = where[1]
+    digit = lax.rem(lax.axis_index("brick"), radix)
+    place = lax.axis_index("state")
     for step in range(radix):
         slab = lax.rem(digit + radix - step, radix)
         own_slabs[slab] = mine[step][...]
@@ -589,10 +663,22 @@
     root[...] = (0.5 * product(factor, inverse)).astype(jnp.bfloat16)
 
 
-def rotate_kernel(width, root, own, other, result):
-    result[...] = jnp.dot(root[:, :width], own[...], preferred_element_type=jnp.float32) + jnp.dot(
-        root[:, width:], other[...], preferred_element_type=jnp.float32
-    )
+def rotate_kernel(width, pieces, root, first, first_other, second, second_other, result, held, sems):
+    half = first.shape[1]
+    size = half // pieces
+    copies = []
+    for k in range(2 * pieces):
+        own, other = (first, first_other) if k < pieces else (second, second_other)
+        at = pl.ds(k % pieces * size, size)
+        if k >= 2:
+            copies[k - 2].wait()
+        held[k % 2] = jnp.dot(root[:, :width], own[:, at], preferred_element_type=jnp.float32) + jnp.dot(
+            root[:, width:], other[:, at], preferred_element_type=jnp.float32
+        )
+        copies.append(pltpu.make_async_copy(held.at[k % 2], result.at[:, pl.ds(k * size, size)], sems.at[k % 2]))
+        copies[k].start()
+    for copy in copies[-2:]:
+        copy.wait()
 
 
 def local(states, kinetic, potential, cell_nodes, face_map):
@@ -608,25 +694,11 @@
     stride = rounded_up(slots, LANES)
     sizes = (cells, early, early_rows, late_rows, stride)
     packed = count + count // (LANES // (width - LANES))
-
-    regular = jnp.all(cell_nodes[:, :early] < owned) & jnp.all(cell_nodes[:, early:] >= owned)
-    regular = (regular & (cells % 4 == 0)).astype(jnp.int32).reshape(1)
-    table = jnp.pad(2 * cell_nodes, ((0, 0), (0, stride - slots))).reshape(-1)
-    late_table = jnp.pad(2 * (cell_nodes[:, early:] - owned), ((0, 0), (0, LANES - late))).reshape(-1)
-
-    def spaced(array, axis):
-        head, tail = jnp.split(array, [early], axis)
-        fill = lambda part, size: jnp.pad(
-            part, [(0, size - part.shape[k]) if k == axis else (0, 0) for k in range(2)]
-        )
-        return jnp.concatenate([fill(head, early_rows), fill(tail, late_rows)], axis)
-
-    matrix = spaced(spaced(kinetic, 0), 1)
+    integers = lambda *shape: jax.ShapeDtypeStruct(shape, jnp.int32)
+
     lumped = potential[None, :]
     wide = jax.ShapeDtypeStruct((2 * owned, LANES), jnp.float32)
     sent = jax.ShapeDtypeStruct((packed, LANES), jnp.bfloat16)
-    sent_wide = jax.ShapeDtypeStruct((packed, LANES), jnp.float32)
-    face_rows = jax.ShapeDtypeStruct((2 * count, LANES), jnp.float32)
     own_values = jax.ShapeDtypeStruct((cells * early_rows, 2 * LANES), jnp.bfloat16)
     late_values = jax.ShapeDtypeStruct((cells * late_rows, 2 * LANES), jnp.bfloat16)
     partial = jax.ShapeDtypeStruct((cells * late_rows, 2 * LANES), jnp.float32)
@@ -639,114 +711,124 @@
     begun, send = called(
         functools.partial(prepare_kernel, width, chunks),
         (wide, sent),
-        [SMEM, ANY],
+        [SMEM, VMEM, HBM],
         [spread, pltpu.VMEM((width, owned), jnp.bfloat16), pltpu.SemaphoreType.DMA((chunks,))],
         6,
-        20,
-    )(face_map, states)
-
-    def shared(arrived, nodes, partial):
+        6,
+    )(face_map, lumped, states)
+
+    table, late_table, matrix, regular = called(
+        functools.partial(tables_kernel, sizes, owned),
+        (
+            integers(cells * (stride // LANES), LANES),
+            integers(cells, LANES),
+            jax.ShapeDtypeStruct((rows, rows), jnp.bfloat16),
+            integers(1),
+        ),
+        [VMEM, VMEM],
+        [],
+        2,
+        8,
+        out_specs=(VMEM, VMEM, VMEM, SMEM),
+    )(cell_nodes, kinetic)
+    table, late_table = table.reshape(-1), late_table.reshape(-1)
+    sent_short = jax.ShapeDtypeStruct((packed, LANES), jnp.int16)
+    tops = jax.ShapeDtypeStruct((packed // group_of(packed), LANES), jnp.bfloat16)
+
+    def shared(again, arrived, nodes, partial):
         return called(
-            functools.partial(shared_kernel, sizes, slots, width),
-            (sent_wide, late_values),
-            [SMEM, SMEM, SMEM, VMEM, VMEM, VMEM, VMEM],
-            [spread, spread, spread, pairs_late, pairs_late, pairs_any, pairs_any],
+            functools.partial(shared_kernel, sizes, slots, width, again),
+            (sent_short, tops, late_values),
+            [SMEM, VMEM, SMEM, VMEM, VMEM, VMEM, VMEM],
+            [spread, spread, spread, pairs_late, pairs_late, pairs_any, pairs_any]
+            + [pltpu.SMEM((cells * stride,), jnp.int32), pltpu.SemaphoreType.DMA],
             6,
-            24,
+            11,
         )(regular, table, late_table, arrived, nodes, matrix, partial)
 
-    (factor,) = called(
-        factor_kernel, (jax.ShapeDtypeStruct((owned, LANES), jnp.float32),), [VMEM], [], 3, 8
-    )(lumped)
+    def own(again, nodes):
+        return called(
+            functools.partial(own_kernel, sizes, again),
+            (own_values, partial),
+            [SMEM, SMEM, VMEM, VMEM],
+            [pairs_own, pairs_own],
+            11,
+            3,
+        )(regular, table, nodes, matrix)
 
     def scattered(again, values, late, arrived, nodes, *before):
         return called(
             functools.partial(scatter_kernel, sizes, slots, width, again),
             (wide,),
-            [SMEM, SMEM] + [VMEM] * (6 + len(before)),
+            [SMEM, SMEM] + [VMEM] * (5 + len(before)),
             [pltpu.VMEM((2 * owned, LANES), jnp.float32)] + [pairs_own] * 4 + [spread, pairs_any, pairs_any],
             18,
-            20,
-        )(regular, table, factor, matrix, values, late, arrived, nodes, *before)[0]
-
-    arrived = passed_along(send, "brick", -1)
-    values, part = called(
-        functools.partial(own_kernel, sizes),
-        (own_values, partial),
-        [SMEM, SMEM, VMEM, VMEM],
-        [pairs_own, pairs_own],
-        10,
-        16,
-    )(regular, table, begun, matrix)
-    back, late_in = shared(arrived, begun, part)
-    returned = passed_along(back, "brick", 1)
-    total = scattered(False, values, late_in, arrived, begun)
-    send, picked = called(
+            14,
+        )(regular, table, matrix, values, late, arrived, nodes, *before)[0]
+
+    def begun_sums(again, send, nodes, *before):
+        arrived = passed_along(send, "brick", -1)
+        values, part = own(again, nodes)
+        back, top, late_in = shared(again, arrived, nodes, part)
+        returned = passed_along(back, "brick", 1)
+        returned_top = passed_along(top, "brick", 1)
+        return scattered(again, values, late_in, arrived, nodes, *before), returned, returned_top
+
+    total, send = called(
         functools.partial(once_kernel, width),
-        (sent, face_rows),
-        [SMEM, VMEM, VMEM],
-        [],
+        (wide, sent),
+        [SMEM, VMEM, VMEM, VMEM],
+        [spread],
         3,
-        16,
-    )(face_map, total, returned)
-    arrived = passed_along(send, "brick", -1)
-    nodes, values, part = called(
-        functools.partial(own_again_kernel, sizes),
-        (wide, own_values, partial),
-        [SMEM, SMEM, SMEM, VMEM, VMEM, VMEM],
-        [pairs_own, pairs_own],
-        12,
-        20,
-    )(regular, face_map, table, total, picked, matrix)
-    back, late_in = shared(arrived, nodes, part)
-    returned = passed_along(back, "brick", 1)
-    total = scattered(True, values, late_in, arrived, nodes, begun)
-    _, filtered = called(
+        6,
+        input_output_aliases={1: 0},
+    )(face_map, *begun_sums(False, send, begun))
+    total, returned, returned_top = begun_sums(True, send, total, begun)
+    half = jax.ShapeDtypeStruct((width, owned // 2), jnp.bfloat16)
+    total, first = called(
         functools.partial(twice_kernel, width),
-        (wide, jax.ShapeDtypeStruct((width, owned), jnp.bfloat16)),
-        [SMEM, VMEM, VMEM],
+        (wide, half),
+        [SMEM, VMEM, VMEM, VMEM],
         [spread],
         5,
-        24,
+        6,
         input_output_aliases={1: 0},
-    )(face_map, total, returned)
-
-    place = lax.axis_index("state")
-    other = passed_along(filtered, "state", 1)
+    )(face_map, total, returned, returned_top)
+    first_other = passed_along(first, "state", 1)
+    (second,) = called(functools.partial(second_half_kernel, width), (half,), [VMEM], [], 2, 4)(total)
+    second_other = passed_along(second, "state", 1)
+
     (gram,) = called(
-        gram_own_kernel, (jax.ShapeDtypeStruct((width, width), jnp.float32),), [VMEM], [], 1, 16
-    )(filtered)
-    (slabs,) = called(
-        functools.partial(gram_kernel, width),
-        (jax.ShapeDtypeStruct((4, width // 2, LANES), jnp.float32),),
-        [SMEM, VMEM, VMEM, VMEM],
-        [],
-        1,
-        20,
-    )(place.astype(jnp.int32).reshape(1), gram, filtered, other)
-    mine, digit = summed_over(slabs, "brick")
+        gram_own_kernel, (jax.ShapeDtypeStruct((width, width), jnp.float32),), [VMEM, VMEM], [], 1, 4
+    )(first, second)
+    (cross,) = called(
+        cross_kernel, (jax.ShapeDtypeStruct((width // 2, width), jnp.float32),), [VMEM, VMEM], [], 1, 4
+    )(first, first_other)
+    slab = jax.ShapeDtypeStruct((width // 2, LANES), jnp.float32)
+    slabs_held = pltpu.VMEM((4, width // 2, LANES), jnp.float32)
+    pieces = called(functools.partial(gram_kernel, width), (slab,) * 4, [VMEM] * 4, [slabs_held], 1, 4)(
+        gram, cross, second, second_other
+    )
+    mine = summed_over(pieces, "brick")
     theirs = [passed_along(piece, "state", 1) for piece in mine]
-    slabs_held = pltpu.VMEM((4, width // 2, LANES), jnp.float32)
     (root,) = called(
         functools.partial(root_kernel, width),
         (jax.ShapeDtypeStruct((width, 2 * width), jnp.bfloat16),),
-        [SMEM] + [VMEM] * 8,
+        [VMEM] * 8,
         [slabs_held, slabs_held],
         6,
-        20,
-    )(jnp.stack([digit, place]).astype(jnp.int32), *mine, *theirs)
-    block = owned // chunks
-    columns = pl.BlockSpec((width, block), lambda i: (0, i))
+        10,
+    )(*mine, *theirs)
+    pieces = 3 if owned // 2 % (3 * LANES) == 0 else 1
     return called(
-        functools.partial(rotate_kernel, width),
+        functools.partial(rotate_kernel, width, pieces),
         jax.ShapeDtypeStruct((width, owned), jnp.float32),
-        [pl.BlockSpec((width, 2 * width), lambda i: (0, 0)), columns, columns],
-        [],
+        [VMEM] * 5,
+        [pltpu.VMEM((2, width, owned // 2 // pieces), jnp.float32), pltpu.SemaphoreType.DMA((2,))],
         3,
-        16,
-        out_specs=columns,
-        grid=(chunks,),
-    )(root, filtered, other)
+        6,
+        out_specs=HBM,
+    )(root, first, first_other, second, second_other)
 
 
 def solution(mesh):

time: 173 us -> 148 us (0.86)
  local copies, waits for them, and re-layouts: 16.7 us -> 3.23 us
  waiting for transfers between devices: 24.2 us -> 15.2 us
  starting transfers between devices: 21.6 us -> 26.9 us
  Pallas kernels: 107 us -> 102 us
  other arithmetic: 1.84 us -> 0.03 us
    unnamed x32 -> x10, local copies, waits for them, and re-layouts: 16.6 us -> 2.45 us
    ppermute x9 -> x12, waiting for transfers between devices: 14.1 us -> 2.96 us  [passed_along(): return lax.ppermute(value, axis, pairs)]
    pallas_call x9 -> x11, Pallas kernels: 61.7 us -> 53.7 us  [the longest x2 24 us: own(): called(functools.partial(own_kernel, sizes, again), (own_values, partial)...]
    ppermute x9, starting transfers between devices: 9.55 us -> 13.4 us  [exchanged(): lax.ppermute(give(step), axis, [(i, partner(i, step)) for i in range(coun...]
    pallas_call x2, Pallas kernels: 31.5 us -> 34.8 us  [scattered(): called(functools.partial(scatter_kernel, sizes, slots, width, again), (wi...]
    ppermute x9, waiting for transfers between devices: 10.2 us -> 12.2 us  [exchanged(): lax.ppermute(give(step), axis, [(i, partner(i, step)) for i in range(coun...]
    ppermute x9 -> x12, starting transfers between devices: 12 us -> 13.5 us  [passed_along(): return lax.ppermute(value, axis, pairs)]
  transfers between devices with their start and end apart: 18 -> 21, of which waited for: 12 -> 12; matrix products, arithmetic and copies ran while one was open for 1% -> 0% of each run, Pallas kernels for 36% -> 42%
where the time goes in v3:
time: 148 us
  Pallas kernels  102 us (69%)
  starting transfers between devices  26.9 us (18%)
  waiting for transfers between devices  15.2 us (10%)
  local copies, waits for them, and re-layouts  3.23 us (2%)
    pallas_call x2, Pallas kernels, scattered(): called(functools.partial(scatter_kernel, sizes, slots, width, again), (wi...  34.8 us
    pallas_call x2, Pallas kernels, own(): called(functools.partial(own_kernel, sizes, again), (own_values, partial)...  24 us
    ppermute x12, starting transfers between devices, passed_along(): return lax.ppermute(value, axis, pairs)  13.5 us
    ppermute x9, starting transfers between devices, exchanged(): lax.ppermute(give(step), axis, [(i, partner(i, step)) for i in range(coun...  13.4 us
    pallas_call x2, Pallas kernels, shared(): called(functools.partial(shared_kernel, sizes, slots, width, again), (sen...  13.1 us
    ppermute x9, waiting for transfers between devices, exchanged(): lax.ppermute(give(step), axis, [(i, partner(i, step)) for i in range(coun...  12.2 us
    pallas_call x1, Pallas kernels, local(): called(functools.partial(root_kernel, width), (jax.ShapeDtypeStruct((widt...  7.16 us
    pallas_call x1, Pallas kernels, local(): called(functools.partial(prepare_kernel, width, chunks), (wide, sent), [S...  5.15 us
  transfers between devices with their start and end apart: 21, of which 12 were waited for; matrix products, arithmetic and copies ran while one was open for 0% of the time, Pallas kernels for 42%

profile of v3, /device:TPU:0, one launch (start us, length us, event | category | flops | bytes accessed | tf_op | source)
XLA Modules:
  0.0 147.5 jit_solution(9519888572214359860)
XLA Ops:
  0.0 0.8 broadcast_in_dim.3.potential
  0.8 0.0 copy-start
  0.8 0.7 copy-done
  1.5 1.7 %copy-done.2 = bf16[192,6912]{1,0:T(8,128)(2,1)S(1)} copy-done((bf16[192,6912]{1,0:T(8,128)(2,1)S(1)}, bf16[192,6912]{1,0:T(8,128)(2,1)}, u32[]{:S(2)}) %copy-start.2) | copy-done | bytes 2654232
  3.2 5.2 %shard_map.56 = (f32[13824,128]{1,0:T(8,128)S(1)}, bf16[1728,128]{1,0:T(8,128)(2,1)S(1)}) custom-call(s32[1152]{0:T(1024)S(1)} %copy-done, f32[1,6912]{1,0:T(1,128)S(1)} %broadcast_in_dim.3.potential, bf16[192,6912]{1,0:T(8,128)(2,1)S(1)} %copy-done.2), custom_call_target="tpu_custom_call" | custom-call | flops 2400000000 | bytes 18000000 | tf_op jit(solution)/shard_map/pallas_call | solution.py:711
  8.4 7.0 %collective-permute-start = (bf16[1728,128]{1,0:T(8,128)(2,1)S(1)}, bf16[1728,128]{1,0:T(8,128)(2,1)S(1)}, u32[]{:S(2)}, u32[]{:S(2)}) collective-permute-start(bf16[1728,128]{1,0:T(8,128)(2,1)S(1)} %get-tuple-element.35), channel_id=1, source_target_pairs={{0,30},{2,0},{4,2},{6,4},{8,6},{10,8},{12,10},{14,12},{16,14},{18,... | collective-permute-start | bytes 1327112 | tf_op jit(solution)/shard_map/ppermute | solution.py:41
  15.4 0.0 copy-done.4
  15.4 0.7 shard_map.55
  16.1 12.0 %shard_map.57 = (bf16[9728,256]{1,0:T(8,128)(2,1)S(1)}, f32[2048,256]{1,0:T(8,128)S(1)}) custom-call(s32[1]{0:T(128)} %get-tuple-element.29.regular, s32[12288]{0:T(1024)S(1)} %bitcast.2, f32[13824,128]{1,0:T(8,128)S(1)} %get-tuple-element.32.nodes.rest_0_, bf16[368,368]{1,0:T(8,128)(2,1)S(1)} %get-tuple-element.31.matrix), custom_call_target="tpu_custom_call" | custom-call | flops 4400000000 | bytes 33000000 | tf_op jit(solution)/shard_map/pallas_call | solution.py:750
  28.2 0.0 collective-permute-done.arrived
  28.2 6.6 %shard_map.58 = (s16[1728,128]{1,0:T(8,128)(2,1)S(1)}, bf16[144,128]{1,0:T(8,128)(2,1)S(1)}, bf16[2048,256]{1,0:T(8,128)(2,1)S(1)}) custom-call(s32[1]{0:T(128)} %get-tuple-element.29.regular, s32[12288]{0:T(1024)S(1)} %bitcast.3, s32[4096]{0:T(1024)S(1)} %bitcast.8, bf16[1728,128]{1,0:T(8,128)(2,1)S(1)} %collective-permute-done.arrived, ...), custom_call_target="tpu_custom_call" | custom-call | flops 2400000000 | bytes 18000000 | tf_op jit(solution)/shard_map/pallas_call | solution.py:739
  34.8 0.1 collective-permute-start.2
  34.8 0.1 collective-permute-start.1
  34.9 0.0 copy-start.1
  34.9 17.1 %shard_map.59.total_in = f32[13824,128]{1,0:T(8,128)S(1)} custom-call(s32[1]{0:T(128)} %get-tuple-element.29.regular, s32[12288]{0:T(1024)S(1)} %bitcast.4, bf16[368,368]{1,0:T(8,128)(2,1)S(1)} %get-tuple-element.31.matrix, bf16[9728,256]{1,0:T(8,128)(2,1)S(1)} %get-tuple-element.33.own_values, bf16[2048,256]{1,0:T(8,128)(2,1)S(1)} %get-tuple-element.37.late_values, ...), custom_call_target="tpu_custom_call" | custom-call | flops 7200000000 | bytes 54000000 | tf_op jit(solution)/shard_map/pallas_call | solution.py:760
  52.0 0.0 collective-permute-done.2.tops
  52.0 0.0 collective-permute-done.1.returned
  52.0 4.5 %shard_map.60 = (f32[13824,128]{1,0:T(8,128)S(1)}, bf16[1728,128]{1,0:T(8,128)(2,1)S(1)}) custom-call(s32[1152]{0:T(1024)S(1)} %copy-done.1, f32[13824,128]{1,0:T(8,128)S(1)} %shard_map.59.total_in, s16[1728,128]{1,0:T(8,128)(2,1)S(1)} %collective-permute-done.1.returned, ...), custom_call_target="tpu_custom_call", output_to_operand_aliasing={{0}: (1, {})} | custom-call | flops 1200000000 | bytes 9000000 | tf_op jit(solution)/shard_map/pallas_call | solution.py:777
  56.5 5.7 %collective-permute-start.3 = (bf16[1728,128]{1,0:T(8,128)(2,1)S(1)}, bf16[1728,128]{1,0:T(8,128)(2,1)S(1)}, u32[]{:S(2)}, u32[]{:S(2)}) collective-permute-start(bf16[1728,128]{1,0:T(8,128)(2,1)S(1)} %get-tuple-element.42), channel_id=1, source_target_pairs={{0,30},{2,0},{4,2},{6,4},{8,6},{10,8},{12,10},{14,12},{16,14},{18,... | collective-permute-start | bytes 1327112 | tf_op jit(solution)/shard_map/ppermute | solution.py:41
  62.2 12.0 %shard_map.61 = (bf16[9728,256]{1,0:T(8,128)(2,1)S(1)}, f32[2048,256]{1,0:T(8,128)S(1)}) custom-call(s32[1]{0:T(128)} %get-tuple-element.29.regular, s32[12288]{0:T(1024)S(1)} %bitcast.5, f32[13824,128]{1,0:T(8,128)S(1)} %get-tuple-element.40.nodes, bf16[368,368]{1,0:T(8,128)(2,1)S(1)} %get-tuple-element.31.matrix), custom_call_target="tpu_custom_call" | custom-call | flops 4400000000 | bytes 33000000 | tf_op jit(solution)/shard_map/pallas_call | solution.py:750
  74.1 0.0 collective-permute-done.3.arrived
  74.1 6.6 %shard_map.62 = (s16[1728,128]{1,0:T(8,128)(2,1)S(1)}, bf16[144,128]{1,0:T(8,128)(2,1)S(1)}, bf16[2048,256]{1,0:T(8,128)(2,1)S(1)}) custom-call(s32[1]{0:T(128)} %get-tuple-element.29.regular, s32[12288]{0:T(1024)S(1)} %bitcast.6, s32[4096]{0:T(1024)S(1)} %bitcast.9, bf16[1728,128]{1,0:T(8,128)(2,1)S(1)} %collective-permute-done.3.arrived, ...), custom_call_target="tpu_custom_call" | custom-call | flops 2400000000 | bytes 18000000 | tf_op jit(solution)/shard_map/pallas_call | solution.py:739
  80.7 0.1 collective-permute-start.5
  80.8 0.1 collective-permute-start.4
  80.8 17.8 %shard_map.63.total_in = f32[13824,128]{1,0:T(8,128)S(1)} custom-call(s32[1]{0:T(128)} %get-tuple-element.29.regular, s32[12288]{0:T(1024)S(1)} %bitcast.7, bf16[368,368]{1,0:T(8,128)(2,1)S(1)} %get-tuple-element.31.matrix, bf16[9728,256]{1,0:T(8,128)(2,1)S(1)} %get-tuple-element.41.own_values, bf16[2048,256]{1,0:T(8,128)(2,1)S(1)} %get-tuple-element.44.late_values, ...), custom_call_target="tpu_custom_call" | custom-call | flops 7200000000 | bytes 54000000 | tf_op jit(solution)/shard_map/pallas_call | solution.py:760
  98.6 0.0 collective-permute-done.5.tops
  98.6 0.0 collective-permute-done.4.returned
  98.6 4.2 %shard_map.64 = (f32[13824,128]{1,0:T(8,128)S(1)}, bf16[192,3456]{1,0:T(8,128)(2,1)S(1)}) custom-call(s32[1152]{0:T(1024)S(1)} %copy-done.1, f32[13824,128]{1,0:T(8,128)S(1)} %shard_map.63.total_in, s16[1728,128]{1,0:T(8,128)(2,1)S(1)} %collective-permute-done.4.returned, ...), custom_call_target="tpu_custom_call", output_to_operand_aliasing={{0}: (1, {})} | custom-call | flops 2000000000 | bytes 15000000 | tf_op jit(solution)/shard_map/pallas_call | solution.py:788
  102.8 0.1 collective-permute-start.6
  102.9 1.2 shard_map.65.second.own
  104.1 0.6 collective-permute-start.7
  104.6 0.9 shard_map.66.gram
  105.5 0.4 collective-permute-done.6.other.first_other
  105.9 0.6 shard_map.67.begun
  106.5 1.3 collective-permute-done.7.other.second_other
  107.8 0.7 shard_map.68
  108.5 0.1 collective-permute-start.8
  108.6 0.1 collective-permute-start.9
  108.7 2.8 %collective-permute-start.10 = (f32[96,128]{1,0:T(8,128)S(1)}, f32[96,128]{1,0:T(8,128)S(1)}, u32[]{:S(2)}, u32[]{:S(2)}) collective-permute-start(f32[96,128]{1,0:T(8,128)S(1)} %get-tuple-element.52), channel_id=1, source_target_pairs={{0,6},{2,0},{4,2},{6,4},{8,14},{10,8},{12,10},{14,12},{16,22},{18,... | collective-permute-start | bytes 147464 | tf_op jit(solution)/shard_map/ppermute | solution.py:593
  111.5 2.3 %collective-permute-done.8 = f32[96,128]{1,0:T(8,128)S(1)} collective-permute-done((f32[96,128]{1,0:T(8,128)S(1)}, f32[96,128]{1,0:T(8,128)S(1)}, u32[]{:S(2)}, u32[]{:S(2)}) %collective-permute-start.8) | collective-permute-done | bytes 49184 | tf_op jit(solution)/shard_map/ppermute | solution.py:593
  113.8 0.0 collective-permute-done.9
  113.8 0.3 collective-permute-done.10
  114.1 5.8 %collective-permute-start.13 = (f32[96,128]{1,0:T(8,128)S(1)}, f32[96,128]{1,0:T(8,128)S(1)}, u32[]{:S(2)}, u32[]{:S(2)}) collective-permute-start(f32[96,128]{1,0:T(8,128)S(1)} %add_add_fusion.1), channel_id=1, source_target_pairs={{0,24},{2,26},{4,28},{6,30},{8,0},{10,2},{12,4},{14,6},{16,8},{18,... | collective-permute-start | bytes 147464 | tf_op jit(solution)/shard_map/ppermute | solution.py:593
  120.0 0.0 collective-permute-start.12
  120.0 0.6 collective-permute-start.11
  120.6 1.1 collective-permute-done.13
  121.7 3.2 %collective-permute-done.12 = f32[96,128]{1,0:T(8,128)S(1)} collective-permute-done((f32[96,128]{1,0:T(8,128)S(1)}, f32[96,128]{1,0:T(8,128)S(1)}, u32[]{:S(2)}, u32[]{:S(2)}) %collective-permute-start.12) | collective-permute-done | bytes 49184 | tf_op jit(solution)/shard_map/ppermute | solution.py:593
  125.0 0.9 collective-permute-done.11
  125.9 3.3 %collective-permute-start.16 = (f32[96,128]{1,0:T(8,128)S(1)}, f32[96,128]{1,0:T(8,128)S(1)}, u32[]{:S(2)}, u32[]{:S(2)}) collective-permute-start(f32[96,128]{1,0:T(8,128)S(1)} %add_add_fusion.refs_0_), channel_id=1, source_target_pairs={{0,6},{2,0},{4,2},{6,4},{8,14},{10,8},{12,10},{14,12},{16,22},{18,... | collective-permute-start | bytes 147464 | tf_op jit(solution)/shard_map/ppermute | solution.py:593
  129.2 0.0 collective-permute-start.15
  129.2 0.6 collective-permute-start.14
  129.8 0.0 collective-permute-start.17
  129.8 1.1 collective-permute-done.16.refs_3_
  130.9 0.0 collective-permute-start.20
  130.9 2.3 %collective-permute-done.15.refs_2_ = f32[96,128]{1,0:T(8,128)S(1)} collective-permute-done((f32[96,128]{1,0:T(8,128)S(1)}, f32[96,128]{1,0:T(8,128)S(1)}, u32[]{:S(2)}, u32[]{:S(2)}) %collective-permute-start.15) | collective-permute-done | bytes 49184 | tf_op jit(solution)/shard_map/ppermute | solution.py:593
  133.3 0.0 collective-permute-start.19
  133.3 0.9 collective-permute-done.14.refs_1_
  134.2 0.0 collective-permute-start.18
  134.2 0.0 collective-permute-done.17.refs_4_
  134.2 0.0 collective-permute-done.20.refs_7_
  134.2 0.3 collective-permute-done.19.refs_6_
  134.5 0.9 collective-permute-done.18.refs_5_
  135.4 7.2 %shard_map.69.root = bf16[192,384]{1,0:T(8,128)(2,1)S(1)} custom-call(f32[96,128]{1,0:T(8,128)S(1)} %add_add_fusion.refs_0_, f32[96,128]{1,0:T(8,128)S(1)} %collective-permute-done.14.refs_1_, f32[96,128]{1,0:T(8,128)S(1)} %collective-permute-done.15.refs_2_, f32[96,128]{1,0:T(8,128)S(1)} %collective-permute-done.16.refs_3_, ...), custom_call_target="tpu_custom_call" | custom-call | flops 2400000000 | bytes 18000000 | tf_op jit(solution)/shard_map/pallas_call | solution.py:814
  142.6 4.8 %shard_map.70 = f32[192,6912]{1,0:T(8,128)} custom-call(bf16[192,384]{1,0:T(8,128)(2,1)S(1)} %shard_map.69.root, bf16[192,3456]{1,0:T(8,128)(2,1)S(1)} %get-tuple-element.47.first.own, bf16[192,3456]{1,0:T(8,128)(2,1)S(1)} %collective-permute-done.6.other.first_other, bf16[192,3456]{1,0:T(8,128)(2,1)S(1)} %shard_map.65.second.own, ...), custom_call_target="tpu_custom_call" | custom-call | flops 1200000000 | bytes 9000000 | tf_op jit(solution)/shard_map/pallas_call | solution.py:823
  (7 shorter events, 0.0 us)
Async XLA Ops:
  0.0 15.4 %copy-start.4 = (s32[32,343]{1,0:T(8,128)S(1)}, s32[32,343]{1,0:T(8,128)}, u32[]{:S(2)}) copy-start(s32[32,343]{1,0:T(8,128)} %cell_nodes.1) | copy-start | bytes 131716
  0.8 0.7 copy-start
  1.5 1.7 %copy-start.2 = (bf16[192,6912]{1,0:T(8,128)(2,1)S(1)}, bf16[192,6912]{1,0:T(8,128)(2,1)}, u32[]{:S(2)}) copy-start(bf16[192,6912]{1,0:T(8,128)(2,1)} %states.1) | copy-start | bytes 7962628
  3.2 12.2 %copy-start.3 = (bf16[343,343]{1,0:T(8,128)(2,1)S(1)}, bf16[343,343]{1,0:T(8,128)(2,1)}, u32[]{:S(2)}) copy-start(bf16[343,343]{1,0:T(8,128)(2,1)} %kinetic.1) | copy-start | bytes 705898
  8.4 19.8 %collective-permute-start = (bf16[1728,128]{1,0:T(8,128)(2,1)S(1)}, bf16[1728,128]{1,0:T(8,128)(2,1)S(1)}, u32[]{:S(2)}, u32[]{:S(2)}) collective-permute-start(bf16[1728,128]{1,0:T(8,128)(2,1)S(1)} %get-tuple-element.35), channel_id=1, source_target_pairs={{0,30},{2,0},{4,2},{6,4},{8,6},{10,8},{12,10},{14,12},{16,14},{18,... | collective-permute-start | bytes 1327112 | tf_op jit(solution)/shard_map/ppermute | solution.py:41
  34.8 17.2 %collective-permute-start.2 = (bf16[144,128]{1,0:T(8,128)(2,1)S(1)}, bf16[144,128]{1,0:T(8,128)(2,1)S(1)}, u32[]{:S(2)}, u32[]{:S(2)}) collective-permute-start(bf16[144,128]{1,0:T(8,128)(2,1)S(1)} %get-tuple-element.39), channel_id=1, source_target_pairs={{0,2},{2,4},{4,6},{6,8},{8,10},{10,12},{12,14},{14,16},{16,18},{18... | collective-permute-start | bytes 110600 | tf_op jit(solution)/shard_map/ppermute | solution.py:41
  34.8 17.2 %collective-permute-start.1 = (s16[1728,128]{1,0:T(8,128)(2,1)S(1)}, s16[1728,128]{1,0:T(8,128)(2,1)S(1)}, u32[]{:S(2)}, u32[]{:S(2)}) collective-permute-start(s16[1728,128]{1,0:T(8,128)(2,1)S(1)} %get-tuple-element.38), channel_id=1, source_target_pairs={{0,2},{2,4},{4,6},{6,8},{8,10},{10,12},{12,14},{14,16},{16,18},{18... | collective-permute-start | bytes 1327112 | tf_op jit(solution)/shard_map/ppermute | solution.py:41
  34.9 17.1 %copy-start.1 = (s32[1152]{0:T(1024)S(1)}, s32[1152]{0:T(1024)}, u32[]{:S(2)}) copy-start(s32[1152]{0:T(1024)} %face.5) | copy-start | bytes 13828
  56.5 17.6 %collective-permute-start.3 = (bf16[1728,128]{1,0:T(8,128)(2,1)S(1)}, bf16[1728,128]{1,0:T(8,128)(2,1)S(1)}, u32[]{:S(2)}, u32[]{:S(2)}) collective-permute-start(bf16[1728,128]{1,0:T(8,128)(2,1)S(1)} %get-tuple-element.42), channel_id=1, source_target_pairs={{0,30},{2,0},{4,2},{6,4},{8,6},{10,8},{12,10},{14,12},{16,14},{18,... | collective-permute-start | bytes 1327112 | tf_op jit(solution)/shard_map/ppermute | solution.py:41
  80.7 17.9 %collective-permute-start.5 = (bf16[144,128]{1,0:T(8,128)(2,1)S(1)}, bf16[144,128]{1,0:T(8,128)(2,1)S(1)}, u32[]{:S(2)}, u32[]{:S(2)}) collective-permute-start(bf16[144,128]{1,0:T(8,128)(2,1)S(1)} %get-tuple-element.46), channel_id=1, source_target_pairs={{0,2},{2,4},{4,6},{6,8},{8,10},{10,12},{12,14},{14,16},{16,18},{18... | collective-permute-start | bytes 110600 | tf_op jit(solution)/shard_map/ppermute | solution.py:41
  80.8 17.9 %collective-permute-start.4 = (s16[1728,128]{1,0:T(8,128)(2,1)S(1)}, s16[1728,128]{1,0:T(8,128)(2,1)S(1)}, u32[]{:S(2)}, u32[]{:S(2)}) collective-permute-start(s16[1728,128]{1,0:T(8,128)(2,1)S(1)} %get-tuple-element.45), channel_id=1, source_target_pairs={{0,2},{2,4},{4,6},{6,8},{8,10},{10,12},{12,14},{14,16},{16,18},{18... | collective-permute-start | bytes 1327112 | tf_op jit(solution)/shard_map/ppermute | solution.py:41
  102.8 3.1 %collective-permute-start.6 = (bf16[192,3456]{1,0:T(8,128)(2,1)S(1)}, bf16[192,3456]{1,0:T(8,128)(2,1)S(1)}, u32[]{:S(2)}, u32[]{:S(2)}) collective-permute-start(bf16[192,3456]{1,0:T(8,128)(2,1)S(1)} %get-tuple-element.47.first.own), channel_id=1, source_target_pairs={{0,1},{1,0},{2,3},{3,2},{4,5},{5,4},{6,7},{7,6},{8,9},{9,8},{10,11... | collective-permute-start | bytes 3981320 | tf_op jit(solution)/shard_map/ppermute | solution.py:41
  104.1 3.8 %collective-permute-start.7 = (bf16[192,3456]{1,0:T(8,128)(2,1)S(1)}, bf16[192,3456]{1,0:T(8,128)(2,1)S(1)}, u32[]{:S(2)}, u32[]{:S(2)}) collective-permute-start(bf16[192,3456]{1,0:T(8,128)(2,1)S(1)} %shard_map.65.second.own), channel_id=1, source_target_pairs={{0,1},{1,0},{2,3},{3,2},{4,5},{5,4},{6,7},{7,6},{8,9},{9,8},{10,11... | collective-permute-start | bytes 3981320 | tf_op jit(solution)/shard_map/ppermute | solution.py:41
  108.5 5.3 %collective-permute-start.8 = (f32[96,128]{1,0:T(8,128)S(1)}, f32[96,128]{1,0:T(8,128)S(1)}, u32[]{:S(2)}, u32[]{:S(2)}) collective-permute-start(f32[96,128]{1,0:T(8,128)S(1)} %get-tuple-element.50), channel_id=1, source_target_pairs={{0,2},{2,4},{4,6},{6,0},{8,10},{10,12},{12,14},{14,8},{16,18},{18,... | collective-permute-start | bytes 147464 | tf_op jit(solution)/shard_map/ppermute | solution.py:593
  108.6 5.2 %collective-permute-start.9 = (f32[96,128]{1,0:T(8,128)S(1)}, f32[96,128]{1,0:T(8,128)S(1)}, u32[]{:S(2)}, u32[]{:S(2)}) collective-permute-start(f32[96,128]{1,0:T(8,128)S(1)} %get-tuple-element.51), channel_id=1, source_target_pairs={{0,4},{2,6},{4,0},{6,2},{8,12},{10,14},{12,8},{14,10},{16,20},{18,... | collective-permute-start | bytes 147464 | tf_op jit(solution)/shard_map/ppermute | solution.py:593
  108.7 5.5 %collective-permute-start.10 = (f32[96,128]{1,0:T(8,128)S(1)}, f32[96,128]{1,0:T(8,128)S(1)}, u32[]{:S(2)}, u32[]{:S(2)}) collective-permute-start(f32[96,128]{1,0:T(8,128)S(1)} %get-tuple-element.52), channel_id=1, source_target_pairs={{0,6},{2,0},{4,2},{6,4},{8,14},{10,8},{12,10},{14,12},{16,22},{18,... | collective-permute-start | bytes 147464 | tf_op jit(solution)/shard_map/ppermute | solution.py:593
  114.1 7.6 %collective-permute-start.13 = (f32[96,128]{1,0:T(8,128)S(1)}, f32[96,128]{1,0:T(8,128)S(1)}, u32[]{:S(2)}, u32[]{:S(2)}) collective-permute-start(f32[96,128]{1,0:T(8,128)S(1)} %add_add_fusion.1), channel_id=1, source_target_pairs={{0,24},{2,26},{4,28},{6,30},{8,0},{10,2},{12,4},{14,6},{16,8},{18,... | collective-permute-start | bytes 147464 | tf_op jit(solution)/shard_map/ppermute | solution.py:593
  120.0 5.0 %collective-permute-start.12 = (f32[96,128]{1,0:T(8,128)S(1)}, f32[96,128]{1,0:T(8,128)S(1)}, u32[]{:S(2)}, u32[]{:S(2)}) collective-permute-start(f32[96,128]{1,0:T(8,128)S(1)} %add_add_fusion.1), channel_id=1, source_target_pairs={{0,16},{2,18},{4,20},{6,22},{8,24},{10,26},{12,28},{14,30},{16,0},... | collective-permute-start | bytes 147464 | tf_op jit(solution)/shard_map/ppermute | solution.py:593
  120.0 5.9 %collective-permute-start.11 = (f32[96,128]{1,0:T(8,128)S(1)}, f32[96,128]{1,0:T(8,128)S(1)}, u32[]{:S(2)}, u32[]{:S(2)}) collective-permute-start(f32[96,128]{1,0:T(8,128)S(1)} %add_add_fusion.1), channel_id=1, source_target_pairs={{0,8},{2,10},{4,12},{6,14},{8,16},{10,18},{12,20},{14,22},{16,24},... | collective-permute-start | bytes 147464 | tf_op jit(solution)/shard_map/ppermute | solution.py:593
  125.9 5.0 %collective-permute-start.16 = (f32[96,128]{1,0:T(8,128)S(1)}, f32[96,128]{1,0:T(8,128)S(1)}, u32[]{:S(2)}, u32[]{:S(2)}) collective-permute-start(f32[96,128]{1,0:T(8,128)S(1)} %add_add_fusion.refs_0_), channel_id=1, source_target_pairs={{0,6},{2,0},{4,2},{6,4},{8,14},{10,8},{12,10},{14,12},{16,22},{18,... | collective-permute-start | bytes 147464 | tf_op jit(solution)/shard_map/ppermute | solution.py:593
  129.2 4.1 %collective-permute-start.15 = (f32[96,128]{1,0:T(8,128)S(1)}, f32[96,128]{1,0:T(8,128)S(1)}, u32[]{:S(2)}, u32[]{:S(2)}) collective-permute-start(f32[96,128]{1,0:T(8,128)S(1)} %add_add_fusion.refs_0_), channel_id=1, source_target_pairs={{0,4},{2,6},{4,0},{6,2},{8,12},{10,14},{12,8},{14,10},{16,20},{18,... | collective-permute-start | bytes 147464 | tf_op jit(solution)/shard_map/ppermute | solution.py:593
  129.2 5.0 %collective-permute-start.14 = (f32[96,128]{1,0:T(8,128)S(1)}, f32[96,128]{1,0:T(8,128)S(1)}, u32[]{:S(2)}, u32[]{:S(2)}) collective-permute-start(f32[96,128]{1,0:T(8,128)S(1)} %add_add_fusion.refs_0_), channel_id=1, source_target_pairs={{0,2},{2,4},{4,6},{6,0},{8,10},{10,12},{12,14},{14,8},{16,18},{18,... | collective-permute-start | bytes 147464 | tf_op jit(solution)/shard_map/ppermute | solution.py:593
  129.8 4.4 %collective-permute-start.17 = (f32[96,128]{1,0:T(8,128)S(1)}, f32[96,128]{1,0:T(8,128)S(1)}, u32[]{:S(2)}, u32[]{:S(2)}) collective-permute-start(f32[96,128]{1,0:T(8,128)S(1)} %add_add_fusion.refs_0_), channel_id=1, source_target_pairs={{0,1},{1,0},{2,3},{3,2},{4,5},{5,4},{6,7},{7,6},{8,9},{9,8},{10,11... | collective-permute-start | bytes 147464 | tf_op jit(solution)/shard_map/ppermute | solution.py:41
  130.9 3.2 %collective-permute-start.20 = (f32[96,128]{1,0:T(8,128)S(1)}, f32[96,128]{1,0:T(8,128)S(1)}, u32[]{:S(2)}, u32[]{:S(2)}) collective-permute-start(f32[96,128]{1,0:T(8,128)S(1)} %collective-permute-done.16.refs_3_), channel_id=1, source_target_pairs={{0,1},{1,0},{2,3},{3,2},{4,5},{5,4},{6,7},{7,6},{8,9},{9,8},{10,11... | collective-permute-start | bytes 147464 | tf_op jit(solution)/shard_map/ppermute | solution.py:41
  133.3 1.2 collective-permute-start.19
  134.2 1.2 collective-permute-start.18

commit v4 on v3

--- a/solution.py
+++ b/solution.py
@@ -114,6 +114,14 @@
     def body(base, size):
         for j in range(size):
             target[pair(2 * (base + j)), :] = source[pair(2 * face[base + j]), :]
+
+    some_rows(face.shape[0], 64, body)
+
+
+def store_face(face, source, target):
+    def body(base, size):
+        for j in range(size):
+            target[pair(2 * face[base + j]), :] = source[pair(2 * (base + j)), :]
 
     some_rows(face.shape[0], 64, body)
 
@@ -187,7 +195,7 @@
     matrix[...] = wide.astype(jnp.bfloat16)
     slot = lax.broadcasted_iota(jnp.int32, nodes.shape, 1)
     odd = jnp.where((nodes >= owned) == (slot >= early), 0, 1)
-    regular[0] = jnp.where((jnp.max(odd) == 0) & (cells % 4 == 0), 1, 0)
+    regular[0] = jnp.where((jnp.max(odd) == 0) & (cells % 8 == 0), 1, 0)
 
 
 def prepare_kernel(width, chunks, face, potential, states, nodes, send, picked, held, sems):
@@ -206,7 +214,10 @@
         def one(i, _):
             first = pl.multiple_of(k * piece + i * block, block)
             at = pl.ds(first, block)
-            local = potential[:, at] - cheb_center
+            rows = block // LANES
+            local = jnp.concatenate(
+                [potential[pl.ds(first // LANES + k, 1), :] for k in range(rows)], axis=1
+            ) - cheb_center
             parts = split3(local)
             row = lax.broadcasted_iota(jnp.int32, (2 * LANES - width, block), 0)
             tail = jnp.zeros(row.shape, jnp.float32)
@@ -226,44 +237,59 @@
     send[count:, :] = high.astype(jnp.bfloat16)
 
 
-def gather_own(sizes, again, table, nodes, matrix, values_out, partial, buffers):
+def gather_own(sizes, again, table_in, nodes, matrix, values_out, partial, table, sems, buffers):
     cells, early, early_rows, late_rows, stride = sizes
+    group = len(buffers) // 2
+    steps = cells // (2 * group)
+    words = 2 * group * stride
+
+    def part_of(step):
+        at = pl.ds(pl.multiple_of(step * words, words), words)
+        return pltpu.make_async_copy(table_in.at[at], table.at[at], sems.at[step])
+
+    for step in range(steps):
+        part_of(step).start()
     for buffer in buffers:
-        buffer[...] = jnp.zeros(buffer.shape, jnp.float32)
-
-    def fetch(cell, buffer):
-        mine = table.at[pl.ds(cell * stride, stride)]
+        buffer[pl.ds(2 * early, 2 * (early_rows - early)), :] = jnp.zeros((2 * (early_rows - early), LANES), jnp.float32)
+
+    def fetch(cell, some):
+        lists = [table.at[pl.ds((cell + k) * stride, stride)] for k in range(group)]
         for a in range(early):
-            buffer[pl.ds(2 * a, 2), :] = nodes[pair(mine[a]), :]
-
-    def finish(cell, buffer):
-        low = buffer[pl.ds(0, early_rows, 2), :]
-        high = buffer[pl.ds(1, early_rows, 2), :]
-        values = once_rounded(jnp.concatenate([low, high], axis=1), again)
-        values_out[pl.ds(pl.multiple_of(cell * early_rows, early_rows), early_rows), :] = values
-        partial[pl.ds(pl.multiple_of(cell * late_rows, late_rows), late_rows), :] = jnp.dot(
-            matrix[early_rows:, :early_rows], values, preferred_element_type=jnp.float32
-        )
-
-    def two(i, _):
-        fetch(2 * i, buffers[0])
-        finish(jnp.maximum(2 * i - 1, 0), buffers[1])
-        fetch(2 * i + 1, buffers[1])
-        finish(2 * i, buffers[0])
+            for k in range(group):
+                some[k][pl.ds(2 * a, 2), :] = nodes[pair(lists[k][a]), :]
+
+    def finish(first, some):
+        for k in range(group):
+            cell = first + k
+            low = some[k][pl.ds(0, early_rows, 2), :]
+            high = some[k][pl.ds(1, early_rows, 2), :]
+            values = once_rounded(jnp.concatenate([low, high], axis=1), again)
+            values_out[pl.ds(pl.multiple_of(cell * early_rows, early_rows), early_rows), :] = values
+            partial[pl.ds(pl.multiple_of(cell * late_rows, late_rows), late_rows), :] = jnp.dot(
+                matrix[early_rows:, :early_rows], values, preferred_element_type=jnp.float32
+            )
+
+    def two(step, _):
+        part_of(step).wait()
+        cell = 2 * group * step
+        fetch(cell, buffers[:group])
+        finish(jnp.maximum(cell - group, 0), buffers[group:])
+        fetch(cell + group, buffers[group:])
+        finish(cell, buffers[:group])
         return 0
 
-    lax.fori_loop(0, cells // 2, two, 0)
-    finish(cells - 1, buffers[1])
+    lax.fori_loop(0, steps, two, 0)
+    finish(cells - group, buffers[group:])
 
 
 def once_rounded(summed, again):
     return (summed * (1.0 / cheb_half) if again else summed).astype(jnp.bfloat16)
 
 
-def own_kernel(sizes, again, regular, table, nodes, matrix, values_out, partial, *buffers):
+def own_kernel(sizes, again, regular, table_in, nodes, matrix, values_out, partial, table, sems, *buffers):
     @pl.when(regular[0] == 1)
     def _():
-        gather_own(sizes, again, table, nodes, matrix, values_out, partial, buffers)
+        gather_own(sizes, again, table_in, nodes, matrix, values_out, partial, table, sems, buffers)
 
 
 def any_cell(sizes, again, cell, table, nodes, ghosts, matrix, gathered, products):
@@ -334,17 +360,21 @@
         group = 4
 
         def fetch(i, _):
-            for cell in (2 * i, 2 * i + 1):
-                mine = late_table.at[pl.ds(cell * LANES, LANES)]
-                here = gathered.at[pl.ds(pl.multiple_of(cell * 2 * late_rows, 2 * late_rows), 2 * late_rows)]
-                for a in range(late):
-                    here[pl.ds(2 * a, 2), :] = ghosts[pair(mine[a]), :]
-                here[pl.ds(2 * late, 2 * (late_rows - late)), :] = jnp.zeros(
+            four = [4 * i + k for k in range(4)]
+            lists = [late_table.at[pl.ds(cell * LANES, LANES)] for cell in four]
+            parts = [
+                gathered.at[pl.ds(pl.multiple_of(cell * 2 * late_rows, 2 * late_rows), 2 * late_rows)] for cell in four
+            ]
+            for a in range(late):
+                for k in range(4):
+                    parts[k][pl.ds(2 * a, 2), :] = ghosts[pair(lists[k][a]), :]
+            for k in range(4):
+                parts[k][pl.ds(2 * late, 2 * (late_rows - late)), :] = jnp.zeros(
                     (2 * (late_rows - late), LANES), jnp.float32
                 )
             return 0
 
-        lax.fori_loop(0, cells // 2, fetch, 0)
+        lax.fori_loop(0, cells // 4, fetch, 0)
 
         def multiply(some, _):
             for j in range(group):
@@ -444,13 +474,15 @@
     lax.fori_loop(0, cells // 4, four, 0)
 
 
-def scatter_kernel(sizes, slots, width, again, regular, table, matrix, own_values, late_values, arrived,
+def scatter_kernel(sizes, slots, width, again, regular, table_in, matrix, own_values, late_values, arrived,
                    nodes, *rest):
     if again:
         states, total, other, *rest = rest
     else:
         total, other, *rest = rest
-    *products, ghosts, any_gathered, any_products = rest
+    *products, ghosts, any_gathered, any_products, table, sem = rest
+    copy = pltpu.make_async_copy(table_in, table, sem)
+    copy.start()
     owned = nodes.shape[0] // 2
     block = block_of(owned)
 
@@ -468,6 +500,7 @@
         return 0
 
     lax.fori_loop(0, owned // block, begin, 0, unroll=3)
+    copy.wait()
 
     @pl.when(regular[0] == 1)
     def _():
@@ -506,13 +539,16 @@
 
 def once_kernel(width, face, total_in, returned, tops, total, send, spread):
     count = face.shape[0]
-    add_returned(width, face, returned, tops, total, spread)
     gather_face(face, total, spread)
-    low = once_rounded(spread[pl.ds(0, count, 2), :], True).astype(jnp.float32)
-    high = once_rounded(spread[pl.ds(1, count, 2), :], True).astype(jnp.float32)
-    low, high = pack(low, high, width)
+    low, high = unpack(decoded(returned[...], tops[...]), count, width)
+    low = spread[pl.ds(0, count, 2), :] + low
+    high = spread[pl.ds(1, count, 2), :] + high
+    spread[pl.ds(0, count, 2), :] = low
+    spread[pl.ds(1, count, 2), :] = high
+    low, high = pack(once_rounded(low, True).astype(jnp.float32), once_rounded(high, True).astype(jnp.float32), width)
     send[:count, :] = low.astype(jnp.bfloat16)
     send[count:, :] = high.astype(jnp.bfloat16)
+    store_face(face, spread, total)
 
 
 def filter_half(total, filtered, start, width):
@@ -609,6 +645,19 @@
         piece = functools.reduce(jnp.add, exchanged(axis, stride, some, lambda step: piece), piece)
         stride *= some
     return [piece] + exchanged(axis, 1, radix, lambda step: piece)
+
+
+def split2(wide):
+    first = wide.astype(jnp.bfloat16)
+    return first, (wide - first.astype(jnp.float32)).astype(jnp.bfloat16)
+
+
+def product(left, right):
+    return jnp.dot(
+        jnp.concatenate([left[0], left[0], left[1]], axis=1),
+        jnp.concatenate([right[0], right[1], right[0]], axis=0),
+        preferred_element_type=jnp.float32,
+    )
 
 
 def root_kernel(width, *refs):
@@ -650,17 +699,16 @@
     rows = lax.broadcasted_iota(jnp.int32, (total, total), 0)
     columns = lax.broadcasted_iota(jnp.int32, (total, total), 1)
     triple = jnp.where(rows == columns, 3.0, 0.0)
-    product = functools.partial(jnp.dot, precision=lax.Precision.HIGHEST, preferred_element_type=jnp.float32)
     current = margin / jnp.sqrt(jnp.sum(margin * margin) + epsilon)
     factor = triple - current
-    current = 0.5 * product(factor, current)
-    inverse = 0.5 * factor
+    current, inverse = 0.5 * product(split2(factor), split2(current)), 0.5 * factor
     for iteration in range(1, NS_STEPS - 1):
-        factor = triple - product(inverse, current)
-        current = 0.5 * product(factor, current)
-        inverse = 0.5 * product(factor, inverse)
-    factor = triple[:width] - product(inverse[:width], current)
-    root[...] = (0.5 * product(factor, inverse)).astype(jnp.bfloat16)
+        parts = split2(inverse), split2(current)
+        factor = split2(triple - product(*parts))
+        current, inverse = 0.5 * product(factor, parts[1]), 0.5 * product(factor, parts[0])
+    parts = split2(inverse), split2(current)
+    factor = triple[:width] - product([part[:width] for part in parts[0]], parts[1])
+    root[...] = (0.5 * product(split2(factor), parts[0])).astype(jnp.bfloat16)
 
 
 def rotate_kernel(width, pieces, root, first, first_other, second, second_other, result, held, sems):
@@ -696,7 +744,7 @@
     packed = count + count // (LANES // (width - LANES))
     integers = lambda *shape: jax.ShapeDtypeStruct(shape, jnp.int32)
 
-    lumped = potential[None, :]
+    lumped = potential.reshape(-1, LANES)
     wide = jax.ShapeDtypeStruct((2 * owned, LANES), jnp.float32)
     sent = jax.ShapeDtypeStruct((packed, LANES), jnp.bfloat16)
     own_values = jax.ShapeDtypeStruct((cells * early_rows, 2 * LANES), jnp.bfloat16)
@@ -735,13 +783,15 @@
     sent_short = jax.ShapeDtypeStruct((packed, LANES), jnp.int16)
     tops = jax.ShapeDtypeStruct((packed // group_of(packed), LANES), jnp.bfloat16)
 
+    held_table = pltpu.SMEM((cells * stride,), jnp.int32)
+
     def shared(again, arrived, nodes, partial):
         return called(
             functools.partial(shared_kernel, sizes, slots, width, again),
             (sent_short, tops, late_values),
             [SMEM, VMEM, SMEM, VMEM, VMEM, VMEM, VMEM],
             [spread, spread, spread, pairs_late, pairs_late, pairs_any, pairs_any]
-            + [pltpu.SMEM((cells * stride,), jnp.int32), pltpu.SemaphoreType.DMA],
+            + [held_table, pltpu.SemaphoreType.DMA],
             6,
             11,
         )(regular, table, late_table, arrived, nodes, matrix, partial)
@@ -750,18 +800,19 @@
         return called(
             functools.partial(own_kernel, sizes, again),
             (own_values, partial),
-            [SMEM, SMEM, VMEM, VMEM],
-            [pairs_own, pairs_own],
-            11,
-            3,
+            [SMEM, VMEM, VMEM, VMEM],
+            [held_table, pltpu.SemaphoreType.DMA((-(-cells // 8),))] + [pairs_own] * 8,
+            10,
+            4,
         )(regular, table, nodes, matrix)
 
     def scattered(again, values, late, arrived, nodes, *before):
         return called(
             functools.partial(scatter_kernel, sizes, slots, width, again),
             (wide,),
-            [SMEM, SMEM] + [VMEM] * (5 + len(before)),
-            [pltpu.VMEM((2 * owned, LANES), jnp.float32)] + [pairs_own] * 4 + [spread, pairs_any, pairs_any],
+            [SMEM] + [VMEM] * (6 + len(before)),
+            [pltpu.VMEM((2 * owned, LANES), jnp.float32)] + [pairs_own] * 4 + [spread, pairs_any, pairs_any]
+            + [held_table, pltpu.SemaphoreType.DMA],
             18,
             14,
         )(regular, table, matrix, values, late, arrived, nodes, *before)[0]

time: 148 us -> 137 us (0.926)
  Pallas kernels: 102 us -> 91.1 us
    pallas_call x1, Pallas kernels: 7.16 us -> 3.76 us  [local(): called(functools.partial(root_kernel, width), (jax.ShapeDtypeStruct((widt...]
    pallas_call x2, Pallas kernels: 24 us -> 20.9 us  [own(): called(functools.partial(own_kernel, sizes, again), (own_values, partial)...]
    pallas_call x2, Pallas kernels: 34.8 us -> 32 us  [scattered(): called(functools.partial(scatter_kernel, sizes, slots, width, again), (wi...]
    unnamed x10 -> x12, local copies, waits for them, and re-layouts: 2.45 us -> 3.21 us
  transfers between devices with their start and end apart: 21 -> 21, of which waited for: 12 -> 13; matrix products, arithmetic and copies ran while one was open for 0% -> 0% of each run, Pallas kernels for 42% -> 41%
where the time goes in v4:
time: 137 us
  Pallas kernels  91.1 us (66%)
  starting transfers between devices  27 us (20%)
  waiting for transfers between devices  15.1 us (11%)
  local copies, waits for them, and re-layouts  3.21 us (2%)
    pallas_call x2, Pallas kernels, scattered(): called(functools.partial(scatter_kernel, sizes, slots, width, again), (wi...  32 us
    pallas_call x2, Pallas kernels, own(): called(functools.partial(own_kernel, sizes, again), (own_values, partial)...  20.9 us
    ppermute x9, starting transfers between devices, exchanged(): lax.ppermute(give(step), axis, [(i, partner(i, step)) for i in range(coun...  13.6 us
    ppermute x12, starting transfers between devices, passed_along(): return lax.ppermute(value, axis, pairs)  13.4 us
    pallas_call x2, Pallas kernels, shared(): called(functools.partial(shared_kernel, sizes, slots, width, again), (sen...  12.7 us
    ppermute x9, waiting for transfers between devices, exchanged(): lax.ppermute(give(step), axis, [(i, partner(i, step)) for i in range(coun...  12 us
    pallas_call x1, Pallas kernels, local(): called(functools.partial(prepare_kernel, width, chunks), (wide, sent), [S...  5.16 us
    pallas_call x1, Pallas kernels, local(): called(functools.partial(rotate_kernel, width, pieces), jax.ShapeDtypeStr...  4.79 us
  transfers between devices with their start and end apart: 21, of which 13 were waited for; matrix products, arithmetic and copies ran while one was open for 0% of the time, Pallas kernels for 41%

profile of v4, /device:TPU:0, one launch (start us, length us, event | category | flops | bytes accessed | tf_op | source)
XLA Modules:
  0.0 136.9 jit_solution(15258475861241588491)
XLA Ops:
  0.0 0.7 copy-done
  0.7 1.7 %copy-done.2 = bf16[192,6912]{1,0:T(8,128)(2,1)S(1)} copy-done((bf16[192,6912]{1,0:T(8,128)(2,1)S(1)}, bf16[192,6912]{1,0:T(8,128)(2,1)}, u32[]{:S(2)}) %copy-start.2) | copy-done | bytes 2654232
  2.5 0.7 copy-done.5
  3.2 5.2 %shard_map.56 = (f32[13824,128]{1,0:T(8,128)S(1)}, bf16[1728,128]{1,0:T(8,128)(2,1)S(1)}) custom-call(s32[1152]{0:T(1024)S(1)} %copy-done, f32[54,128]{1,0:T(8,128)S(1)} %bitcast.11, bf16[192,6912]{1,0:T(8,128)(2,1)S(1)} %copy-done.2), custom_call_target="tpu_custom_call" | custom-call | flops 2400000000 | bytes 18000000 | tf_op jit(solution)/shard_map/pallas_call | solution.py:759
  8.4 7.0 %collective-permute-start = (bf16[1728,128]{1,0:T(8,128)(2,1)S(1)}, bf16[1728,128]{1,0:T(8,128)(2,1)S(1)}, u32[]{:S(2)}, u32[]{:S(2)}) collective-permute-start(bf16[1728,128]{1,0:T(8,128)(2,1)S(1)} %get-tuple-element.35), channel_id=1, source_target_pairs={{0,30},{2,0},{4,2},{6,4},{8,6},{10,8},{12,10},{14,12},{16,14},{18,... | collective-permute-start | bytes 1327112 | tf_op jit(solution)/shard_map/ppermute | solution.py:41
  15.4 0.0 copy-done.3
  15.4 0.0 copy-done.4
  15.4 0.7 shard_map.55
  16.1 10.4 %shard_map.57 = (bf16[9728,256]{1,0:T(8,128)(2,1)S(1)}, f32[2048,256]{1,0:T(8,128)S(1)}) custom-call(s32[1]{0:T(128)} %get-tuple-element.29.regular, s32[12288]{0:T(1024)S(1)} %bitcast.3, f32[13824,128]{1,0:T(8,128)S(1)} %get-tuple-element.32.nodes.rest_0_, bf16[368,368]{1,0:T(8,128)(2,1)S(1)} %get-tuple-element.31.matrix), custom_call_target="tpu_custom_call" | custom-call | flops 4000000000 | bytes 30000000 | tf_op jit(solution)/shard_map/pallas_call | solution.py:800
  26.5 0.0 collective-permute-done.arrived
  26.5 6.3 %shard_map.58 = (s16[1728,128]{1,0:T(8,128)(2,1)S(1)}, bf16[144,128]{1,0:T(8,128)(2,1)S(1)}, bf16[2048,256]{1,0:T(8,128)(2,1)S(1)}) custom-call(s32[1]{0:T(128)} %get-tuple-element.29.regular, s32[12288]{0:T(1024)S(1)} %bitcast.4, s32[4096]{0:T(1024)S(1)} %bitcast.9, bf16[1728,128]{1,0:T(8,128)(2,1)S(1)} %collective-permute-done.arrived, ...), custom_call_target="tpu_custom_call" | custom-call | flops 2400000000 | bytes 18000000 | tf_op jit(solution)/shard_map/pallas_call | solution.py:789
  32.8 0.1 collective-permute-start.2
  32.8 0.1 collective-permute-start.1
  32.9 0.0 copy-start.1
  32.9 15.8 %shard_map.59.total_in = f32[13824,128]{1,0:T(8,128)S(1)} custom-call(s32[1]{0:T(128)} %get-tuple-element.29.regular, s32[12288]{0:T(1024)S(1)} %bitcast.5, bf16[368,368]{1,0:T(8,128)(2,1)S(1)} %get-tuple-element.31.matrix, bf16[9728,256]{1,0:T(8,128)(2,1)S(1)} %get-tuple-element.33.own_values, bf16[2048,256]{1,0:T(8,128)(2,1)S(1)} %get-tuple-element.37.late_values, ...), custom_call_target="tpu_custom_call" | custom-call | flops 7200000000 | bytes 54000000 | tf_op jit(solution)/shard_map/pallas_call | solution.py:810
  48.7 0.0 collective-permute-done.2.tops
  48.7 0.1 collective-permute-done.1.returned
  48.8 3.6 %shard_map.60 = (f32[13824,128]{1,0:T(8,128)S(1)}, bf16[1728,128]{1,0:T(8,128)(2,1)S(1)}) custom-call(s32[1152]{0:T(1024)S(1)} %copy-done.1, f32[13824,128]{1,0:T(8,128)S(1)} %shard_map.59.total_in, s16[1728,128]{1,0:T(8,128)(2,1)S(1)} %collective-permute-done.1.returned, ...), custom_call_target="tpu_custom_call", output_to_operand_aliasing={{0}: (1, {})} | custom-call | flops 1200000000 | bytes 9000000 | tf_op jit(solution)/shard_map/pallas_call | solution.py:828
  52.4 5.5 %collective-permute-start.3 = (bf16[1728,128]{1,0:T(8,128)(2,1)S(1)}, bf16[1728,128]{1,0:T(8,128)(2,1)S(1)}, u32[]{:S(2)}, u32[]{:S(2)}) collective-permute-start(bf16[1728,128]{1,0:T(8,128)(2,1)S(1)} %get-tuple-element.42), channel_id=1, source_target_pairs={{0,30},{2,0},{4,2},{6,4},{8,6},{10,8},{12,10},{14,12},{16,14},{18,... | collective-permute-start | bytes 1327112 | tf_op jit(solution)/shard_map/ppermute | solution.py:41
  58.0 10.5 %shard_map.61 = (bf16[9728,256]{1,0:T(8,128)(2,1)S(1)}, f32[2048,256]{1,0:T(8,128)S(1)}) custom-call(s32[1]{0:T(128)} %get-tuple-element.29.regular, s32[12288]{0:T(1024)S(1)} %bitcast.6, f32[13824,128]{1,0:T(8,128)S(1)} %get-tuple-element.40.nodes, bf16[368,368]{1,0:T(8,128)(2,1)S(1)} %get-tuple-element.31.matrix), custom_call_target="tpu_custom_call" | custom-call | flops 4000000000 | bytes 30000000 | tf_op jit(solution)/shard_map/pallas_call | solution.py:800
  68.5 0.0 collective-permute-done.3.arrived
  68.5 6.4 %shard_map.62 = (s16[1728,128]{1,0:T(8,128)(2,1)S(1)}, bf16[144,128]{1,0:T(8,128)(2,1)S(1)}, bf16[2048,256]{1,0:T(8,128)(2,1)S(1)}) custom-call(s32[1]{0:T(128)} %get-tuple-element.29.regular, s32[12288]{0:T(1024)S(1)} %bitcast.7, s32[4096]{0:T(1024)S(1)} %bitcast.10, bf16[1728,128]{1,0:T(8,128)(2,1)S(1)} %collective-permute-done.3.arrived, ...), custom_call_target="tpu_custom_call" | custom-call | flops 2400000000 | bytes 18000000 | tf_op jit(solution)/shard_map/pallas_call | solution.py:789
  75.0 0.1 collective-permute-start.5
  75.0 0.1 collective-permute-start.4
  75.1 16.2 %shard_map.63.total_in = f32[13824,128]{1,0:T(8,128)S(1)} custom-call(s32[1]{0:T(128)} %get-tuple-element.29.regular, s32[12288]{0:T(1024)S(1)} %bitcast.8, bf16[368,368]{1,0:T(8,128)(2,1)S(1)} %get-tuple-element.31.matrix, bf16[9728,256]{1,0:T(8,128)(2,1)S(1)} %get-tuple-element.41.own_values, bf16[2048,256]{1,0:T(8,128)(2,1)S(1)} %get-tuple-element.44.late_values, ...), custom_call_target="tpu_custom_call" | custom-call | flops 7200000000 | bytes 54000000 | tf_op jit(solution)/shard_map/pallas_call | solution.py:810
  91.4 0.0 collective-permute-done.5.tops
  91.4 0.0 collective-permute-done.4.returned
  91.4 4.2 %shard_map.64 = (f32[13824,128]{1,0:T(8,128)S(1)}, bf16[192,3456]{1,0:T(8,128)(2,1)S(1)}) custom-call(s32[1152]{0:T(1024)S(1)} %copy-done.1, f32[13824,128]{1,0:T(8,128)S(1)} %shard_map.63.total_in, s16[1728,128]{1,0:T(8,128)(2,1)S(1)} %collective-permute-done.4.returned, ...), custom_call_target="tpu_custom_call", output_to_operand_aliasing={{0}: (1, {})} | custom-call | flops 2000000000 | bytes 15000000 | tf_op jit(solution)/shard_map/pallas_call | solution.py:839
  95.6 0.1 collective-permute-start.6
  95.6 1.2 shard_map.65.second.own
  96.8 0.6 collective-permute-start.7
  97.4 0.9 shard_map.66.gram
  98.3 0.4 collective-permute-done.6.other.first_other
  98.7 0.6 shard_map.67.begun
  99.3 1.3 collective-permute-done.7.other.second_other
  100.6 0.7 shard_map.68
  101.3 0.1 collective-permute-start.8
  101.3 1.1 collective-permute-start.9
  102.4 2.1 %collective-permute-start.10 = (f32[96,128]{1,0:T(8,128)S(1)}, f32[96,128]{1,0:T(8,128)S(1)}, u32[]{:S(2)}, u32[]{:S(2)}) collective-permute-start(f32[96,128]{1,0:T(8,128)S(1)} %get-tuple-element.52), channel_id=1, source_target_pairs={{0,6},{2,0},{4,2},{6,4},{8,14},{10,8},{12,10},{14,12},{16,22},{18,... | collective-permute-start | bytes 147464 | tf_op jit(solution)/shard_map/ppermute | solution.py:629
  104.5 2.1 %collective-permute-done.8 = f32[96,128]{1,0:T(8,128)S(1)} collective-permute-done((f32[96,128]{1,0:T(8,128)S(1)}, f32[96,128]{1,0:T(8,128)S(1)}, u32[]{:S(2)}, u32[]{:S(2)}) %collective-permute-start.8) | collective-permute-done | bytes 49184 | tf_op jit(solution)/shard_map/ppermute | solution.py:629
  106.5 0.0 collective-permute-done.9
  106.5 0.3 collective-permute-done.10
  106.9 5.9 %collective-permute-start.13 = (f32[96,128]{1,0:T(8,128)S(1)}, f32[96,128]{1,0:T(8,128)S(1)}, u32[]{:S(2)}, u32[]{:S(2)}) collective-permute-start(f32[96,128]{1,0:T(8,128)S(1)} %add_add_fusion.1), channel_id=1, source_target_pairs={{0,24},{2,26},{4,28},{6,30},{8,0},{10,2},{12,4},{14,6},{16,8},{18,... | collective-permute-start | bytes 147464 | tf_op jit(solution)/shard_map/ppermute | solution.py:629
  112.7 0.0 collective-permute-start.12
  112.7 0.6 collective-permute-start.11
  113.4 1.1 collective-permute-done.13
  114.5 3.2 %collective-permute-done.12 = f32[96,128]{1,0:T(8,128)S(1)} collective-permute-done((f32[96,128]{1,0:T(8,128)S(1)}, f32[96,128]{1,0:T(8,128)S(1)}, u32[]{:S(2)}, u32[]{:S(2)}) %collective-permute-start.12) | collective-permute-done | bytes 49184 | tf_op jit(solution)/shard_map/ppermute | solution.py:629
  117.7 0.9 collective-permute-done.11
  118.7 3.3 %collective-permute-start.16 = (f32[96,128]{1,0:T(8,128)S(1)}, f32[96,128]{1,0:T(8,128)S(1)}, u32[]{:S(2)}, u32[]{:S(2)}) collective-permute-start(f32[96,128]{1,0:T(8,128)S(1)} %add_add_fusion.refs_0_), channel_id=1, source_target_pairs={{0,6},{2,0},{4,2},{6,4},{8,14},{10,8},{12,10},{14,12},{16,22},{18,... | collective-permute-start | bytes 147464 | tf_op jit(solution)/shard_map/ppermute | solution.py:629
  121.9 0.0 collective-permute-start.15
  121.9 0.6 collective-permute-start.14
  122.6 0.0 collective-permute-start.17
  122.6 1.1 collective-permute-done.16.refs_3_
  123.7 0.0 collective-permute-start.20
  123.7 2.3 %collective-permute-done.15.refs_2_ = f32[96,128]{1,0:T(8,128)S(1)} collective-permute-done((f32[96,128]{1,0:T(8,128)S(1)}, f32[96,128]{1,0:T(8,128)S(1)}, u32[]{:S(2)}, u32[]{:S(2)}) %collective-permute-start.15) | collective-permute-done | bytes 49184 | tf_op jit(solution)/shard_map/ppermute | solution.py:629
  126.0 0.0 collective-permute-start.19
  126.0 0.9 collective-permute-done.14.refs_1_
  126.9 0.0 collective-permute-start.18
  126.9 0.0 collective-permute-done.17.refs_4_
  126.9 0.0 collective-permute-done.20.refs_7_
  126.9 0.3 collective-permute-done.19.refs_6_
  127.3 0.9 collective-permute-done.18.refs_5_
  128.2 3.8 %shard_map.69.root = bf16[192,384]{1,0:T(8,128)(2,1)S(1)} custom-call(f32[96,128]{1,0:T(8,128)S(1)} %add_add_fusion.refs_0_, f32[96,128]{1,0:T(8,128)S(1)} %collective-permute-done.14.refs_1_, f32[96,128]{1,0:T(8,128)S(1)} %collective-permute-done.15.refs_2_, f32[96,128]{1,0:T(8,128)S(1)} %collective-permute-done.16.refs_3_, ...), custom_call_target="tpu_custom_call" | custom-call | flops 2400000000 | bytes 18000000 | tf_op jit(solution)/shard_map/pallas_call | solution.py:865
  131.9 4.8 %shard_map.70 = f32[192,6912]{1,0:T(8,128)} custom-call(bf16[192,384]{1,0:T(8,128)(2,1)S(1)} %shard_map.69.root, bf16[192,3456]{1,0:T(8,128)(2,1)S(1)} %get-tuple-element.47.first.own, bf16[192,3456]{1,0:T(8,128)(2,1)S(1)} %collective-permute-done.6.other.first_other, bf16[192,3456]{1,0:T(8,128)(2,1)S(1)} %shard_map.65.second.own, ...), custom_call_target="tpu_custom_call" | custom-call | flops 1200000000 | bytes 9000000 | tf_op jit(solution)/shard_map/pallas_call | solution.py:874
  (8 shorter events, 0.0 us)
Async XLA Ops:
  0.0 0.7 copy-start
  0.7 1.7 %copy-start.2 = (bf16[192,6912]{1,0:T(8,128)(2,1)S(1)}, bf16[192,6912]{1,0:T(8,128)(2,1)}, u32[]{:S(2)}) copy-start(bf16[192,6912]{1,0:T(8,128)(2,1)} %states.1) | copy-start | bytes 7962628
  2.4 0.7 copy-start.5
  3.2 12.2 %copy-start.3 = (bf16[343,343]{1,0:T(8,128)(2,1)S(1)}, bf16[343,343]{1,0:T(8,128)(2,1)}, u32[]{:S(2)}) copy-start(bf16[343,343]{1,0:T(8,128)(2,1)} %kinetic.1) | copy-start | bytes 705898
  3.2 12.2 %copy-start.4 = (s32[32,343]{1,0:T(8,128)S(1)}, s32[32,343]{1,0:T(8,128)}, u32[]{:S(2)}) copy-start(s32[32,343]{1,0:T(8,128)} %cell_nodes.1) | copy-start | bytes 131716
  8.4 18.1 %collective-permute-start = (bf16[1728,128]{1,0:T(8,128)(2,1)S(1)}, bf16[1728,128]{1,0:T(8,128)(2,1)S(1)}, u32[]{:S(2)}, u32[]{:S(2)}) collective-permute-start(bf16[1728,128]{1,0:T(8,128)(2,1)S(1)} %get-tuple-element.35), channel_id=1, source_target_pairs={{0,30},{2,0},{4,2},{6,4},{8,6},{10,8},{12,10},{14,12},{16,14},{18,... | collective-permute-start | bytes 1327112 | tf_op jit(solution)/shard_map/ppermute | solution.py:41
  32.8 15.9 %collective-permute-start.2 = (bf16[144,128]{1,0:T(8,128)(2,1)S(1)}, bf16[144,128]{1,0:T(8,128)(2,1)S(1)}, u32[]{:S(2)}, u32[]{:S(2)}) collective-permute-start(bf16[144,128]{1,0:T(8,128)(2,1)S(1)} %get-tuple-element.39), channel_id=1, source_target_pairs={{0,2},{2,4},{4,6},{6,8},{8,10},{10,12},{12,14},{14,16},{16,18},{18... | collective-permute-start | bytes 110600 | tf_op jit(solution)/shard_map/ppermute | solution.py:41
  32.8 16.0 %collective-permute-start.1 = (s16[1728,128]{1,0:T(8,128)(2,1)S(1)}, s16[1728,128]{1,0:T(8,128)(2,1)S(1)}, u32[]{:S(2)}, u32[]{:S(2)}) collective-permute-start(s16[1728,128]{1,0:T(8,128)(2,1)S(1)} %get-tuple-element.38), channel_id=1, source_target_pairs={{0,2},{2,4},{4,6},{6,8},{8,10},{10,12},{12,14},{14,16},{16,18},{18... | collective-permute-start | bytes 1327112 | tf_op jit(solution)/shard_map/ppermute | solution.py:41
  32.9 15.9 %copy-start.1 = (s32[1152]{0:T(1024)S(1)}, s32[1152]{0:T(1024)}, u32[]{:S(2)}) copy-start(s32[1152]{0:T(1024)} %face.5) | copy-start | bytes 13828
  52.4 16.1 %collective-permute-start.3 = (bf16[1728,128]{1,0:T(8,128)(2,1)S(1)}, bf16[1728,128]{1,0:T(8,128)(2,1)S(1)}, u32[]{:S(2)}, u32[]{:S(2)}) collective-permute-start(bf16[1728,128]{1,0:T(8,128)(2,1)S(1)} %get-tuple-element.42), channel_id=1, source_target_pairs={{0,30},{2,0},{4,2},{6,4},{8,6},{10,8},{12,10},{14,12},{16,14},{18,... | collective-permute-start | bytes 1327112 | tf_op jit(solution)/shard_map/ppermute | solution.py:41
  75.0 16.4 %collective-permute-start.5 = (bf16[144,128]{1,0:T(8,128)(2,1)S(1)}, bf16[144,128]{1,0:T(8,128)(2,1)S(1)}, u32[]{:S(2)}, u32[]{:S(2)}) collective-permute-start(bf16[144,128]{1,0:T(8,128)(2,1)S(1)} %get-tuple-element.46), channel_id=1, source_target_pairs={{0,2},{2,4},{4,6},{6,8},{8,10},{10,12},{12,14},{14,16},{16,18},{18... | collective-permute-start | bytes 110600 | tf_op jit(solution)/shard_map/ppermute | solution.py:41
  75.0 16.3 %collective-permute-start.4 = (s16[1728,128]{1,0:T(8,128)(2,1)S(1)}, s16[1728,128]{1,0:T(8,128)(2,1)S(1)}, u32[]{:S(2)}, u32[]{:S(2)}) collective-permute-start(s16[1728,128]{1,0:T(8,128)(2,1)S(1)} %get-tuple-element.45), channel_id=1, source_target_pairs={{0,2},{2,4},{4,6},{6,8},{8,10},{10,12},{12,14},{14,16},{16,18},{18... | collective-permute-start | bytes 1327112 | tf_op jit(solution)/shard_map/ppermute | solution.py:41
  95.6 3.1 %collective-permute-start.6 = (bf16[192,3456]{1,0:T(8,128)(2,1)S(1)}, bf16[192,3456]{1,0:T(8,128)(2,1)S(1)}, u32[]{:S(2)}, u32[]{:S(2)}) collective-permute-start(bf16[192,3456]{1,0:T(8,128)(2,1)S(1)} %get-tuple-element.47.first.own), channel_id=1, source_target_pairs={{0,1},{1,0},{2,3},{3,2},{4,5},{5,4},{6,7},{7,6},{8,9},{9,8},{10,11... | collective-permute-start | bytes 3981320 | tf_op jit(solution)/shard_map/ppermute | solution.py:41
  96.8 3.8 %collective-permute-start.7 = (bf16[192,3456]{1,0:T(8,128)(2,1)S(1)}, bf16[192,3456]{1,0:T(8,128)(2,1)S(1)}, u32[]{:S(2)}, u32[]{:S(2)}) collective-permute-start(bf16[192,3456]{1,0:T(8,128)(2,1)S(1)} %shard_map.65.second.own), channel_id=1, source_target_pairs={{0,1},{1,0},{2,3},{3,2},{4,5},{5,4},{6,7},{7,6},{8,9},{9,8},{10,11... | collective-permute-start | bytes 3981320 | tf_op jit(solution)/shard_map/ppermute | solution.py:41
  101.3 5.3 %collective-permute-start.8 = (f32[96,128]{1,0:T(8,128)S(1)}, f32[96,128]{1,0:T(8,128)S(1)}, u32[]{:S(2)}, u32[]{:S(2)}) collective-permute-start(f32[96,128]{1,0:T(8,128)S(1)} %get-tuple-element.50), channel_id=1, source_target_pairs={{0,2},{2,4},{4,6},{6,0},{8,10},{10,12},{12,14},{14,8},{16,18},{18,... | collective-permute-start | bytes 147464 | tf_op jit(solution)/shard_map/ppermute | solution.py:629
  101.3 5.2 %collective-permute-start.9 = (f32[96,128]{1,0:T(8,128)S(1)}, f32[96,128]{1,0:T(8,128)S(1)}, u32[]{:S(2)}, u32[]{:S(2)}) collective-permute-start(f32[96,128]{1,0:T(8,128)S(1)} %get-tuple-element.51), channel_id=1, source_target_pairs={{0,4},{2,6},{4,0},{6,2},{8,12},{10,14},{12,8},{14,10},{16,20},{18,... | collective-permute-start | bytes 147464 | tf_op jit(solution)/shard_map/ppermute | solution.py:629
  102.4 4.5 %collective-permute-start.10 = (f32[96,128]{1,0:T(8,128)S(1)}, f32[96,128]{1,0:T(8,128)S(1)}, u32[]{:S(2)}, u32[]{:S(2)}) collective-permute-start(f32[96,128]{1,0:T(8,128)S(1)} %get-tuple-element.52), channel_id=1, source_target_pairs={{0,6},{2,0},{4,2},{6,4},{8,14},{10,8},{12,10},{14,12},{16,22},{18,... | collective-permute-start | bytes 147464 | tf_op jit(solution)/shard_map/ppermute | solution.py:629
  106.9 7.6 %collective-permute-start.13 = (f32[96,128]{1,0:T(8,128)S(1)}, f32[96,128]{1,0:T(8,128)S(1)}, u32[]{:S(2)}, u32[]{:S(2)}) collective-permute-start(f32[96,128]{1,0:T(8,128)S(1)} %add_add_fusion.1), channel_id=1, source_target_pairs={{0,24},{2,26},{4,28},{6,30},{8,0},{10,2},{12,4},{14,6},{16,8},{18,... | collective-permute-start | bytes 147464 | tf_op jit(solution)/shard_map/ppermute | solution.py:629
  112.7 5.0 %collective-permute-start.12 = (f32[96,128]{1,0:T(8,128)S(1)}, f32[96,128]{1,0:T(8,128)S(1)}, u32[]{:S(2)}, u32[]{:S(2)}) collective-permute-start(f32[96,128]{1,0:T(8,128)S(1)} %add_add_fusion.1), channel_id=1, source_target_pairs={{0,16},{2,18},{4,20},{6,22},{8,24},{10,26},{12,28},{14,30},{16,0},... | collective-permute-start | bytes 147464 | tf_op jit(solution)/shard_map/ppermute | solution.py:629
  112.7 5.9 %collective-permute-start.11 = (f32[96,128]{1,0:T(8,128)S(1)}, f32[96,128]{1,0:T(8,128)S(1)}, u32[]{:S(2)}, u32[]{:S(2)}) collective-permute-start(f32[96,128]{1,0:T(8,128)S(1)} %add_add_fusion.1), channel_id=1, source_target_pairs={{0,8},{2,10},{4,12},{6,14},{8,16},{10,18},{12,20},{14,22},{16,24},... | collective-permute-start | bytes 147464 | tf_op jit(solution)/shard_map/ppermute | solution.py:629
  118.7 5.0 %collective-permute-start.16 = (f32[96,128]{1,0:T(8,128)S(1)}, f32[96,128]{1,0:T(8,128)S(1)}, u32[]{:S(2)}, u32[]{:S(2)}) collective-permute-start(f32[96,128]{1,0:T(8,128)S(1)} %add_add_fusion.refs_0_), channel_id=1, source_target_pairs={{0,6},{2,0},{4,2},{6,4},{8,14},{10,8},{12,10},{14,12},{16,22},{18,... | collective-permute-start | bytes 147464 | tf_op jit(solution)/shard_map/ppermute | solution.py:629
  121.9 4.1 %collective-permute-start.15 = (f32[96,128]{1,0:T(8,128)S(1)}, f32[96,128]{1,0:T(8,128)S(1)}, u32[]{:S(2)}, u32[]{:S(2)}) collective-permute-start(f32[96,128]{1,0:T(8,128)S(1)} %add_add_fusion.refs_0_), channel_id=1, source_target_pairs={{0,4},{2,6},{4,0},{6,2},{8,12},{10,14},{12,8},{14,10},{16,20},{18,... | collective-permute-start | bytes 147464 | tf_op jit(solution)/shard_map/ppermute | solution.py:629
  121.9 5.0 %collective-permute-start.14 = (f32[96,128]{1,0:T(8,128)S(1)}, f32[96,128]{1,0:T(8,128)S(1)}, u32[]{:S(2)}, u32[]{:S(2)}) collective-permute-start(f32[96,128]{1,0:T(8,128)S(1)} %add_add_fusion.refs_0_), channel_id=1, source_target_pairs={{0,2},{2,4},{4,6},{6,0},{8,10},{10,12},{12,14},{14,8},{16,18},{18,... | collective-permute-start | bytes 147464 | tf_op jit(solution)/shard_map/ppermute | solution.py:629
  122.6 4.4 %collective-permute-start.17 = (f32[96,128]{1,0:T(8,128)S(1)}, f32[96,128]{1,0:T(8,128)S(1)}, u32[]{:S(2)}, u32[]{:S(2)}) collective-permute-start(f32[96,128]{1,0:T(8,128)S(1)} %add_add_fusion.refs_0_), channel_id=1, source_target_pairs={{0,1},{1,0},{2,3},{3,2},{4,5},{5,4},{6,7},{7,6},{8,9},{9,8},{10,11... | collective-permute-start | bytes 147464 | tf_op jit(solution)/shard_map/ppermute | solution.py:41
  123.7 3.2 %collective-permute-start.20 = (f32[96,128]{1,0:T(8,128)S(1)}, f32[96,128]{1,0:T(8,128)S(1)}, u32[]{:S(2)}, u32[]{:S(2)}) collective-permute-start(f32[96,128]{1,0:T(8,128)S(1)} %collective-permute-done.16.refs_3_), channel_id=1, source_target_pairs={{0,1},{1,0},{2,3},{3,2},{4,5},{5,4},{6,7},{7,6},{8,9},{9,8},{10,11... | collective-permute-start | bytes 147464 | tf_op jit(solution)/shard_map/ppermute | solution.py:41
  126.0 1.2 collective-permute-start.19
  126.9 1.2 collective-permute-start.18

commit v5 on v4

--- a/solution.py
+++ b/solution.py
@@ -8,8 +8,10 @@
 
 NS_STEPS = 3
 LANES = 128
-BATCH = 8
+OWN_BATCH = 5
+LATE_BATCH = 7
 CODES = 32767.0
+STEP = 0.0625
 
 cheb_center = 3.0
 cheb_half = 7.0
@@ -92,6 +94,10 @@
     return low, jnp.concatenate([high[i * part : (i + 1) * part, :rest] for i in range(fold)], axis=1)
 
 
+def packed_rows(count, width):
+    return count + count // (LANES // (width - LANES))
+
+
 def unpack(packed, count, width):
     rest = width - LANES
     fold = LANES // rest
@@ -143,21 +149,27 @@
     return 1
 
 
+def unit_of(steps):
+    return jnp.exp(steps * STEP)
+
+
 def coded(values):
     count = values.shape[0]
     size = group_of(count)
     grouped = values.reshape(count // (8 * size), size, 8, LANES)
-    top = jnp.max(jnp.abs(grouped), axis=1, keepdims=True)
-    top = jnp.maximum(top * 1.01, 1e-30).astype(jnp.bfloat16)
-    codes = jnp.round(grouped * (CODES / top.astype(jnp.float32)))
-    return codes.reshape(count, LANES).astype(jnp.int32).astype(jnp.int16), top.reshape(count // size, LANES)
-
-
-def decoded(codes, top):
-    count = codes.shape[0]
-    size = count // top.shape[0]
-    grouped = codes.astype(jnp.int32).astype(jnp.float32).reshape(count // (8 * size), size, 8, LANES)
-    unit = top.astype(jnp.float32).reshape(count // (8 * size), 1, 8, LANES) / CODES
+    top = jnp.maximum(jnp.max(jnp.abs(grouped), axis=1, keepdims=True), 1e-30)
+    steps = jnp.ceil(jnp.log(top * 1.001) / STEP)
+    codes = jnp.round(grouped * (CODES / unit_of(steps)))
+    codes = jnp.clip(codes, -CODES, CODES).reshape(count, LANES)
+    both = jnp.concatenate([codes, steps.reshape(count // size, LANES)], axis=0)
+    return both.astype(jnp.int32).astype(jnp.int16)
+
+
+def decoded(both, count):
+    size = group_of(count)
+    wide = both.astype(jnp.int32).astype(jnp.float32)
+    grouped = wide[:count].reshape(count // (8 * size), size, 8, LANES)
+    unit = unit_of(wide[count:]).reshape(count // (8 * size), 1, 8, LANES) / CODES
     return (grouped * unit).reshape(count, LANES)
 
 
@@ -344,7 +356,7 @@
 
 
 def shared_kernel(sizes, slots, width, again, regular, table_in, late_table, arrived, nodes, matrix, partial,
-                  send, tops, values_out, ghosts, total, other, gathered, products, any_gathered, any_products,
+                  send, values_out, ghosts, total, other, gathered, products, any_gathered, any_products,
                   table, sem):
     cells, early, early_rows, late_rows, stride = sizes
     late = slots - early
@@ -402,7 +414,7 @@
             parts = [
                 products.at[pl.ds(pl.multiple_of(cell * 2 * late_rows, 2 * late_rows), 2 * late_rows)] for cell in two
             ]
-            scatter_rows(lists, late, parts, (total, other))
+            scatter_rows(lists, late, parts, (total, other), LATE_BATCH)
             return 0
 
         lax.fori_loop(0, cells // 2, give, 0)
@@ -416,14 +428,12 @@
 
     low, high = (total[pl.ds(k, count, 2), :] + other[pl.ds(k, count, 2), :] for k in range(2))
     low, high = pack(low, high, width)
-    codes, top = coded(jnp.concatenate([low, high], axis=0))
-    send[...] = codes
-    tops[...] = top
-
-
-def scatter_rows(lists, slots, products, totals):
+    send[...] = coded(jnp.concatenate([low, high], axis=0))
+
+
+def scatter_rows(lists, slots, products, totals, batch):
     def start(k, begin):
-        size = min(BATCH, slots - begin)
+        size = min(batch, slots - begin)
         places = [pair(lists[k][begin + j]) for j in range(size)]
         held = [totals[k][place, :] for place in places]
 
@@ -434,7 +444,7 @@
         return end
 
     waiting = []
-    for begin in range(0, slots, BATCH):
+    for begin in range(0, slots, batch):
         for k in range(len(totals)):
             waiting.append(start(k, begin))
             if len(waiting) == len(totals):
@@ -456,7 +466,7 @@
 
     def give(cell, pairs):
         lists = [table.at[pl.ds((cell + k) * stride, stride)] for k in range(2)]
-        scatter_rows(lists, early, pairs, totals)
+        scatter_rows(lists, early, pairs, totals, OWN_BATCH)
 
     multiply(0, products[0])
     multiply(1, products[1])
@@ -529,18 +539,18 @@
         any_cells(sizes, again, slots, True, table, nodes, ghosts, matrix, any_gathered, any_products, total)
 
 
-def add_returned(width, face, returned, tops, total, spread):
+def add_returned(width, face, returned, total, spread):
     count = face.shape[0]
-    low, high = unpack(decoded(returned[...], tops[...]), count, width)
+    low, high = unpack(decoded(returned[...], packed_rows(count, width)), count, width)
     spread[pl.ds(0, count, 2), :] = low
     spread[pl.ds(1, count, 2), :] = high
     add_face(face, spread, total)
 
 
-def once_kernel(width, face, total_in, returned, tops, total, send, spread):
+def once_kernel(width, face, total_in, returned, total, send, spread):
     count = face.shape[0]
     gather_face(face, total, spread)
-    low, high = unpack(decoded(returned[...], tops[...]), count, width)
+    low, high = unpack(decoded(returned[...], packed_rows(count, width)), count, width)
     low = spread[pl.ds(0, count, 2), :] + low
     high = spread[pl.ds(1, count, 2), :] + high
     spread[pl.ds(0, count, 2), :] = low
@@ -566,8 +576,8 @@
     lax.fori_loop(0, half // block, one, 0, unroll=3)
 
 
-def twice_kernel(width, face, total_in, returned, tops, total, filtered, spread):
-    add_returned(width, face, returned, tops, total, spread)
+def twice_kernel(width, face, total_in, returned, total, filtered, spread):
+    add_returned(width, face, returned, total, spread)
     filter_half(total, filtered, 0, width)
 
 
@@ -741,7 +751,7 @@
     rows = early_rows + late_rows
     stride = rounded_up(slots, LANES)
     sizes = (cells, early, early_rows, late_rows, stride)
-    packed = count + count // (LANES // (width - LANES))
+    packed = packed_rows(count, width)
     integers = lambda *shape: jax.ShapeDtypeStruct(shape, jnp.int32)
 
     lumped = potential.reshape(-1, LANES)
@@ -780,15 +790,14 @@
         out_specs=(VMEM, VMEM, VMEM, SMEM),
     )(cell_nodes, kinetic)
     table, late_table = table.reshape(-1), late_table.reshape(-1)
-    sent_short = jax.ShapeDtypeStruct((packed, LANES), jnp.int16)
-    tops = jax.ShapeDtypeStruct((packed // group_of(packed), LANES), jnp.bfloat16)
+    sent_short = jax.ShapeDtypeStruct((packed + packed // group_of(packed), LANES), jnp.int16)
 
     held_table = pltpu.SMEM((cells * stride,), jnp.int32)
 
     def shared(again, arrived, nodes, partial):
         return called(
             functools.partial(shared_kernel, sizes, slots, width, again),
-            (sent_short, tops, late_values),
+            (sent_short, late_values),
             [SMEM, VMEM, SMEM, VMEM, VMEM, VMEM, VMEM],
             [spread, spread, spread, pairs_late, pairs_late, pairs_any, pairs_any]
             + [held_table, pltpu.SemaphoreType.DMA],
@@ -820,31 +829,30 @@
     def begun_sums(again, send, nodes, *before):
         arrived = passed_along(send, "brick", -1)
         values, part = own(again, nodes)
-        back, top, late_in = shared(again, arrived, nodes, part)
+        back, late_in = shared(again, arrived, nodes, part)
         returned = passed_along(back, "brick", 1)
-        returned_top = passed_along(top, "brick", 1)
-        return scattered(again, values, late_in, arrived, nodes, *before), returned, returned_top
+        return scattered(again, values, late_in, arrived, nodes, *before), returned
 
     total, send = called(
         functools.partial(once_kernel, width),
         (wide, sent),
-        [SMEM, VMEM, VMEM, VMEM],
+        [SMEM, VMEM, VMEM],
         [spread],
         3,
         6,
         input_output_aliases={1: 0},
     )(face_map, *begun_sums(False, send, begun))
-    total, returned, returned_top = begun_sums(True, send, total, begun)
+    total, returned = begun_sums(True, send, total, begun)
     half = jax.ShapeDtypeStruct((width, owned // 2), jnp.bfloat16)
     total, first = called(
         functools.partial(twice_kernel, width),
         (wide, half),
-        [SMEM, VMEM, VMEM, VMEM],
+        [SMEM, VMEM, VMEM],
         [spread],
         5,
         6,
         input_output_aliases={1: 0},
-    )(face_map, total, returned, returned_top)
+    )(face_map, total, returned)
     first_other = passed_along(first, "state", 1)
     (second,) = called(functools.partial(second_half_kernel, width), (half,), [VMEM], [], 2, 4)(total)
     second_other = passed_along(second, "state", 1)
@@ -870,14 +878,14 @@
         6,
         10,
     )(*mine, *theirs)
-    pieces = 3 if owned // 2 % (3 * LANES) == 0 else 1
+    pieces = 1
     return called(
         functools.partial(rotate_kernel, width, pieces),
         jax.ShapeDtypeStruct((width, owned), jnp.float32),
         [VMEM] * 5,
         [pltpu.VMEM((2, width, owned // 2 // pieces), jnp.float32), pltpu.SemaphoreType.DMA((2,))],
         3,
-        6,
+        8,
         out_specs=HBM,
     )(root, first, first_other, second, second_other)
 

time: 137 us -> 129 us (0.942)
  Pallas kernels: 91.1 us -> 84.6 us
  starting transfers between devices: 27 us -> 21.7 us
  waiting for transfers between devices: 15.1 us -> 19.3 us
    pallas_call x2, Pallas kernels: 32 us -> 27.3 us  [scattered(): called(functools.partial(scatter_kernel, sizes, slots, width, again), (wi...]
    ppermute x12 -> x10, waiting for transfers between devices: 3.1 us -> 7.07 us  [passed_along(): return lax.ppermute(value, axis, pairs)]
    ppermute x9, starting transfers between devices: 13.6 us -> 10.7 us  [exchanged(): lax.ppermute(give(step), axis, [(i, partner(i, step)) for i in range(coun...]
    ppermute x12 -> x10, starting transfers between devices: 13.4 us -> 11 us  [passed_along(): return lax.ppermute(value, axis, pairs)]
    pallas_call x1, Pallas kernels: 4.79 us -> 3.31 us  [local(): called(functools.partial(rotate_kernel, width, pieces), jax.ShapeDtypeStr...]
  transfers between devices with their start and end apart: 21 -> 19, of which waited for: 13 -> 14; matrix products, arithmetic and copies ran while one was open for 0% -> 0% of each run, Pallas kernels for 41% -> 40%
where the time goes in v5:
time: 129 us
  Pallas kernels  84.6 us (66%)
  starting transfers between devices  21.7 us (17%)
  waiting for transfers between devices  19.3 us (15%)
  local copies, waits for them, and re-layouts  3.21 us (2%)
    pallas_call x2, Pallas kernels, scattered(): called(functools.partial(scatter_kernel, sizes, slots, width, again), (wi...  27.3 us
    pallas_call x2, Pallas kernels, own(): called(functools.partial(own_kernel, sizes, again), (own_values, partial)...  20.9 us
    pallas_call x2, Pallas kernels, shared(): called(functools.partial(shared_kernel, sizes, slots, width, again), (sen...  12.3 us
    ppermute x9, waiting for transfers between devices, exchanged(): lax.ppermute(give(step), axis, [(i, partner(i, step)) for i in range(coun...  12.2 us
    ppermute x10, starting transfers between devices, passed_along(): return lax.ppermute(value, axis, pairs)  11 us
    ppermute x9, starting transfers between devices, exchanged(): lax.ppermute(give(step), axis, [(i, partner(i, step)) for i in range(coun...  10.7 us
    ppermute x10, waiting for transfers between devices, passed_along(): return lax.ppermute(value, axis, pairs)  7.07 us
    pallas_call x1, Pallas kernels, local(): called(functools.partial(prepare_kernel, width, chunks), (wide, sent), [S...  5.16 us
  transfers between devices with their start and end apart: 19, of which 14 were waited for; matrix products, arithmetic and copies ran while one was open for 0% of the time, Pallas kernels for 40%

profile of v5, /device:TPU:0, one launch (start us, length us, event | category | flops | bytes accessed | tf_op | source)
XLA Modules:
  0.0 129.1 jit_solution(12562095437803234809)
XLA Ops:
  0.0 0.0 copy-start
  0.0 0.7 copy-done
  0.7 0.0 copy-start.2
  0.7 1.7 %copy-done.2 = bf16[192,6912]{1,0:T(8,128)(2,1)S(1)} copy-done((bf16[192,6912]{1,0:T(8,128)(2,1)S(1)}, bf16[192,6912]{1,0:T(8,128)(2,1)}, u32[]{:S(2)}) %copy-start.2) | copy-done | bytes 2654232
  2.4 0.0 copy-start.5
  2.5 0.7 copy-done.5
  3.2 5.2 %shard_map.56 = (f32[13824,128]{1,0:T(8,128)S(1)}, bf16[1728,128]{1,0:T(8,128)(2,1)S(1)}) custom-call(s32[1152]{0:T(1024)S(1)} %copy-done, f32[54,128]{1,0:T(8,128)S(1)} %bitcast.11, bf16[192,6912]{1,0:T(8,128)(2,1)S(1)} %copy-done.2), custom_call_target="tpu_custom_call" | custom-call | flops 2400000000 | bytes 18000000 | tf_op jit(solution)/shard_map/pallas_call | solution.py:769
  8.4 7.0 %collective-permute-start = (bf16[1728,128]{1,0:T(8,128)(2,1)S(1)}, bf16[1728,128]{1,0:T(8,128)(2,1)S(1)}, u32[]{:S(2)}, u32[]{:S(2)}) collective-permute-start(bf16[1728,128]{1,0:T(8,128)(2,1)S(1)} %get-tuple-element.33), channel_id=1, source_target_pairs={{0,30},{2,0},{4,2},{6,4},{8,6},{10,8},{12,10},{14,12},{16,14},{18,... | collective-permute-start | bytes 1327112 | tf_op jit(solution)/shard_map/ppermute | solution.py:43
  15.4 0.0 copy-done.3
  15.4 0.0 copy-done.4
  15.4 0.7 shard_map.55
  16.1 10.4 %shard_map.57 = (bf16[9728,256]{1,0:T(8,128)(2,1)S(1)}, f32[2048,256]{1,0:T(8,128)S(1)}) custom-call(s32[1]{0:T(128)} %get-tuple-element.27.regular, s32[12288]{0:T(1024)S(1)} %bitcast.3, f32[13824,128]{1,0:T(8,128)S(1)} %get-tuple-element.30.nodes.rest_0_, bf16[368,368]{1,0:T(8,128)(2,1)S(1)} %get-tuple-element.29.matrix), custom_call_target="tpu_custom_call" | custom-call | flops 4000000000 | bytes 30000000 | tf_op jit(solution)/shard_map/pallas_call | solution.py:809
  26.5 0.0 collective-permute-done.arrived
  26.5 6.1 %shard_map.58 = (s16[1872,128]{1,0:T(8,128)(2,1)S(1)}, bf16[2048,256]{1,0:T(8,128)(2,1)S(1)}) custom-call(s32[1]{0:T(128)} %get-tuple-element.27.regular, s32[12288]{0:T(1024)S(1)} %bitcast.4, s32[4096]{0:T(1024)S(1)} %bitcast.9, bf16[1728,128]{1,0:T(8,128)(2,1)S(1)} %collective-permute-done.arrived, f32[13824,128]{1,0:T(8,128)S(1)} %get-tuple-element.30.nodes.rest_0_, ...), custom_call_target="tpu_custom_call" | custom-call | flops 2400000000 | bytes 18000000 | tf_op jit(solution)/shard_map/pallas_call | solution.py:798
  32.6 0.1 collective-permute-start.1
  32.7 0.0 copy-start.1
  32.7 13.4 %shard_map.59.total_in = f32[13824,128]{1,0:T(8,128)S(1)} custom-call(s32[1]{0:T(128)} %get-tuple-element.27.regular, s32[12288]{0:T(1024)S(1)} %bitcast.5, bf16[368,368]{1,0:T(8,128)(2,1)S(1)} %get-tuple-element.29.matrix, bf16[9728,256]{1,0:T(8,128)(2,1)S(1)} %get-tuple-element.31.own_values, bf16[2048,256]{1,0:T(8,128)(2,1)S(1)} %get-tuple-element.35.late_values, ...), custom_call_target="tpu_custom_call" | custom-call | flops 7200000000 | bytes 54000000 | tf_op jit(solution)/shard_map/pallas_call | solution.py:819
  46.1 2.6 %collective-permute-done.1.returned = s16[1872,128]{1,0:T(8,128)(2,1)S(1)} collective-permute-done((s16[1872,128]{1,0:T(8,128)(2,1)S(1)}, s16[1872,128]{1,0:T(8,128)(2,1)S(1)}, u32[]{:S(2)}, u32[]{:S(2)}) %collective-permute-start.1) | collective-permute-done | bytes 479264 | tf_op jit(solution)/shard_map/ppermute | solution.py:43
  48.7 0.0 copy-done.1
  48.7 3.6 %shard_map.60 = (f32[13824,128]{1,0:T(8,128)S(1)}, bf16[1728,128]{1,0:T(8,128)(2,1)S(1)}) custom-call(s32[1152]{0:T(1024)S(1)} %copy-done.1, f32[13824,128]{1,0:T(8,128)S(1)} %shard_map.59.total_in, s16[1872,128]{1,0:T(8,128)(2,1)S(1)} %collective-permute-done.1.returned), custom_call_target="tpu_custom_call", output_to_operand_aliasing={{0}: (1, {})} | custom-call | flops 1200000000 | bytes 9000000 | tf_op jit(solution)/shard_map/pallas_call | solution.py:836
  52.4 3.1 %collective-permute-start.2 = (bf16[1728,128]{1,0:T(8,128)(2,1)S(1)}, bf16[1728,128]{1,0:T(8,128)(2,1)S(1)}, u32[]{:S(2)}, u32[]{:S(2)}) collective-permute-start(bf16[1728,128]{1,0:T(8,128)(2,1)S(1)} %get-tuple-element.39), channel_id=1, source_target_pairs={{0,30},{2,0},{4,2},{6,4},{8,6},{10,8},{12,10},{14,12},{16,14},{18,... | collective-permute-start | bytes 1327112 | tf_op jit(solution)/shard_map/ppermute | solution.py:43
  55.5 10.5 %shard_map.61 = (bf16[9728,256]{1,0:T(8,128)(2,1)S(1)}, f32[2048,256]{1,0:T(8,128)S(1)}) custom-call(s32[1]{0:T(128)} %get-tuple-element.27.regular, s32[12288]{0:T(1024)S(1)} %bitcast.6, f32[13824,128]{1,0:T(8,128)S(1)} %get-tuple-element.37.nodes, bf16[368,368]{1,0:T(8,128)(2,1)S(1)} %get-tuple-element.29.matrix), custom_call_target="tpu_custom_call" | custom-call | flops 4000000000 | bytes 30000000 | tf_op jit(solution)/shard_map/pallas_call | solution.py:809
  66.0 0.0 collective-permute-done.2.arrived
  66.0 6.1 %shard_map.62 = (s16[1872,128]{1,0:T(8,128)(2,1)S(1)}, bf16[2048,256]{1,0:T(8,128)(2,1)S(1)}) custom-call(s32[1]{0:T(128)} %get-tuple-element.27.regular, s32[12288]{0:T(1024)S(1)} %bitcast.7, s32[4096]{0:T(1024)S(1)} %bitcast.10, bf16[1728,128]{1,0:T(8,128)(2,1)S(1)} %collective-permute-done.2.arrived, f32[13824,128]{1,0:T(8,128)S(1)} %get-tuple-element.37.nodes, ...), custom_call_target="tpu_custom_call" | custom-call | flops 2400000000 | bytes 18000000 | tf_op jit(solution)/shard_map/pallas_call | solution.py:798
  72.2 0.2 collective-permute-start.3
  72.4 13.9 %shard_map.63.total_in = f32[13824,128]{1,0:T(8,128)S(1)} custom-call(s32[1]{0:T(128)} %get-tuple-element.27.regular, s32[12288]{0:T(1024)S(1)} %bitcast.8, bf16[368,368]{1,0:T(8,128)(2,1)S(1)} %get-tuple-element.29.matrix, bf16[9728,256]{1,0:T(8,128)(2,1)S(1)} %get-tuple-element.38.own_values, bf16[2048,256]{1,0:T(8,128)(2,1)S(1)} %get-tuple-element.41.late_values, ...), custom_call_target="tpu_custom_call" | custom-call | flops 7200000000 | bytes 54000000 | tf_op jit(solution)/shard_map/pallas_call | solution.py:819
  86.3 1.5 %collective-permute-done.3.returned = s16[1872,128]{1,0:T(8,128)(2,1)S(1)} collective-permute-done((s16[1872,128]{1,0:T(8,128)(2,1)S(1)}, s16[1872,128]{1,0:T(8,128)(2,1)S(1)}, u32[]{:S(2)}, u32[]{:S(2)}) %collective-permute-start.3) | collective-permute-done | bytes 479264 | tf_op jit(solution)/shard_map/ppermute | solution.py:43
  87.9 4.2 %shard_map.64 = (f32[13824,128]{1,0:T(8,128)S(1)}, bf16[192,3456]{1,0:T(8,128)(2,1)S(1)}) custom-call(s32[1152]{0:T(1024)S(1)} %copy-done.1, f32[13824,128]{1,0:T(8,128)S(1)} %shard_map.63.total_in, s16[1872,128]{1,0:T(8,128)(2,1)S(1)} %collective-permute-done.3.returned), custom_call_target="tpu_custom_call", output_to_operand_aliasing={{0}: (1, {})} | custom-call | flops 2000000000 | bytes 15000000 | tf_op jit(solution)/shard_map/pallas_call | solution.py:847
  92.0 0.1 collective-permute-start.4
  92.1 1.2 shard_map.65.second.own
  93.3 0.6 collective-permute-start.5
  93.9 0.9 shard_map.66.gram
  94.8 0.4 collective-permute-done.4.other.first_other
  95.2 0.6 shard_map.67.begun
  95.7 1.3 %collective-permute-done.5.other.second_other = bf16[192,3456]{1,0:T(8,128)(2,1)S(1)} collective-permute-done((bf16[192,3456]{1,0:T(8,128)(2,1)S(1)}, bf16[192,3456]{1,0:T(8,128)(2,1)S(1)}, u32[]{:S(2)}, u32[]{:S(2)}) %collective-permute-start.5) | collective-permute-done | bytes 1327136 | tf_op jit(solution)/shard_map/ppermute | solution.py:43
  97.1 0.7 shard_map.68
  97.7 0.1 collective-permute-start.6
  97.8 0.1 collective-permute-start.7
  97.9 2.8 %collective-permute-start.8 = (f32[96,128]{1,0:T(8,128)S(1)}, f32[96,128]{1,0:T(8,128)S(1)}, u32[]{:S(2)}, u32[]{:S(2)}) collective-permute-start(f32[96,128]{1,0:T(8,128)S(1)} %get-tuple-element.48), channel_id=1, source_target_pairs={{0,6},{2,0},{4,2},{6,4},{8,14},{10,8},{12,10},{14,12},{16,22},{18,... | collective-permute-start | bytes 147464 | tf_op jit(solution)/shard_map/ppermute | solution.py:639
  100.7 2.3 %collective-permute-done.6 = f32[96,128]{1,0:T(8,128)S(1)} collective-permute-done((f32[96,128]{1,0:T(8,128)S(1)}, f32[96,128]{1,0:T(8,128)S(1)}, u32[]{:S(2)}, u32[]{:S(2)}) %collective-permute-start.6) | collective-permute-done | bytes 49184 | tf_op jit(solution)/shard_map/ppermute | solution.py:639
  103.0 0.0 collective-permute-done.7
  103.0 0.3 collective-permute-done.8
  103.4 3.8 %collective-permute-start.11 = (f32[96,128]{1,0:T(8,128)S(1)}, f32[96,128]{1,0:T(8,128)S(1)}, u32[]{:S(2)}, u32[]{:S(2)}) collective-permute-start(f32[96,128]{1,0:T(8,128)S(1)} %add_add_fusion.1), channel_id=1, source_target_pairs={{0,24},{2,26},{4,28},{6,30},{8,0},{10,2},{12,4},{14,6},{16,8},{18,... | collective-permute-start | bytes 147464 | tf_op jit(solution)/shard_map/ppermute | solution.py:639
  107.2 0.0 collective-permute-start.10
  107.2 0.6 collective-permute-start.9
  107.8 1.1 collective-permute-done.11
  108.9 3.2 %collective-permute-done.10 = f32[96,128]{1,0:T(8,128)S(1)} collective-permute-done((f32[96,128]{1,0:T(8,128)S(1)}, f32[96,128]{1,0:T(8,128)S(1)}, u32[]{:S(2)}, u32[]{:S(2)}) %collective-permute-start.10) | collective-permute-done | bytes 49184 | tf_op jit(solution)/shard_map/ppermute | solution.py:639
  112.2 0.9 collective-permute-done.9
  113.1 2.6 %collective-permute-start.14 = (f32[96,128]{1,0:T(8,128)S(1)}, f32[96,128]{1,0:T(8,128)S(1)}, u32[]{:S(2)}, u32[]{:S(2)}) collective-permute-start(f32[96,128]{1,0:T(8,128)S(1)} %add_add_fusion.refs_0_), channel_id=1, source_target_pairs={{0,6},{2,0},{4,2},{6,4},{8,14},{10,8},{12,10},{14,12},{16,22},{18,... | collective-permute-start | bytes 147464 | tf_op jit(solution)/shard_map/ppermute | solution.py:639
  115.7 0.0 collective-permute-start.13
  115.7 0.6 collective-permute-start.12
  116.3 0.0 collective-permute-start.15
  116.3 1.1 collective-permute-done.14.refs_3_
  117.4 0.0 collective-permute-start.18
  117.4 2.3 %collective-permute-done.13.refs_2_ = f32[96,128]{1,0:T(8,128)S(1)} collective-permute-done((f32[96,128]{1,0:T(8,128)S(1)}, f32[96,128]{1,0:T(8,128)S(1)}, u32[]{:S(2)}, u32[]{:S(2)}) %collective-permute-start.13) | collective-permute-done | bytes 49184 | tf_op jit(solution)/shard_map/ppermute | solution.py:639
  119.8 0.0 collective-permute-start.17
  119.8 0.9 collective-permute-done.12.refs_1_
  120.7 0.0 collective-permute-start.16
  120.7 0.0 collective-permute-done.15.refs_4_
  120.7 0.0 collective-permute-done.18.refs_7_
  120.7 0.3 collective-permute-done.17.refs_6_
  121.0 0.9 collective-permute-done.16.refs_5_
  121.9 3.8 %shard_map.69.root = bf16[192,384]{1,0:T(8,128)(2,1)S(1)} custom-call(f32[96,128]{1,0:T(8,128)S(1)} %add_add_fusion.refs_0_, f32[96,128]{1,0:T(8,128)S(1)} %collective-permute-done.12.refs_1_, f32[96,128]{1,0:T(8,128)S(1)} %collective-permute-done.13.refs_2_, f32[96,128]{1,0:T(8,128)S(1)} %collective-permute-done.14.refs_3_, ...), custom_call_target="tpu_custom_call" | custom-call | flops 2400000000 | bytes 18000000 | tf_op jit(solution)/shard_map/pallas_call | solution.py:873
  125.7 3.3 %shard_map.70 = f32[192,6912]{1,0:T(8,128)} custom-call(bf16[192,384]{1,0:T(8,128)(2,1)S(1)} %shard_map.69.root, bf16[192,3456]{1,0:T(8,128)(2,1)S(1)} %get-tuple-element.43.first.own, bf16[192,3456]{1,0:T(8,128)(2,1)S(1)} %collective-permute-done.4.other.first_other, bf16[192,3456]{1,0:T(8,128)(2,1)S(1)} %shard_map.65.second.own, ...), custom_call_target="tpu_custom_call" | custom-call | flops 1200000000 | bytes 9000000 | tf_op jit(solution)/shard_map/pallas_call | solution.py:882
  (4 shorter events, 0.0 us)
Async XLA Ops:
  0.0 0.7 copy-start
  0.7 1.7 %copy-start.2 = (bf16[192,6912]{1,0:T(8,128)(2,1)S(1)}, bf16[192,6912]{1,0:T(8,128)(2,1)}, u32[]{:S(2)}) copy-start(bf16[192,6912]{1,0:T(8,128)(2,1)} %states.1) | copy-start | bytes 7962628
  2.4 0.7 copy-start.5
  3.2 12.2 %copy-start.3 = (bf16[343,343]{1,0:T(8,128)(2,1)S(1)}, bf16[343,343]{1,0:T(8,128)(2,1)}, u32[]{:S(2)}) copy-start(bf16[343,343]{1,0:T(8,128)(2,1)} %kinetic.1) | copy-start | bytes 705898
  3.2 12.2 %copy-start.4 = (s32[32,343]{1,0:T(8,128)S(1)}, s32[32,343]{1,0:T(8,128)}, u32[]{:S(2)}) copy-start(s32[32,343]{1,0:T(8,128)} %cell_nodes.1) | copy-start | bytes 131716
  8.4 18.1 %collective-permute-start = (bf16[1728,128]{1,0:T(8,128)(2,1)S(1)}, bf16[1728,128]{1,0:T(8,128)(2,1)S(1)}, u32[]{:S(2)}, u32[]{:S(2)}) collective-permute-start(bf16[1728,128]{1,0:T(8,128)(2,1)S(1)} %get-tuple-element.33), channel_id=1, source_target_pairs={{0,30},{2,0},{4,2},{6,4},{8,6},{10,8},{12,10},{14,12},{16,14},{18,... | collective-permute-start | bytes 1327112 | tf_op jit(solution)/shard_map/ppermute | solution.py:43
  32.6 16.1 %collective-permute-start.1 = (s16[1872,128]{1,0:T(8,128)(2,1)S(1)}, s16[1872,128]{1,0:T(8,128)(2,1)S(1)}, u32[]{:S(2)}, u32[]{:S(2)}) collective-permute-start(s16[1872,128]{1,0:T(8,128)(2,1)S(1)} %get-tuple-element.36), channel_id=1, source_target_pairs={{0,2},{2,4},{4,6},{6,8},{8,10},{10,12},{12,14},{14,16},{16,18},{18... | collective-permute-start | bytes 1437704 | tf_op jit(solution)/shard_map/ppermute | solution.py:43
  32.7 16.0 %copy-start.1 = (s32[1152]{0:T(1024)S(1)}, s32[1152]{0:T(1024)}, u32[]{:S(2)}) copy-start(s32[1152]{0:T(1024)} %face.5) | copy-start | bytes 13828
  52.4 13.7 %collective-permute-start.2 = (bf16[1728,128]{1,0:T(8,128)(2,1)S(1)}, bf16[1728,128]{1,0:T(8,128)(2,1)S(1)}, u32[]{:S(2)}, u32[]{:S(2)}) collective-permute-start(bf16[1728,128]{1,0:T(8,128)(2,1)S(1)} %get-tuple-element.39), channel_id=1, source_target_pairs={{0,30},{2,0},{4,2},{6,4},{8,6},{10,8},{12,10},{14,12},{16,14},{18,... | collective-permute-start | bytes 1327112 | tf_op jit(solution)/shard_map/ppermute | solution.py:43
  72.2 15.7 %collective-permute-start.3 = (s16[1872,128]{1,0:T(8,128)(2,1)S(1)}, s16[1872,128]{1,0:T(8,128)(2,1)S(1)}, u32[]{:S(2)}, u32[]{:S(2)}) collective-permute-start(s16[1872,128]{1,0:T(8,128)(2,1)S(1)} %get-tuple-element.42), channel_id=1, source_target_pairs={{0,2},{2,4},{4,6},{6,8},{8,10},{10,12},{12,14},{14,16},{16,18},{18... | collective-permute-start | bytes 1437704 | tf_op jit(solution)/shard_map/ppermute | solution.py:43
  92.0 3.1 %collective-permute-start.4 = (bf16[192,3456]{1,0:T(8,128)(2,1)S(1)}, bf16[192,3456]{1,0:T(8,128)(2,1)S(1)}, u32[]{:S(2)}, u32[]{:S(2)}) collective-permute-start(bf16[192,3456]{1,0:T(8,128)(2,1)S(1)} %get-tuple-element.43.first.own), channel_id=1, source_target_pairs={{0,1},{1,0},{2,3},{3,2},{4,5},{5,4},{6,7},{7,6},{8,9},{9,8},{10,11... | collective-permute-start | bytes 3981320 | tf_op jit(solution)/shard_map/ppermute | solution.py:43
  93.3 3.8 %collective-permute-start.5 = (bf16[192,3456]{1,0:T(8,128)(2,1)S(1)}, bf16[192,3456]{1,0:T(8,128)(2,1)S(1)}, u32[]{:S(2)}, u32[]{:S(2)}) collective-permute-start(bf16[192,3456]{1,0:T(8,128)(2,1)S(1)} %shard_map.65.second.own), channel_id=1, source_target_pairs={{0,1},{1,0},{2,3},{3,2},{4,5},{5,4},{6,7},{7,6},{8,9},{9,8},{10,11... | collective-permute-start | bytes 3981320 | tf_op jit(solution)/shard_map/ppermute | solution.py:43
  97.7 5.3 %collective-permute-start.6 = (f32[96,128]{1,0:T(8,128)S(1)}, f32[96,128]{1,0:T(8,128)S(1)}, u32[]{:S(2)}, u32[]{:S(2)}) collective-permute-start(f32[96,128]{1,0:T(8,128)S(1)} %get-tuple-element.46), channel_id=1, source_target_pairs={{0,2},{2,4},{4,6},{6,0},{8,10},{10,12},{12,14},{14,8},{16,18},{18,... | collective-permute-start | bytes 147464 | tf_op jit(solution)/shard_map/ppermute | solution.py:639
  97.8 5.2 %collective-permute-start.7 = (f32[96,128]{1,0:T(8,128)S(1)}, f32[96,128]{1,0:T(8,128)S(1)}, u32[]{:S(2)}, u32[]{:S(2)}) collective-permute-start(f32[96,128]{1,0:T(8,128)S(1)} %get-tuple-element.47), channel_id=1, source_target_pairs={{0,4},{2,6},{4,0},{6,2},{8,12},{10,14},{12,8},{14,10},{16,20},{18,... | collective-permute-start | bytes 147464 | tf_op jit(solution)/shard_map/ppermute | solution.py:639
  97.9 5.5 %collective-permute-start.8 = (f32[96,128]{1,0:T(8,128)S(1)}, f32[96,128]{1,0:T(8,128)S(1)}, u32[]{:S(2)}, u32[]{:S(2)}) collective-permute-start(f32[96,128]{1,0:T(8,128)S(1)} %get-tuple-element.48), channel_id=1, source_target_pairs={{0,6},{2,0},{4,2},{6,4},{8,14},{10,8},{12,10},{14,12},{16,22},{18,... | collective-permute-start | bytes 147464 | tf_op jit(solution)/shard_map/ppermute | solution.py:639
  103.4 5.5 %collective-permute-start.11 = (f32[96,128]{1,0:T(8,128)S(1)}, f32[96,128]{1,0:T(8,128)S(1)}, u32[]{:S(2)}, u32[]{:S(2)}) collective-permute-start(f32[96,128]{1,0:T(8,128)S(1)} %add_add_fusion.1), channel_id=1, source_target_pairs={{0,24},{2,26},{4,28},{6,30},{8,0},{10,2},{12,4},{14,6},{16,8},{18,... | collective-permute-start | bytes 147464 | tf_op jit(solution)/shard_map/ppermute | solution.py:639
  107.2 5.0 %collective-permute-start.10 = (f32[96,128]{1,0:T(8,128)S(1)}, f32[96,128]{1,0:T(8,128)S(1)}, u32[]{:S(2)}, u32[]{:S(2)}) collective-permute-start(f32[96,128]{1,0:T(8,128)S(1)} %add_add_fusion.1), channel_id=1, source_target_pairs={{0,16},{2,18},{4,20},{6,22},{8,24},{10,26},{12,28},{14,30},{16,0},... | collective-permute-start | bytes 147464 | tf_op jit(solution)/shard_map/ppermute | solution.py:639
  107.2 5.9 %collective-permute-start.9 = (f32[96,128]{1,0:T(8,128)S(1)}, f32[96,128]{1,0:T(8,128)S(1)}, u32[]{:S(2)}, u32[]{:S(2)}) collective-permute-start(f32[96,128]{1,0:T(8,128)S(1)} %add_add_fusion.1), channel_id=1, source_target_pairs={{0,8},{2,10},{4,12},{6,14},{8,16},{10,18},{12,20},{14,22},{16,24},... | collective-permute-start | bytes 147464 | tf_op jit(solution)/shard_map/ppermute | solution.py:639
  113.1 4.4 %collective-permute-start.14 = (f32[96,128]{1,0:T(8,128)S(1)}, f32[96,128]{1,0:T(8,128)S(1)}, u32[]{:S(2)}, u32[]{:S(2)}) collective-permute-start(f32[96,128]{1,0:T(8,128)S(1)} %add_add_fusion.refs_0_), channel_id=1, source_target_pairs={{0,6},{2,0},{4,2},{6,4},{8,14},{10,8},{12,10},{14,12},{16,22},{18,... | collective-permute-start | bytes 147464 | tf_op jit(solution)/shard_map/ppermute | solution.py:639
  115.7 4.1 %collective-permute-start.13 = (f32[96,128]{1,0:T(8,128)S(1)}, f32[96,128]{1,0:T(8,128)S(1)}, u32[]{:S(2)}, u32[]{:S(2)}) collective-permute-start(f32[96,128]{1,0:T(8,128)S(1)} %add_add_fusion.refs_0_), channel_id=1, source_target_pairs={{0,4},{2,6},{4,0},{6,2},{8,12},{10,14},{12,8},{14,10},{16,20},{18,... | collective-permute-start | bytes 147464 | tf_op jit(solution)/shard_map/ppermute | solution.py:639
  115.7 5.0 %collective-permute-start.12 = (f32[96,128]{1,0:T(8,128)S(1)}, f32[96,128]{1,0:T(8,128)S(1)}, u32[]{:S(2)}, u32[]{:S(2)}) collective-permute-start(f32[96,128]{1,0:T(8,128)S(1)} %add_add_fusion.refs_0_), channel_id=1, source_target_pairs={{0,2},{2,4},{4,6},{6,0},{8,10},{10,12},{12,14},{14,8},{16,18},{18,... | collective-permute-start | bytes 147464 | tf_op jit(solution)/shard_map/ppermute | solution.py:639
  116.3 4.4 %collective-permute-start.15 = (f32[96,128]{1,0:T(8,128)S(1)}, f32[96,128]{1,0:T(8,128)S(1)}, u32[]{:S(2)}, u32[]{:S(2)}) collective-permute-start(f32[96,128]{1,0:T(8,128)S(1)} %add_add_fusion.refs_0_), channel_id=1, source_target_pairs={{0,1},{1,0},{2,3},{3,2},{4,5},{5,4},{6,7},{7,6},{8,9},{9,8},{10,11... | collective-permute-start | bytes 147464 | tf_op jit(solution)/shard_map/ppermute | solution.py:43
  117.4 3.2 %collective-permute-start.18 = (f32[96,128]{1,0:T(8,128)S(1)}, f32[96,128]{1,0:T(8,128)S(1)}, u32[]{:S(2)}, u32[]{:S(2)}) collective-permute-start(f32[96,128]{1,0:T(8,128)S(1)} %collective-permute-done.14.refs_3_), channel_id=1, source_target_pairs={{0,1},{1,0},{2,3},{3,2},{4,5},{5,4},{6,7},{7,6},{8,9},{9,8},{10,11... | collective-permute-start | bytes 147464 | tf_op jit(solution)/shard_map/ppermute | solution.py:43
  119.8 1.2 collective-permute-start.17
  120.7 1.2 collective-permute-start.16

commit v6 on v5

--- a/solution.py
+++ b/solution.py
@@ -210,18 +210,12 @@
     regular[0] = jnp.where((jnp.max(odd) == 0) & (cells % 8 == 0), 1, 0)
 
 
-def prepare_kernel(width, chunks, face, potential, states, nodes, send, picked, held, sems):
+def prepare_kernel(width, chunks, face, potential, states, nodes, send, picked):
     owned = states.shape[1]
     block = block_of(owned)
     piece = owned // chunks
-    copies = []
-    for k in range(chunks):
-        part = pl.ds(k * piece, piece)
-        copies.append(pltpu.make_async_copy(states.at[:, part], held.at[:, part], sems.at[k]))
-        copies[-1].start()
     unit = identity(block)
     for k in range(chunks):
-        copies[k].wait()
 
         def one(i, _):
             first = pl.multiple_of(k * piece + i * block, block)
@@ -235,7 +229,7 @@
             tail = jnp.zeros(row.shape, jnp.float32)
             for place, part in enumerate(parts):
                 tail = jnp.where(row == place, part.astype(jnp.float32), tail)
-            turned = across(unit, jnp.concatenate([held[:, at], tail.astype(jnp.bfloat16)], axis=0))
+            turned = across(unit, jnp.concatenate([states[:, at], tail.astype(jnp.bfloat16)], axis=0))
             low, high = node_rows(first, block)
             nodes[low, :] = turned[:, :LANES]
             nodes[high, :] = turned[:, LANES:]
@@ -769,8 +763,8 @@
     begun, send = called(
         functools.partial(prepare_kernel, width, chunks),
         (wide, sent),
-        [SMEM, VMEM, HBM],
-        [spread, pltpu.VMEM((width, owned), jnp.bfloat16), pltpu.SemaphoreType.DMA((chunks,))],
+        [SMEM, VMEM, VMEM],
+        [spread],
         6,
         6,
     )(face_map, lumped, states)

time: 129 us -> 127 us (0.984)
  Pallas kernels: 84.6 us -> 82.7 us
    pallas_call x1, Pallas kernels: 5.16 us -> 3.13 us  [local(): called(functools.partial(prepare_kernel, width, chunks), (wide, sent), [S...]
  transfers between devices with their start and end apart: 19 -> 19, of which waited for: 14 -> 14; matrix products, arithmetic and copies ran while one was open for 0% -> 0% of each run, Pallas kernels for 40% -> 41%
where the time goes in v6:
time: 127 us
  Pallas kernels  82.7 us (65%)
  starting transfers between devices  21.6 us (17%)
  waiting for transfers between devices  19.1 us (15%)
  local copies, waits for them, and re-layouts  3.21 us (3%)
    pallas_call x2, Pallas kernels, scattered(): called(functools.partial(scatter_kernel, sizes, slots, width, again), (wi...  27.5 us
    pallas_call x2, Pallas kernels, own(): called(functools.partial(own_kernel, sizes, again), (own_values, partial)...  20.9 us
    pallas_call x2, Pallas kernels, shared(): called(functools.partial(shared_kernel, sizes, slots, width, again), (sen...  12.3 us
    ppermute x9, waiting for transfers between devices, exchanged(): lax.ppermute(give(step), axis, [(i, partner(i, step)) for i in range(coun...  12.2 us
    ppermute x9, starting transfers between devices, exchanged(): lax.ppermute(give(step), axis, [(i, partner(i, step)) for i in range(coun...  10.8 us
    ppermute x10, starting transfers between devices, passed_along(): return lax.ppermute(value, axis, pairs)  10.8 us
    ppermute x10, waiting for transfers between devices, passed_along(): return lax.ppermute(value, axis, pairs)  6.9 us
    pallas_call x1, Pallas kernels, local(): called(functools.partial(twice_kernel, width), (wide, half), [SMEM, VMEM,...  4.18 us
  transfers between devices with their start and end apart: 19, of which 14 were waited for; matrix products, arithmetic and copies ran while one was open for 0% of the time, Pallas kernels for 41%

profile of v6, /device:TPU:0, one launch (start us, length us, event | category | flops | bytes accessed | tf_op | source)
XLA Modules:
  0.0 127.1 jit_solution(13000390751643948469)
XLA Ops:
  0.0 0.0 copy-start
  0.0 0.7 copy-done
  0.7 0.0 copy-start.2
  0.7 1.7 %copy-done.2 = bf16[192,6912]{1,0:T(8,128)(2,1)S(1)} copy-done((bf16[192,6912]{1,0:T(8,128)(2,1)S(1)}, bf16[192,6912]{1,0:T(8,128)(2,1)}, u32[]{:S(2)}) %copy-start.2) | copy-done | bytes 2654232
  2.4 0.0 copy-start.5
  2.5 0.7 copy-done.5
  3.2 3.1 %shard_map.56 = (f32[13824,128]{1,0:T(8,128)S(1)}, bf16[1728,128]{1,0:T(8,128)(2,1)S(1)}) custom-call(s32[1152]{0:T(1024)S(1)} %copy-done, f32[54,128]{1,0:T(8,128)S(1)} %bitcast.11, bf16[192,6912]{1,0:T(8,128)(2,1)S(1)} %copy-done.2), custom_call_target="tpu_custom_call" | custom-call | flops 2400000000 | bytes 18000000 | tf_op jit(solution)/shard_map/pallas_call | solution.py:763
  6.3 7.0 %collective-permute-start = (bf16[1728,128]{1,0:T(8,128)(2,1)S(1)}, bf16[1728,128]{1,0:T(8,128)(2,1)S(1)}, u32[]{:S(2)}, u32[]{:S(2)}) collective-permute-start(bf16[1728,128]{1,0:T(8,128)(2,1)S(1)} %get-tuple-element.33), channel_id=1, source_target_pairs={{0,30},{2,0},{4,2},{6,4},{8,6},{10,8},{12,10},{14,12},{16,14},{18,... | collective-permute-start | bytes 1327112 | tf_op jit(solution)/shard_map/ppermute | solution.py:43
  13.3 0.0 copy-done.3
  13.3 0.0 copy-done.4
  13.3 0.7 shard_map.55
  14.1 10.4 %shard_map.57 = (bf16[9728,256]{1,0:T(8,128)(2,1)S(1)}, f32[2048,256]{1,0:T(8,128)S(1)}) custom-call(s32[1]{0:T(128)} %get-tuple-element.27.regular, s32[12288]{0:T(1024)S(1)} %bitcast.3, f32[13824,128]{1,0:T(8,128)S(1)} %get-tuple-element.30.nodes.rest_0_, bf16[368,368]{1,0:T(8,128)(2,1)S(1)} %get-tuple-element.29.matrix), custom_call_target="tpu_custom_call" | custom-call | flops 4000000000 | bytes 30000000 | tf_op jit(solution)/shard_map/pallas_call | solution.py:803
  24.4 0.0 collective-permute-done.arrived
  24.4 6.1 %shard_map.58 = (s16[1872,128]{1,0:T(8,128)(2,1)S(1)}, bf16[2048,256]{1,0:T(8,128)(2,1)S(1)}) custom-call(s32[1]{0:T(128)} %get-tuple-element.27.regular, s32[12288]{0:T(1024)S(1)} %bitcast.4, s32[4096]{0:T(1024)S(1)} %bitcast.9, bf16[1728,128]{1,0:T(8,128)(2,1)S(1)} %collective-permute-done.arrived, f32[13824,128]{1,0:T(8,128)S(1)} %get-tuple-element.30.nodes.rest_0_, ...), custom_call_target="tpu_custom_call" | custom-call | flops 2400000000 | bytes 18000000 | tf_op jit(solution)/shard_map/pallas_call | solution.py:792
  30.6 0.1 collective-permute-start.1
  30.7 0.0 copy-start.1
  30.7 13.4 %shard_map.59.total_in = f32[13824,128]{1,0:T(8,128)S(1)} custom-call(s32[1]{0:T(128)} %get-tuple-element.27.regular, s32[12288]{0:T(1024)S(1)} %bitcast.5, bf16[368,368]{1,0:T(8,128)(2,1)S(1)} %get-tuple-element.29.matrix, bf16[9728,256]{1,0:T(8,128)(2,1)S(1)} %get-tuple-element.31.own_values, bf16[2048,256]{1,0:T(8,128)(2,1)S(1)} %get-tuple-element.35.late_values, ...), custom_call_target="tpu_custom_call" | custom-call | flops 7200000000 | bytes 54000000 | tf_op jit(solution)/shard_map/pallas_call | solution.py:813
  44.1 2.6 %collective-permute-done.1.returned = s16[1872,128]{1,0:T(8,128)(2,1)S(1)} collective-permute-done((s16[1872,128]{1,0:T(8,128)(2,1)S(1)}, s16[1872,128]{1,0:T(8,128)(2,1)S(1)}, u32[]{:S(2)}, u32[]{:S(2)}) %collective-permute-start.1) | collective-permute-done | bytes 479264 | tf_op jit(solution)/shard_map/ppermute | solution.py:43
  46.7 0.0 copy-done.1
  46.7 3.6 %shard_map.60 = (f32[13824,128]{1,0:T(8,128)S(1)}, bf16[1728,128]{1,0:T(8,128)(2,1)S(1)}) custom-call(s32[1152]{0:T(1024)S(1)} %copy-done.1, f32[13824,128]{1,0:T(8,128)S(1)} %shard_map.59.total_in, s16[1872,128]{1,0:T(8,128)(2,1)S(1)} %collective-permute-done.1.returned), custom_call_target="tpu_custom_call", output_to_operand_aliasing={{0}: (1, {})} | custom-call | flops 1200000000 | bytes 9000000 | tf_op jit(solution)/shard_map/pallas_call | solution.py:830
  50.3 3.1 %collective-permute-start.2 = (bf16[1728,128]{1,0:T(8,128)(2,1)S(1)}, bf16[1728,128]{1,0:T(8,128)(2,1)S(1)}, u32[]{:S(2)}, u32[]{:S(2)}) collective-permute-start(bf16[1728,128]{1,0:T(8,128)(2,1)S(1)} %get-tuple-element.39), channel_id=1, source_target_pairs={{0,30},{2,0},{4,2},{6,4},{8,6},{10,8},{12,10},{14,12},{16,14},{18,... | collective-permute-start | bytes 1327112 | tf_op jit(solution)/shard_map/ppermute | solution.py:43
  53.4 10.5 %shard_map.61 = (bf16[9728,256]{1,0:T(8,128)(2,1)S(1)}, f32[2048,256]{1,0:T(8,128)S(1)}) custom-call(s32[1]{0:T(128)} %get-tuple-element.27.regular, s32[12288]{0:T(1024)S(1)} %bitcast.6, f32[13824,128]{1,0:T(8,128)S(1)} %get-tuple-element.37.nodes, bf16[368,368]{1,0:T(8,128)(2,1)S(1)} %get-tuple-element.29.matrix), custom_call_target="tpu_custom_call" | custom-call | flops 4000000000 | bytes 30000000 | tf_op jit(solution)/shard_map/pallas_call | solution.py:803
  63.9 0.0 collective-permute-done.2.arrived
  63.9 6.1 %shard_map.62 = (s16[1872,128]{1,0:T(8,128)(2,1)S(1)}, bf16[2048,256]{1,0:T(8,128)(2,1)S(1)}) custom-call(s32[1]{0:T(128)} %get-tuple-element.27.regular, s32[12288]{0:T(1024)S(1)} %bitcast.7, s32[4096]{0:T(1024)S(1)} %bitcast.10, bf16[1728,128]{1,0:T(8,128)(2,1)S(1)} %collective-permute-done.2.arrived, f32[13824,128]{1,0:T(8,128)S(1)} %get-tuple-element.37.nodes, ...), custom_call_target="tpu_custom_call" | custom-call | flops 2400000000 | bytes 18000000 | tf_op jit(solution)/shard_map/pallas_call | solution.py:792
  70.1 0.1 collective-permute-start.3
  70.2 14.1 %shard_map.63.total_in = f32[13824,128]{1,0:T(8,128)S(1)} custom-call(s32[1]{0:T(128)} %get-tuple-element.27.regular, s32[12288]{0:T(1024)S(1)} %bitcast.8, bf16[368,368]{1,0:T(8,128)(2,1)S(1)} %get-tuple-element.29.matrix, bf16[9728,256]{1,0:T(8,128)(2,1)S(1)} %get-tuple-element.38.own_values, bf16[2048,256]{1,0:T(8,128)(2,1)S(1)} %get-tuple-element.41.late_values, ...), custom_call_target="tpu_custom_call" | custom-call | flops 7200000000 | bytes 54000000 | tf_op jit(solution)/shard_map/pallas_call | solution.py:813
  84.3 1.4 %collective-permute-done.3.returned = s16[1872,128]{1,0:T(8,128)(2,1)S(1)} collective-permute-done((s16[1872,128]{1,0:T(8,128)(2,1)S(1)}, s16[1872,128]{1,0:T(8,128)(2,1)S(1)}, u32[]{:S(2)}, u32[]{:S(2)}) %collective-permute-start.3) | collective-permute-done | bytes 479264 | tf_op jit(solution)/shard_map/ppermute | solution.py:43
  85.6 4.2 %shard_map.64 = (f32[13824,128]{1,0:T(8,128)S(1)}, bf16[192,3456]{1,0:T(8,128)(2,1)S(1)}) custom-call(s32[1152]{0:T(1024)S(1)} %copy-done.1, f32[13824,128]{1,0:T(8,128)S(1)} %shard_map.63.total_in, s16[1872,128]{1,0:T(8,128)(2,1)S(1)} %collective-permute-done.3.returned), custom_call_target="tpu_custom_call", output_to_operand_aliasing={{0}: (1, {})} | custom-call | flops 2000000000 | bytes 15000000 | tf_op jit(solution)/shard_map/pallas_call | solution.py:841
  89.8 0.1 collective-permute-start.4
  89.9 1.2 shard_map.65.second.own
  91.1 0.6 collective-permute-start.5
  91.6 0.9 shard_map.66.gram
  92.5 0.4 collective-permute-done.4.other.first_other
  92.9 0.6 shard_map.67.begun
  93.5 1.3 %collective-permute-done.5.other.second_other = bf16[192,3456]{1,0:T(8,128)(2,1)S(1)} collective-permute-done((bf16[192,3456]{1,0:T(8,128)(2,1)S(1)}, bf16[192,3456]{1,0:T(8,128)(2,1)S(1)}, u32[]{:S(2)}, u32[]{:S(2)}) %collective-permute-start.5) | collective-permute-done | bytes 1327136 | tf_op jit(solution)/shard_map/ppermute | solution.py:43
  94.8 0.7 shard_map.68
  95.5 0.1 collective-permute-start.6
  95.6 0.1 collective-permute-start.7
  95.6 2.8 %collective-permute-start.8 = (f32[96,128]{1,0:T(8,128)S(1)}, f32[96,128]{1,0:T(8,128)S(1)}, u32[]{:S(2)}, u32[]{:S(2)}) collective-permute-start(f32[96,128]{1,0:T(8,128)S(1)} %get-tuple-element.48), channel_id=1, source_target_pairs={{0,6},{2,0},{4,2},{6,4},{8,14},{10,8},{12,10},{14,12},{16,22},{18,... | collective-permute-start | bytes 147464 | tf_op jit(solution)/shard_map/ppermute | solution.py:633
  98.5 2.3 %collective-permute-done.6 = f32[96,128]{1,0:T(8,128)S(1)} collective-permute-done((f32[96,128]{1,0:T(8,128)S(1)}, f32[96,128]{1,0:T(8,128)S(1)}, u32[]{:S(2)}, u32[]{:S(2)}) %collective-permute-start.6) | collective-permute-done | bytes 49184 | tf_op jit(solution)/shard_map/ppermute | solution.py:633
  100.8 0.0 collective-permute-done.7
  100.8 0.3 collective-permute-done.8
  101.1 3.9 %collective-permute-start.11 = (f32[96,128]{1,0:T(8,128)S(1)}, f32[96,128]{1,0:T(8,128)S(1)}, u32[]{:S(2)}, u32[]{:S(2)}) collective-permute-start(f32[96,128]{1,0:T(8,128)S(1)} %add_add_fusion.1), channel_id=1, source_target_pairs={{0,24},{2,26},{4,28},{6,30},{8,0},{10,2},{12,4},{14,6},{16,8},{18,... | collective-permute-start | bytes 147464 | tf_op jit(solution)/shard_map/ppermute | solution.py:633
  105.1 0.0 collective-permute-start.10
  105.1 0.6 collective-permute-start.9
  105.7 1.1 collective-permute-done.11
  106.8 3.2 %collective-permute-done.10 = f32[96,128]{1,0:T(8,128)S(1)} collective-permute-done((f32[96,128]{1,0:T(8,128)S(1)}, f32[96,128]{1,0:T(8,128)S(1)}, u32[]{:S(2)}, u32[]{:S(2)}) %collective-permute-start.10) | collective-permute-done | bytes 49184 | tf_op jit(solution)/shard_map/ppermute | solution.py:633
  110.1 0.9 collective-permute-done.9
  111.0 2.6 %collective-permute-start.14 = (f32[96,128]{1,0:T(8,128)S(1)}, f32[96,128]{1,0:T(8,128)S(1)}, u32[]{:S(2)}, u32[]{:S(2)}) collective-permute-start(f32[96,128]{1,0:T(8,128)S(1)} %add_add_fusion.refs_0_), channel_id=1, source_target_pairs={{0,6},{2,0},{4,2},{6,4},{8,14},{10,8},{12,10},{14,12},{16,22},{18,... | collective-permute-start | bytes 147464 | tf_op jit(solution)/shard_map/ppermute | solution.py:633
  113.6 0.0 collective-permute-start.13
  113.6 0.6 collective-permute-start.12
  114.3 0.0 collective-permute-start.15
  114.3 1.1 collective-permute-done.14.refs_3_
  115.4 0.0 collective-permute-start.18
  115.4 2.3 %collective-permute-done.13.refs_2_ = f32[96,128]{1,0:T(8,128)S(1)} collective-permute-done((f32[96,128]{1,0:T(8,128)S(1)}, f32[96,128]{1,0:T(8,128)S(1)}, u32[]{:S(2)}, u32[]{:S(2)}) %collective-permute-start.13) | collective-permute-done | bytes 49184 | tf_op jit(solution)/shard_map/ppermute | solution.py:633
  117.7 0.0 collective-permute-start.17
  117.7 0.9 collective-permute-done.12.refs_1_
  118.6 0.0 collective-permute-start.16
  118.6 0.0 collective-permute-done.15.refs_4_
  118.6 0.0 collective-permute-done.18.refs_7_
  118.6 0.3 collective-permute-done.17.refs_6_
  118.9 0.9 collective-permute-done.16.refs_5_
  119.8 3.8 %shard_map.69.root = bf16[192,384]{1,0:T(8,128)(2,1)S(1)} custom-call(f32[96,128]{1,0:T(8,128)S(1)} %add_add_fusion.refs_0_, f32[96,128]{1,0:T(8,128)S(1)} %collective-permute-done.12.refs_1_, f32[96,128]{1,0:T(8,128)S(1)} %collective-permute-done.13.refs_2_, f32[96,128]{1,0:T(8,128)S(1)} %collective-permute-done.14.refs_3_, ...), custom_call_target="tpu_custom_call" | custom-call | flops 2400000000 | bytes 18000000 | tf_op jit(solution)/shard_map/pallas_call | solution.py:867
  123.6 3.3 %shard_map.70 = f32[192,6912]{1,0:T(8,128)} custom-call(bf16[192,384]{1,0:T(8,128)(2,1)S(1)} %shard_map.69.root, bf16[192,3456]{1,0:T(8,128)(2,1)S(1)} %get-tuple-element.43.first.own, bf16[192,3456]{1,0:T(8,128)(2,1)S(1)} %collective-permute-done.4.other.first_other, bf16[192,3456]{1,0:T(8,128)(2,1)S(1)} %shard_map.65.second.own, ...), custom_call_target="tpu_custom_call" | custom-call | flops 1200000000 | bytes 9000000 | tf_op jit(solution)/shard_map/pallas_call | solution.py:876
  (4 shorter events, 0.0 us)
Async XLA Ops:
  0.0 0.7 copy-start
  0.7 1.7 %copy-start.2 = (bf16[192,6912]{1,0:T(8,128)(2,1)S(1)}, bf16[192,6912]{1,0:T(8,128)(2,1)}, u32[]{:S(2)}) copy-start(bf16[192,6912]{1,0:T(8,128)(2,1)} %states.1) | copy-start | bytes 7962628
  2.4 0.7 copy-start.5
  3.2 10.1 %copy-start.3 = (bf16[343,343]{1,0:T(8,128)(2,1)S(1)}, bf16[343,343]{1,0:T(8,128)(2,1)}, u32[]{:S(2)}) copy-start(bf16[343,343]{1,0:T(8,128)(2,1)} %kinetic.1) | copy-start | bytes 705898
  3.2 10.1 %copy-start.4 = (s32[32,343]{1,0:T(8,128)S(1)}, s32[32,343]{1,0:T(8,128)}, u32[]{:S(2)}) copy-start(s32[32,343]{1,0:T(8,128)} %cell_nodes.1) | copy-start | bytes 131716
  6.3 18.1 %collective-permute-start = (bf16[1728,128]{1,0:T(8,128)(2,1)S(1)}, bf16[1728,128]{1,0:T(8,128)(2,1)S(1)}, u32[]{:S(2)}, u32[]{:S(2)}) collective-permute-start(bf16[1728,128]{1,0:T(8,128)(2,1)S(1)} %get-tuple-element.33), channel_id=1, source_target_pairs={{0,30},{2,0},{4,2},{6,4},{8,6},{10,8},{12,10},{14,12},{16,14},{18,... | collective-permute-start | bytes 1327112 | tf_op jit(solution)/shard_map/ppermute | solution.py:43
  30.6 16.1 %collective-permute-start.1 = (s16[1872,128]{1,0:T(8,128)(2,1)S(1)}, s16[1872,128]{1,0:T(8,128)(2,1)S(1)}, u32[]{:S(2)}, u32[]{:S(2)}) collective-permute-start(s16[1872,128]{1,0:T(8,128)(2,1)S(1)} %get-tuple-element.36), channel_id=1, source_target_pairs={{0,2},{2,4},{4,6},{6,8},{8,10},{10,12},{12,14},{14,16},{16,18},{18... | collective-permute-start | bytes 1437704 | tf_op jit(solution)/shard_map/ppermute | solution.py:43
  30.7 16.0 %copy-start.1 = (s32[1152]{0:T(1024)S(1)}, s32[1152]{0:T(1024)}, u32[]{:S(2)}) copy-start(s32[1152]{0:T(1024)} %face.5) | copy-start | bytes 13828
  50.3 13.6 %collective-permute-start.2 = (bf16[1728,128]{1,0:T(8,128)(2,1)S(1)}, bf16[1728,128]{1,0:T(8,128)(2,1)S(1)}, u32[]{:S(2)}, u32[]{:S(2)}) collective-permute-start(bf16[1728,128]{1,0:T(8,128)(2,1)S(1)} %get-tuple-element.39), channel_id=1, source_target_pairs={{0,30},{2,0},{4,2},{6,4},{8,6},{10,8},{12,10},{14,12},{16,14},{18,... | collective-permute-start | bytes 1327112 | tf_op jit(solution)/shard_map/ppermute | solution.py:43
  70.1 15.5 %collective-permute-start.3 = (s16[1872,128]{1,0:T(8,128)(2,1)S(1)}, s16[1872,128]{1,0:T(8,128)(2,1)S(1)}, u32[]{:S(2)}, u32[]{:S(2)}) collective-permute-start(s16[1872,128]{1,0:T(8,128)(2,1)S(1)} %get-tuple-element.42), channel_id=1, source_target_pairs={{0,2},{2,4},{4,6},{6,8},{8,10},{10,12},{12,14},{14,16},{16,18},{18... | collective-permute-start | bytes 1437704 | tf_op jit(solution)/shard_map/ppermute | solution.py:43
  89.8 3.1 %collective-permute-start.4 = (bf16[192,3456]{1,0:T(8,128)(2,1)S(1)}, bf16[192,3456]{1,0:T(8,128)(2,1)S(1)}, u32[]{:S(2)}, u32[]{:S(2)}) collective-permute-start(bf16[192,3456]{1,0:T(8,128)(2,1)S(1)} %get-tuple-element.43.first.own), channel_id=1, source_target_pairs={{0,1},{1,0},{2,3},{3,2},{4,5},{5,4},{6,7},{7,6},{8,9},{9,8},{10,11... | collective-permute-start | bytes 3981320 | tf_op jit(solution)/shard_map/ppermute | solution.py:43
  91.1 3.8 %collective-permute-start.5 = (bf16[192,3456]{1,0:T(8,128)(2,1)S(1)}, bf16[192,3456]{1,0:T(8,128)(2,1)S(1)}, u32[]{:S(2)}, u32[]{:S(2)}) collective-permute-start(bf16[192,3456]{1,0:T(8,128)(2,1)S(1)} %shard_map.65.second.own), channel_id=1, source_target_pairs={{0,1},{1,0},{2,3},{3,2},{4,5},{5,4},{6,7},{7,6},{8,9},{9,8},{10,11... | collective-permute-start | bytes 3981320 | tf_op jit(solution)/shard_map/ppermute | solution.py:43
  95.5 5.3 %collective-permute-start.6 = (f32[96,128]{1,0:T(8,128)S(1)}, f32[96,128]{1,0:T(8,128)S(1)}, u32[]{:S(2)}, u32[]{:S(2)}) collective-permute-start(f32[96,128]{1,0:T(8,128)S(1)} %get-tuple-element.46), channel_id=1, source_target_pairs={{0,2},{2,4},{4,6},{6,0},{8,10},{10,12},{12,14},{14,8},{16,18},{18,... | collective-permute-start | bytes 147464 | tf_op jit(solution)/shard_map/ppermute | solution.py:633
  95.6 5.2 %collective-permute-start.7 = (f32[96,128]{1,0:T(8,128)S(1)}, f32[96,128]{1,0:T(8,128)S(1)}, u32[]{:S(2)}, u32[]{:S(2)}) collective-permute-start(f32[96,128]{1,0:T(8,128)S(1)} %get-tuple-element.47), channel_id=1, source_target_pairs={{0,4},{2,6},{4,0},{6,2},{8,12},{10,14},{12,8},{14,10},{16,20},{18,... | collective-permute-start | bytes 147464 | tf_op jit(solution)/shard_map/ppermute | solution.py:633
  95.6 5.5 %collective-permute-start.8 = (f32[96,128]{1,0:T(8,128)S(1)}, f32[96,128]{1,0:T(8,128)S(1)}, u32[]{:S(2)}, u32[]{:S(2)}) collective-permute-start(f32[96,128]{1,0:T(8,128)S(1)} %get-tuple-element.48), channel_id=1, source_target_pairs={{0,6},{2,0},{4,2},{6,4},{8,14},{10,8},{12,10},{14,12},{16,22},{18,... | collective-permute-start | bytes 147464 | tf_op jit(solution)/shard_map/ppermute | solution.py:633
  101.1 5.7 %collective-permute-start.11 = (f32[96,128]{1,0:T(8,128)S(1)}, f32[96,128]{1,0:T(8,128)S(1)}, u32[]{:S(2)}, u32[]{:S(2)}) collective-permute-start(f32[96,128]{1,0:T(8,128)S(1)} %add_add_fusion.1), channel_id=1, source_target_pairs={{0,24},{2,26},{4,28},{6,30},{8,0},{10,2},{12,4},{14,6},{16,8},{18,... | collective-permute-start | bytes 147464 | tf_op jit(solution)/shard_map/ppermute | solution.py:633
  105.1 5.0 %collective-permute-start.10 = (f32[96,128]{1,0:T(8,128)S(1)}, f32[96,128]{1,0:T(8,128)S(1)}, u32[]{:S(2)}, u32[]{:S(2)}) collective-permute-start(f32[96,128]{1,0:T(8,128)S(1)} %add_add_fusion.1), channel_id=1, source_target_pairs={{0,16},{2,18},{4,20},{6,22},{8,24},{10,26},{12,28},{14,30},{16,0},... | collective-permute-start | bytes 147464 | tf_op jit(solution)/shard_map/ppermute | solution.py:633
  105.1 5.9 %collective-permute-start.9 = (f32[96,128]{1,0:T(8,128)S(1)}, f32[96,128]{1,0:T(8,128)S(1)}, u32[]{:S(2)}, u32[]{:S(2)}) collective-permute-start(f32[96,128]{1,0:T(8,128)S(1)} %add_add_fusion.1), channel_id=1, source_target_pairs={{0,8},{2,10},{4,12},{6,14},{8,16},{10,18},{12,20},{14,22},{16,24},... | collective-permute-start | bytes 147464 | tf_op jit(solution)/shard_map/ppermute | solution.py:633
  111.0 4.4 %collective-permute-start.14 = (f32[96,128]{1,0:T(8,128)S(1)}, f32[96,128]{1,0:T(8,128)S(1)}, u32[]{:S(2)}, u32[]{:S(2)}) collective-permute-start(f32[96,128]{1,0:T(8,128)S(1)} %add_add_fusion.refs_0_), channel_id=1, source_target_pairs={{0,6},{2,0},{4,2},{6,4},{8,14},{10,8},{12,10},{14,12},{16,22},{18,... | collective-permute-start | bytes 147464 | tf_op jit(solution)/shard_map/ppermute | solution.py:633
  113.6 4.1 %collective-permute-start.13 = (f32[96,128]{1,0:T(8,128)S(1)}, f32[96,128]{1,0:T(8,128)S(1)}, u32[]{:S(2)}, u32[]{:S(2)}) collective-permute-start(f32[96,128]{1,0:T(8,128)S(1)} %add_add_fusion.refs_0_), channel_id=1, source_target_pairs={{0,4},{2,6},{4,0},{6,2},{8,12},{10,14},{12,8},{14,10},{16,20},{18,... | collective-permute-start | bytes 147464 | tf_op jit(solution)/shard_map/ppermute | solution.py:633
  113.6 5.0 %collective-permute-start.12 = (f32[96,128]{1,0:T(8,128)S(1)}, f32[96,128]{1,0:T(8,128)S(1)}, u32[]{:S(2)}, u32[]{:S(2)}) collective-permute-start(f32[96,128]{1,0:T(8,128)S(1)} %add_add_fusion.refs_0_), channel_id=1, source_target_pairs={{0,2},{2,4},{4,6},{6,0},{8,10},{10,12},{12,14},{14,8},{16,18},{18,... | collective-permute-start | bytes 147464 | tf_op jit(solution)/shard_map/ppermute | solution.py:633
  114.3 4.4 %collective-permute-start.15 = (f32[96,128]{1,0:T(8,128)S(1)}, f32[96,128]{1,0:T(8,128)S(1)}, u32[]{:S(2)}, u32[]{:S(2)}) collective-permute-start(f32[96,128]{1,0:T(8,128)S(1)} %add_add_fusion.refs_0_), channel_id=1, source_target_pairs={{0,1},{1,0},{2,3},{3,2},{4,5},{5,4},{6,7},{7,6},{8,9},{9,8},{10,11... | collective-permute-start | bytes 147464 | tf_op jit(solution)/shard_map/ppermute | solution.py:43
  115.4 3.2 %collective-permute-start.18 = (f32[96,128]{1,0:T(8,128)S(1)}, f32[96,128]{1,0:T(8,128)S(1)}, u32[]{:S(2)}, u32[]{:S(2)}) collective-permute-start(f32[96,128]{1,0:T(8,128)S(1)} %collective-permute-done.14.refs_3_), channel_id=1, source_target_pairs={{0,1},{1,0},{2,3},{3,2},{4,5},{5,4},{6,7},{7,6},{8,9},{9,8},{10,11... | collective-permute-start | bytes 147464 | tf_op jit(solution)/shard_map/ppermute | solution.py:43
  117.7 1.2 collective-permute-start.17
  118.6 1.2 collective-permute-start.16
